TPU v7x, 1024 devices: a whole 4x4x32 slice. The times are simulated.
1024 devices in a mesh: dp: 128 (over z, x), mp: 8 (over y, core).
Axes of the slice: x: 4, y: 4, z: 32, core: 2. Of those that a mesh axis runs over, the one named last changes fastest.
Arguments:
- embeddings: bfloat16 [262144, 1024], P(('dp', 'mp')), may hold values from -6 to 6
- assignments: int32 [262144], P(('dp', 'mp')), may hold values from 0 to 2047
- old_centroids: float32 [2048, 1024], P('dp', 'mp'), may hold values from -6 to 6
- slab_rows: int32 [2048, 128], P(('dp', 'mp')), may hold values from 0 to 2047
- slab_len: int32 [2048], P(('dp', 'mp')), may hold values from 2 to 128
Outputs:
- centroids: float32 [2048, 1024], P('dp', 'mp')
- best_cosine: float32 [2048, 128], P(('dp', 'mp'))
Inputs may be any that keep to these rules, and one draw needn't show every extreme that they name: `slab_rows`: entries index rows of the slab's own group of 2048 rows, those held by one index of dp.
All inputs are finite; a program needn't handle non-finite values.
Results may differ from a plain program's by a relative error of at most 0.0004.
Values may be sent and summed in bfloat16 or wider, within the bound.
No kernel may reach another device: no remote copies, remote signals or barrier semaphores. Data moves between devices by JAX's collectives and lax.ppermute only.
A program may use at most 32 MiB of HBM per device.

v0:
```python
import jax
import jax.numpy as jnp
from jax import lax
from jax.sharding import PartitionSpec as P

K_DEV = 2


def best_match(gram_tile, length):
    diagonal_part = jnp.diagonal(gram_tile, axis1=-2, axis2=-1)
    inverse_norm = lax.rsqrt(diagonal_part + 1e-06)
    cosine = gram_tile * inverse_norm[..., :, None] * inverse_norm[..., None, :]
    position = jnp.arange(gram_tile.shape[-1], dtype=jnp.int32)
    live = position < jnp.asarray(length)[..., None]
    pair_mask = live[..., None, :] & (position[:, None] != position[None, :])
    largest = jnp.max(jnp.where(pair_mask, cosine, -2.0), axis=-1)
    return jnp.where(live, largest, 0.0)


def local(embeddings, assignments, old_centroids, slab_rows, slab_len):
    groups = lax.axis_size("mp")
    data_size = lax.axis_size("dp")
    owner = lax.axis_index("mp")
    total_clusters = K_DEV * data_size * groups
    gathered, labels = (
        lax.all_gather(embeddings, "mp", axis=0, tiled=True),
        lax.all_gather(assignments, "mp", axis=0, tiled=True),
    )
    cluster_ids = (
        (jnp.arange(data_size, dtype=jnp.int32)[:, None] * groups + owner) * K_DEV
        + jnp.arange(K_DEV, dtype=jnp.int32)[None, :]
    ).reshape(-1)
    onehot = (cluster_ids[:, None] == labels[None, :]).astype(jnp.bfloat16)
    partial_value = jnp.dot(onehot, gathered, preferred_element_type=jnp.float32)
    count_term = jax.ops.segment_sum(
        jnp.ones(labels.shape, jnp.float32), labels, num_segments=total_clusters
    )
    summed, counts = (
        lax.psum_scatter(partial_value, "dp", scatter_dimension=0, tiled=True),
        lax.psum_scatter(count_term, "dp", scatter_dimension=0, tiled=True),
    )
    summed = lax.all_to_all(summed, "mp", split_axis=1, concat_axis=0, tiled=True)
    members = gathered[slab_rows]
    gram_tile = jnp.einsum("sid,sjd->sij", members, members, preferred_element_type=jnp.float32)
    centroids = (summed + old_centroids) / (counts[:, None] + 1.0)
    best_cosine = best_match(gram_tile, slab_len)
    return (centroids, best_cosine)


def solution(mesh):
    placed = (
        P(("dp", "mp"), None),
        P(("dp", "mp")),
        P("dp", "mp"),
        P(("dp", "mp"), None),
        P(("dp", "mp")),
    )
    return jax.shard_map(
        local,
        mesh=mesh,
        in_specs=placed,
        out_specs=(P("dp", "mp"), P(("dp", "mp"), None)),
        check_vma=False,
    )
```

profile of v0, /device:TPU:1, one launch (start us, length us, event | category | flops | bytes accessed | tf_op | source)
XLA Modules:
  0.0 848.3 jit_solution(14902441803949858167)
XLA Ops:
  7.2 0.0 all-gather.3.cloned.1.call-start
  7.2 0.7 all-gather.3.cloned.1.call-update
  7.9 0.0 all-reduce.4.cloned.1.call-start
  8.0 0.1 iota_add_fusion
  8.1 0.1 add.73
  8.2 1.3 dynamic-slice
  10.8 22.1 %all-gather = s32[8,1,256]{2,1,0:T(1,128)S(1)} all-gather(s32[1,1,256]{2,1,0:T(1,128)} %bitcast.22), channel_id=1, replica_groups=mesh['dp'=128,'mp'=8] {'mp'}, dimensions={0}, use_global_device_ids=true | all-gather | bytes 9216 | tf_op jit(solution)/shard_map/all_gather | solution.py:27
  32.9 11.4 %scatter_custom_fusion = f32[2048]{0:T(1024)S(1)} fusion(s32[2048]{0:T(1024)S(1)} %bitcast.20, f32[2048]{0:T(1024)S(1)} %broadcast.67, f32[]{:T(128)} %constant.13.clone.1), kind=kCustom, calls=%fused_computation.14 | custom fusion | flops 2048 | bytes 8196 | tf_op jit(solution)/shard_map/scatter-add | solution.py:35
  44.2 232.7 %all-reduce.1 = f32[2048]{0:T(1024)S(1)} all-reduce(f32[2048]{0:T(1024)S(1)} %scatter_custom_fusion), channel_id=3, replica_groups=mesh['dp'=128,'mp'=8] {'dp'}, use_global_device_ids=true, to_apply=%region_2.0.clone | all-reduce | flops 2048 | bytes 16384
  276.9 0.7 fusion.6
  277.6 0.0 copy-start.1
  277.6 0.0 all-gather.3.cloned.1.call-done
  277.7 4.5 fusion
  282.1 0.0 all-reduce.4.cloned.1.call-update
  282.1 0.1 dynamic-slice_add_fusion
  282.2 0.0 copy-done.1
  282.3 0.1 iota_compare_fusion.1
  282.3 4.3 gather_fusion
  286.6 0.3 fusion.7
  286.9 0.0 copy-start
  286.9 7.5 copy.16
  294.5 1.8 gather_fusion.1
  296.3 0.1 copy.17
  296.3 0.2 select_reduce_fusion
  296.5 513.3 %all-reduce.4.cloned.1.call-done = f32[256,1024]{1,0:T(8,128)} async-done(((f32[256,1024]{1,0:T(8,128)}), f32[256,1024]{1,0:T(8,128)}) %all-reduce.4.cloned.1.call-update) | async-done | bytes 1048592
  809.8 1.4 dynamic-slice_bitcast_fusion
  811.2 25.0 %all-to-all-start = ((f32[2,8,128]{2,0,1:T(2,128)}), f32[2,8,128]{2,0,1:T(2,128)S(1)}, u32[]{:S(2)}, u32[]{:S(2)}) async-start(f32[2,8,128]{2,0,1:T(2,128)} %dynamic-slice_bitcast_fusion), calls=%async_computation | async-start | bytes 16384 | tf_op jit(solution)/shard_map/all_to_all | solution.py:42
  836.2 0.6 broadcast_select_fusion
  836.8 4.0 all-to-all-done
  840.8 0.0 copy-done
  840.8 0.7 add_divide_fusion
  (6 shorter events, 0.1 us)
Async XLA Ops:
  7.2 270.5 %all-gather.3.cloned.1.call-start = ((), (), s32[]{:S(2)}) async-start(), calls=%async_computation.1 | async-start | bytes 4718592 | tf_op jit(solution)/shard_map/all_gather | solution.py:26
  7.9 801.9 %all-reduce.4.cloned.1.call-start = ((), (), s32[]{:S(2)}) async-start(), calls=%async_computation.2 | async-start | bytes 2097152
  277.6 4.6 copy-start.1
  286.9 553.9 %copy-start = (f32[16,128]{1,0:T(8,128)S(1)}, f32[16,128]{1,0:T(8,128)}, u32[]{:S(2)}) copy-start(f32[16,128]{1,0:T(8,128)} %param.7) | copy-start | bytes 24580
  811.2 29.7 %all-to-all-start = ((f32[2,8,128]{2,0,1:T(2,128)}), f32[2,8,128]{2,0,1:T(2,128)S(1)}, u32[]{:S(2)}, u32[]{:S(2)}) async-start(f32[2,8,128]{2,0,1:T(2,128)} %dynamic-slice_bitcast_fusion), calls=%async_computation | async-start | bytes 16384 | tf_op jit(solution)/shard_map/all_to_all | solution.py:42
Sparse Core Ops, SparseCore 0:
  10.7 58.7 all-gather.2
  282.3 527.4 all-reduce.3
where the time goes:
time: 849 us; the launch traced here: 848 us
  waiting for transfers between devices  518 us (61%)
  blocking collectives  255 us (30%)
  starting transfers between devices  25.1 us (3%)
  local copies, waits for them, and re-layouts  16.4 us (2%)
  between operations  15.5 us (2%)
  other arithmetic  13.8 us (2%)
    unnamed x3, waiting for transfers between devices  514 us
    unnamed x1, blocking collectives  233 us
    all_to_all x1, starting transfers between devices, local(): lax.all_to_all(summed, 'mp', split_axis=1, concat_axis=0, tiled=True)  25 us
    all_gather x1, blocking collectives, local(): lax.all_gather(assignments, 'mp', axis=0, tiled=True)  22.1 us
  transfers between devices with their start and end apart: 3, of which 2 were waited for; matrix products, arithmetic and copies ran while one was open for 3% of the time, Pallas kernels for 0%

commit v1 on v0

v1 whole, which is shorter than its diff:
```python
import jax
import jax.numpy as jnp
from jax import lax
from jax.experimental import pallas as pl
from jax.experimental.pallas import tpu as pltpu
from jax.sharding import Mesh, PartitionSpec as P

F32, BF16, I32 = jnp.float32, jnp.bfloat16, jnp.int32
SIZES = (8, 4, 4, 4, 2)
NAMES = ("zh", "zl", "x", "y", "c")
BLOCK = 32
ROWS = 256
FEATS = 32
MSG = 80
MIB = 1 << 20


def params(mib):
    return pltpu.CompilerParams(vmem_limit_bytes=mib * MIB)


def cost(flops, moved):
    return pl.CostEstimate(flops=flops, bytes_accessed=moved, transcendentals=0)


def pack_kernel(emb_ref, label_ref, out_ref):
    turned = emb_ref[...].T
    c = label_ref[...]
    high = ((c >> 6) & 3) * 64 + (c >> 8) * 8 + ((c >> 4) & 3) * 2 + (c & 1)
    low = ((c >> 1) & 1) * 4 + ((c >> 2) & 3)
    row = lax.broadcasted_iota(I32, (16, 128), 0)
    codes = jnp.where(row == 0, high[0:1], 0)
    codes = jnp.where(row == 1, high[1:2], codes)
    codes = jnp.where(row == 2, low[0:1], codes)
    codes = jnp.where(row == 3, low[1:2], codes)
    codes = codes.astype(F32).astype(BF16)
    for x in range(4):
        for mp in range(8):
            d, f = x * 8 + mp, (mp * 4 + x) * FEATS
            out_ref[d, 0:32, :] = turned[f : f + FEATS, 0:128]
            out_ref[d, 32:64, :] = turned[f : f + FEATS, 128:256]
            out_ref[d, 64:80, :] = codes


def sum_kernel(msg_ref, out_ref, a_ref, b_ref, p_ref, q_ref):
    cluster = lax.broadcasted_iota(I32, (256, 128), 0)
    group = lax.broadcasted_iota(I32, (128, 128), 0)

    def build(s, carry):
        codes = msg_ref[s, 64:80, :].astype(F32).astype(I32)
        for t in range(2):
            high, low = codes[t : t + 1], codes[2 + t : 3 + t]
            at = pl.ds(pl.multiple_of(s * 256 + t * 128, 128), 128)
            a_ref[:, at] = jnp.where(cluster == high, 1.0, 0.0).astype(BF16)
            part = msg_ref[s, 32 * t : 32 * t + 32, :]
            for g in range(8):
                b_ref[32 * g : 32 * g + 32, at] = part * jnp.where(low == g, 1.0, 0.0).astype(BF16)
            within = ((high >> 1) & 7) * 16 + (low & 3) * 4 + (low >> 2) * 2 + (high & 1)
            p_ref[:, at] = jnp.where(cluster[0:16] == (high >> 4), 1.0, 0.0).astype(BF16)
            q_ref[:, at] = jnp.where(group == within, 1.0, 0.0).astype(BF16)
        return carry

    lax.fori_loop(0, BLOCK, build, 0)
    contract = (((1,), (1,)), ((), ()))
    sums = lax.dot_general(a_ref[...], b_ref[...], contract, preferred_element_type=F32)
    counts = lax.dot_general(p_ref[...], q_ref[...], contract, preferred_element_type=F32)
    for zl in range(4):
        out_ref[zl, 0:64, :] = sums[zl * 64 : zl * 64 + 64, 0:128]
        out_ref[zl, 64:128, :] = sums[zl * 64 : zl * 64 + 64, 128:256]
        out_ref[zl, 128:132, :] = counts[zl * 4 : zl * 4 + 4, :]
        out_ref[zl, 132:136, :] = jnp.zeros((4, 128), F32)


def regroup_kernel(in_ref, out_ref, s_ref):
    s_ref[...] = (in_ref[0] + in_ref[1]) + (in_ref[2] + in_ref[3])
    for m in range(32):
        out_ref[5 * m : 5 * m + 2, :] = s_ref[2 * m : 2 * m + 2, :]
        out_ref[5 * m + 2 : 5 * m + 4, :] = s_ref[64 + 2 * m : 66 + 2 * m, :]
        out_ref[5 * m + 4 : 5 * m + 5, :] = s_ref[128 + m // 8 : 129 + m // 8, :]


def finish_kernel(at_ref, in_ref, old_ref, out_ref):
    slot = lax.broadcasted_iota(I32, (4, 128), 1) // FEATS
    parts = []
    for x in range(4):
        total = in_ref[5 * x : 5 * x + 4, :]
        for zh in range(1, 8):
            m = zh * 4 + x
            total = total + in_ref[5 * m : 5 * m + 4, :]
        parts.append(total)
    count_row = in_ref[4:5, :]
    for zh in range(1, 8):
        count_row = count_row + in_ref[20 * zh + 4 : 20 * zh + 5, :]
    lane = lax.broadcasted_iota(I32, (16, 128), 1)
    own = lane == at_ref[0] + lax.broadcasted_iota(I32, (16, 128), 0)
    counts = jnp.sum(jnp.where(own, count_row, 0.0), axis=1, keepdims=True)
    for low in range(4):
        rows = jnp.zeros((4, 128), F32)
        for x in range(4):
            shift = ((x - low) * FEATS) % 128
            moved = pltpu.roll(parts[x], shift, 1) if shift else parts[x]
            rows = jnp.where(slot == x, moved, rows)
        j = slice(4 * low, 4 * low + 4)
        out_ref[j, :] = (rows + old_ref[j, :]) / (counts[j] + 1.0)


def match_kernel(len_ref, rows_ref, emb_ref, out_ref):
    row = lax.broadcasted_iota(I32, (256, 2048), 1)
    pick = jnp.where(row == rows_ref[...], 1.0, 0.0).astype(BF16)
    members = jnp.dot(pick, emb_ref[...], preferred_element_type=F32).astype(BF16)
    i = lax.broadcasted_iota(I32, (128, 128), 0)
    j = lax.broadcasted_iota(I32, (128, 128), 1)
    for s in range(2):
        one = members[128 * s : 128 * s + 128]
        gram = lax.dot_general(one, one, (((1,), (1,)), ((), ())), preferred_element_type=F32)
        diagonal = jnp.where(i == j, gram, 0.0)
        down = lax.rsqrt(jnp.sum(diagonal, axis=1, keepdims=True) + 1e-06)
        across = lax.rsqrt(jnp.sum(diagonal, axis=0, keepdims=True) + 1e-06)
        cosine = gram * down * across
        length = len_ref[s]
        largest = jnp.max(jnp.where((i < length) & (i != j), cosine, -2.0), axis=0, keepdims=True)
        out_ref[s : s + 1, :] = jnp.where(j[0:1] < length, largest, 0.0)


VMEM = pl.BlockSpec(memory_space=pltpu.VMEM)
SMEM = pl.BlockSpec(memory_space=pltpu.SMEM)


def local(embeddings, assignments, old_centroids, slab_rows, slab_len):
    gathered = lax.all_gather(embeddings, ("y", "c"), axis=0, tiled=True)
    messages = pl.pallas_call(
        pack_kernel,
        out_shape=jax.ShapeDtypeStruct((BLOCK, MSG, 128), BF16),
        in_specs=[VMEM, VMEM],
        out_specs=VMEM,
        compiler_params=params(8),
        cost_estimate=cost(1 << 20, 3 << 19),
        name="pack",
    )(embeddings, assignments.reshape(2, 128))
    messages = lax.all_to_all(messages, ("x", "y", "c"), 0, 0, tiled=True)
    parts = pl.pallas_call(
        sum_kernel,
        out_shape=jax.ShapeDtypeStruct((4, 136, 128), F32),
        in_specs=[VMEM],
        out_specs=VMEM,
        scratch_shapes=[
            pltpu.VMEM((256, 8192), BF16),
            pltpu.VMEM((256, 8192), BF16),
            pltpu.VMEM((16, 8192), BF16),
            pltpu.VMEM((128, 8192), BF16),
        ],
        compiler_params=params(20),
        cost_estimate=cost(1 << 31, 1 << 20),
        name="sums",
    )(messages)
    parts = lax.all_to_all(parts, "zl", 0, 0, tiled=True)
    parts = pl.pallas_call(
        regroup_kernel,
        out_shape=jax.ShapeDtypeStruct((160, 128), F32),
        in_specs=[VMEM],
        out_specs=VMEM,
        scratch_shapes=[pltpu.VMEM((136, 128), F32)],
        compiler_params=params(4),
        cost_estimate=cost(1 << 18, 1 << 19),
        name="regroup",
    )(parts)
    parts = lax.all_to_all(parts.reshape(32, 5, 1, 128), ("zh", "x"), 0, 0, tiled=True)
    first = ((lax.axis_index("zh") % 2) * 4 + lax.axis_index("x")) * 16
    centroids = pl.pallas_call(
        finish_kernel,
        out_shape=jax.ShapeDtypeStruct((16, 128), F32),
        in_specs=[SMEM, VMEM, VMEM],
        out_specs=VMEM,
        compiler_params=params(4),
        cost_estimate=cost(1 << 18, 1 << 18),
        name="finish",
    )(first.astype(I32).reshape(1), parts.reshape(160, 128), old_centroids)
    best_cosine = pl.pallas_call(
        match_kernel,
        out_shape=jax.ShapeDtypeStruct((2, 128), F32),
        in_specs=[SMEM, VMEM, VMEM],
        out_specs=VMEM,
        compiler_params=params(16),
        cost_estimate=cost(1 << 31, 5 << 20),
        name="match",
    )(slab_len, slab_rows.reshape(256, 1), gathered)
    return (centroids, best_cosine)


def solution(mesh):
    fine = Mesh(mesh.devices.reshape(SIZES), NAMES)
    dp, mp = ("zh", "zl", "x"), ("y", "c")
    placed = (
        P(dp + mp, None),
        P(dp + mp),
        P(dp, mp),
        P(dp + mp, None),
        P(dp + mp),
    )
    return jax.shard_map(
        local,
        mesh=fine,
        in_specs=placed,
        out_specs=(P(dp, mp), P(dp + mp, None)),
        check_vma=False,
    )
```

time: 849 us -> 117 us (0.14)
  the two profiles are of different devices: /device:TPU:1 before, /device:TPU:40 now
where the time goes in v1:
time: 117 us
  blocking collectives  38.1 us (33%)
  waiting for transfers between devices  29.5 us (25%)
  starting transfers between devices  21.9 us (19%)
  between operations  14.1 us (12%)
  Pallas kernels  9.23 us (8%)
  local copies, waits for them, and re-layouts  4.05 us (3%)
    all_to_all x1, waiting for transfers between devices, local(): lax.all_to_all(parts.reshape(32, 5, 1, 128), ('zh', 'x'), 0, 0, tiled=True)  28.8 us
    all_to_all x1, starting transfers between devices, local(): lax.all_to_all(parts.reshape(32, 5, 1, 128), ('zh', 'x'), 0, 0, tiled=True)  21.8 us
    all_to_all x1, blocking collectives, local(): parts = lax.all_to_all(parts, 'zl', 0, 0, tiled=True)  19.3 us
    all_to_all x1, blocking collectives, local(): messages = lax.all_to_all(messages, ('x', 'y', 'c'), 0, 0, tiled=True)  18.8 us
    pallas_call x1, Pallas kernels, local(): pl.pallas_call(sum_kernel, out_shape=jax.ShapeDtypeStruct((4, 136, 128),...  4.98 us
    unnamed x12, local copies, waits for them, and re-layouts  3.91 us
    pallas_call x1, Pallas kernels, local(): pl.pallas_call(match_kernel, out_shape=jax.ShapeDtypeStruct((2, 128), F32...  2.7 us
  transfers between devices with their start and end apart: 2, of which 1 were waited for; matrix products, arithmetic and copies ran while one was open for 0% of the time, Pallas kernels for 6%

profile of v1, /device:TPU:40, one launch (start us, length us, event | category | flops | bytes accessed | tf_op | source)
XLA Modules:
  0.0 116.8 jit_solution(10466994247504239031)
XLA Ops:
  7.2 0.0 all-gather.2.cloned.1.call-start
  7.2 0.7 all-gather.2.cloned.1.call-update
  7.9 0.0 copy-start
  7.9 1.0 copy-done
  8.9 0.0 copy-start.2
  8.9 0.7 copy-done.2
  9.6 0.2 pack.1
  9.8 18.8 %all_to_all.15.msg_ref = bf16[32,80,128]{2,1,0:T(8,128)(2,1)S(1)} all-to-all(bf16[32,80,128]{2,1,0:T(8,128)(2,1)S(1)} %pack.1), channel_id=1, replica_groups=mesh['zh'=8,'zl'=4,'x'=4,'y'=4,'c'=2] {'x','y','c'}, dimensions={0} | all-to-all | bytes 1310720 | tf_op jit(solution)/shard_map/all_to_all | solution.py:140
  28.6 0.0 copy-start.5
  28.6 0.0 copy-start.1
  28.6 0.0 copy-start.4
  28.6 5.0 %sums.1 = f32[4,136,128]{2,1,0:T(8,128)S(1)} custom-call(bf16[32,80,128]{2,1,0:T(8,128)(2,1)S(1)} %all_to_all.15.msg_ref), custom_call_target="tpu_custom_call" | custom-call | flops 2147483648 | bytes 1048576 | tf_op jit(solution)/shard_map/sums/pallas_call | solution.py:141
  33.6 19.3 %all_to_all.16.in_ref = f32[4,136,128]{2,1,0:T(8,128)S(1)} all-to-all(f32[4,136,128]{2,1,0:T(8,128)S(1)} %sums.1), channel_id=1, replica_groups=mesh['zh'=8,'zl'=4,'x'=4,'y'=4,'c'=2] {'zl'}, dimensions={0} | all-to-all | bytes 557056 | tf_op jit(solution)/shard_map/all_to_all | solution.py:156
  52.9 0.7 regroup.1
  53.6 21.8 %all-to-all-start.2 = ((f32[32,5,1,128]{3,2,1,0:T(1,128)}), f32[32,5,1,128]{3,2,1,0:T(1,128)S(1)}, u32[]{:S(2)}, u32[]{:S(2)}) async-start(f32[32,5,1,128]{3,2,1,0:T(1,128)} %bitcast.2), calls=%async_computation.2 | async-start | bytes 163840 | tf_op jit(solution)/shard_map/all_to_all | solution.py:167
  75.4 0.0 copy-done.5
  75.4 0.1 copy.9.rows_ref
  75.6 28.8 %all-to-all-done.2 = f32[32,5,1,128]{3,2,1,0:T(1,128)S(1)} async-done(((f32[32,5,1,128]{3,2,1,0:T(1,128)}), f32[32,5,1,128]{3,2,1,0:T(1,128)S(1)}, u32[]{:S(2)}, u32[]{:S(2)}) %all-to-all-start.2) | async-done | bytes 81952 | tf_op jit(solution)/shard_map/all_to_all | solution.py:167
  104.4 0.0 copy-done.1
  104.4 0.7 finish.1
  105.1 0.0 all-gather.2.cloned.1.call-done.emb_ref
  105.1 0.0 copy-done.4
  105.1 0.0 copy-start.3
  105.1 2.2 %copy-done.3 = bf16[2048,1024]{1,0:T(8,128)(2,1)S(1)} copy-done((bf16[2048,1024]{1,0:T(8,128)(2,1)S(1)}, bf16[2048,1024]{1,0:T(8,128)(2,1)}, u32[]{:S(2)}) %copy-start.3) | copy-done | bytes 4194328
  107.3 2.7 %match.1 = f32[2,128]{1,0:T(2,128)} custom-call(s32[2]{0:T(128)S(1)} %copy-done.4, s32[256,1]{1,0:T(8,128)S(1)} %copy.9.rows_ref, bf16[2048,1024]{1,0:T(8,128)(2,1)S(1)} %copy-done.3), custom_call_target="tpu_custom_call" | custom-call | flops 2147483648 | bytes 5242880 | tf_op jit(solution)/shard_map/match/pallas_call | solution.py:178
Async XLA Ops:
  7.2 97.9 %all-gather.2.cloned.1.call-start = ((), (), s32[]{:S(2)}) async-start(), calls=%async_computation.3 | async-start | bytes 4718592 | tf_op jit(solution)/shard_map/all_gather | solution.py:130
  7.9 1.0 copy-start
  8.9 0.7 copy-start.2
  28.6 46.9 %copy-start.5 = (s32[2,128]{1,0:T(2,128)S(1)}, s32[2,128]{1,0:T(2,128)}, u32[]{:S(2)}) copy-start(s32[2,128]{1,0:T(2,128)} %param.8) | copy-start | bytes 3076
  28.6 75.8 %copy-start.1 = (f32[16,128]{1,0:T(8,128)S(1)}, f32[16,128]{1,0:T(8,128)}, u32[]{:S(2)}) copy-start(f32[16,128]{1,0:T(8,128)} %old_ref.1) | copy-start | bytes 24580
  28.6 76.5 %copy-start.4 = (s32[2]{0:T(128)S(1)}, s32[2]{0:T(128)}, u32[]{:S(2)}) copy-start(s32[2]{0:T(128)} %len_ref.1) | copy-start | bytes 28
  53.6 50.8 %all-to-all-start.2 = ((f32[32,5,1,128]{3,2,1,0:T(1,128)}), f32[32,5,1,128]{3,2,1,0:T(1,128)S(1)}, u32[]{:S(2)}, u32[]{:S(2)}) async-start(f32[32,5,1,128]{3,2,1,0:T(1,128)} %bitcast.2), calls=%async_computation.2 | async-start | bytes 163840 | tf_op jit(solution)/shard_map/all_to_all | solution.py:167
  105.1 2.2 %copy-start.3 = (bf16[2048,1024]{1,0:T(8,128)(2,1)S(1)}, bf16[2048,1024]{1,0:T(8,128)(2,1)}, u32[]{:S(2)}) copy-start(bf16[2048,1024]{1,0:T(8,128)(2,1)} %all-gather.2.cloned.1.call-done.emb_ref) | copy-start | bytes 12582916
Sparse Core Ops, SparseCore 0:
  10.7 56.0 all-gather.1

commit v2 on v1

--- a/solution.py
+++ b/solution.py
@@ -104,10 +104,17 @@
         out_ref[j, :] = (rows + old_ref[j, :]) / (counts[j] + 1.0)
 
 
-def match_kernel(len_ref, rows_ref, emb_ref, out_ref):
-    row = lax.broadcasted_iota(I32, (256, 2048), 1)
-    pick = jnp.where(row == rows_ref[...], 1.0, 0.0).astype(BF16)
-    members = jnp.dot(pick, emb_ref[...], preferred_element_type=F32).astype(BF16)
+def match_kernel(place_ref, len_ref, rows_ref, own_ref, other_ref, out_ref):
+    r = rows_ref[...]
+    away = (r >> 9) ^ place_ref[1]
+    away = jnp.where(away == 2, 3, jnp.where(away == 3, 2, away))
+    at = (((r >> 8) & 1) ^ place_ref[0]) * 1024 + away * 256 + (r & 255)
+    lane = lax.broadcasted_iota(I32, (256, 1024), 1)
+    pick = jnp.where(lane == at, 1.0, 0.0).astype(BF16)
+    members = jnp.dot(pick, own_ref[...], preferred_element_type=F32)
+    pick = jnp.where(lane + 1024 == at, 1.0, 0.0).astype(BF16)
+    members = members + jnp.dot(pick, other_ref[...], preferred_element_type=F32)
+    members = members.astype(BF16)
     i = lax.broadcasted_iota(I32, (128, 128), 0)
     j = lax.broadcasted_iota(I32, (128, 128), 1)
     for s in range(2):
@@ -127,7 +134,6 @@
 
 
 def local(embeddings, assignments, old_centroids, slab_rows, slab_len):
-    gathered = lax.all_gather(embeddings, ("y", "c"), axis=0, tiled=True)
     messages = pl.pallas_call(
         pack_kernel,
         out_shape=jax.ShapeDtypeStruct((BLOCK, MSG, 128), BF16),
@@ -137,6 +143,8 @@
         cost_estimate=cost(1 << 20, 3 << 19),
         name="pack",
     )(embeddings, assignments.reshape(2, 128))
+    line, messages = lax.optimization_barrier((embeddings, messages))
+    line = [line] + [lax.ppermute(line, "y", [(i, i ^ d) for i in range(4)]) for d in (1, 3, 2)]
     messages = lax.all_to_all(messages, ("x", "y", "c"), 0, 0, tiled=True)
     parts = pl.pallas_call(
         sum_kernel,
@@ -165,6 +173,19 @@
         name="regroup",
     )(parts)
     parts = lax.all_to_all(parts.reshape(32, 5, 1, 128), ("zh", "x"), 0, 0, tiled=True)
+    own = jnp.concatenate(line)
+    other = lax.ppermute(own, "c", [(0, 1), (1, 0)])
+    place = jnp.stack([lax.axis_index("c"), lax.axis_index("y")]).astype(I32)
+    best_cosine = pl.pallas_call(
+        match_kernel,
+        out_shape=jax.ShapeDtypeStruct((2, 128), F32),
+        in_specs=[SMEM, SMEM, VMEM, VMEM, VMEM],
+        out_specs=VMEM,
+        compiler_params=params(16),
+        cost_estimate=cost(1 << 31, 5 << 20),
+        name="match",
+    )(place, slab_len, slab_rows.reshape(256, 1), own, other)
+    parts, best_cosine = lax.optimization_barrier((parts, best_cosine))
     first = ((lax.axis_index("zh") % 2) * 4 + lax.axis_index("x")) * 16
     centroids = pl.pallas_call(
         finish_kernel,
@@ -175,15 +196,6 @@
         cost_estimate=cost(1 << 18, 1 << 18),
         name="finish",
     )(first.astype(I32).reshape(1), parts.reshape(160, 128), old_centroids)
-    best_cosine = pl.pallas_call(
-        match_kernel,
-        out_shape=jax.ShapeDtypeStruct((2, 128), F32),
-        in_specs=[SMEM, VMEM, VMEM],
-        out_specs=VMEM,
-        compiler_params=params(16),
-        cost_estimate=cost(1 << 31, 5 << 20),
-        name="match",
-    )(slab_len, slab_rows.reshape(256, 1), gathered)
     return (centroids, best_cosine)
 
 

time: 117 us -> 119 us (1.017)
  the two profiles are of different devices: /device:TPU:40 before, /device:TPU:32 now
where the time goes in v2:
time: 119 us; the launch traced here: 118 us
  starting transfers between devices  55.2 us (46%)
  waiting for transfers between devices  44.9 us (38%)
  Pallas kernels  12.9 us (11%)
  local copies, waits for them, and re-layouts  4.09 us (3%)
    all_to_all x1, starting transfers between devices, local(): lax.all_to_all(parts.reshape(32, 5, 1, 128), ('zh', 'x'), 0, 0, tiled=True)  25.5 us
    all_to_all x1, waiting for transfers between devices, local(): lax.all_to_all(parts.reshape(32, 5, 1, 128), ('zh', 'x'), 0, 0, tiled=True)  22.6 us
    ppermute x3, waiting for transfers between devices, local(): lax.ppermute(line, 'y', [(i, i ^ d) for i in range(4)])  17.9 us
    ppermute x3, starting transfers between devices, local(): lax.ppermute(line, 'y', [(i, i ^ d) for i in range(4)])  12.8 us
    all_to_all x1, starting transfers between devices, local(): parts = lax.all_to_all(parts, 'zl', 0, 0, tiled=True)  9.78 us
    pallas_call x1, Pallas kernels, local(): pl.pallas_call(sum_kernel, out_shape=jax.ShapeDtypeStruct((4, 136, 128),...  5.7 us
    all_to_all x1, starting transfers between devices, local(): messages = lax.all_to_all(messages, ('x', 'y', 'c'), 0, 0, tiled=True)  5.19 us
    all_to_all x1, waiting for transfers between devices, local(): parts = lax.all_to_all(parts, 'zl', 0, 0, tiled=True)  4.38 us
  transfers between devices with their start and end apart: 7, of which 3 were waited for; matrix products, arithmetic and copies ran while one was open for 3% of the time, Pallas kernels for 9%

profile of v2, /device:TPU:32, one launch (start us, length us, event | category | flops | bytes accessed | tf_op | source)
XLA Modules:
  0.0 117.9 jit_solution(16689165690718049181)
XLA Ops:
  0.6 0.0 copy-start.1
  0.6 0.7 copy-done.1
  1.3 2.1 %pack.1 = bf16[32,80,128]{2,1,0:T(8,128)(2,1)} custom-call(bf16[256,1024]{1,0:T(8,128)(2,1)} %emb_ref.1, s32[2,128]{1,0:T(2,128)S(1)} %bitcast.8), custom_call_target="tpu_custom_call" | custom-call | flops 1048576 | bytes 1572864 | tf_op jit(solution)/shard_map/pack/pallas_call | solution.py:137
  3.4 3.5 %collective-permute-start = (bf16[256,1024]{1,0:T(8,128)(2,1)}, bf16[256,1024]{1,0:T(8,128)(2,1)}, u32[]{:S(2)}, u32[]{:S(2)}) collective-permute-start(bf16[256,1024]{1,0:T(8,128)(2,1)} %emb_ref.1), channel_id=1, source_target_pairs={{0,2},{2,0},{4,6},{6,4},{1,3},{3,1},{5,7},{7,5},{8,10},{10,8},{12,... | collective-permute-start | bytes 1572872 | tf_op jit(solution)/shard_map/ppermute | solution.py:147
  6.9 4.1 %collective-permute-start.1 = (bf16[256,1024]{1,0:T(8,128)(2,1)}, bf16[256,1024]{1,0:T(8,128)(2,1)}, u32[]{:S(2)}, u32[]{:S(2)}) collective-permute-start(bf16[256,1024]{1,0:T(8,128)(2,1)} %emb_ref.1), channel_id=1, source_target_pairs={{0,6},{2,4},{4,2},{6,0},{1,7},{3,5},{5,3},{7,1},{8,14},{10,12},{12... | collective-permute-start | bytes 1572872 | tf_op jit(solution)/shard_map/ppermute | solution.py:147
  11.0 5.2 %all-to-all-start = ((bf16[32,80,128]{2,1,0:T(8,128)(2,1)}), bf16[32,80,128]{2,1,0:T(8,128)(2,1)S(1)}, u32[]{:S(2)}, u32[]{:S(2)}) async-start(bf16[32,80,128]{2,1,0:T(8,128)(2,1)} %pack.1), calls=%async_computation | async-start | bytes 1310720 | tf_op jit(solution)/shard_map/all_to_all | solution.py:148
  16.2 5.2 %collective-permute-start.2 = (bf16[256,1024]{1,0:T(8,128)(2,1)}, bf16[256,1024]{1,0:T(8,128)(2,1)S(1)}, u32[]{:S(2)}, u32[]{:S(2)}) collective-permute-start(bf16[256,1024]{1,0:T(8,128)(2,1)} %emb_ref.1), channel_id=1, source_target_pairs={{0,4},{2,6},{4,0},{6,2},{1,5},{3,7},{5,1},{7,3},{8,12},{10,14},{12... | collective-permute-start | bytes 1572872 | tf_op jit(solution)/shard_map/ppermute | solution.py:147
  21.4 1.1 constant_dynamic-update-slice_fusion.3
  22.5 0.0 collective-permute-done
  22.5 1.1 constant_dynamic-update-slice_fusion.2
  23.6 17.9 %collective-permute-done.1 = bf16[256,1024]{1,0:T(8,128)(2,1)} collective-permute-done((bf16[256,1024]{1,0:T(8,128)(2,1)}, bf16[256,1024]{1,0:T(8,128)(2,1)}, u32[]{:S(2)}, u32[]{:S(2)}) %collective-permute-start.1) | collective-permute-done | bytes 524320 | tf_op jit(solution)/shard_map/ppermute | solution.py:147
  41.5 1.1 constant_dynamic-update-slice_fusion.1
  42.6 0.0 all-to-all-done.msg_ref
  42.6 5.7 %sums.1 = f32[4,136,128]{2,1,0:T(8,128)} custom-call(bf16[32,80,128]{2,1,0:T(8,128)(2,1)S(1)} %all-to-all-done.msg_ref), custom_call_target="tpu_custom_call" | custom-call | flops 2147483648 | bytes 1048576 | tf_op jit(solution)/shard_map/sums/pallas_call | solution.py:149
  48.3 0.0 copy-start.3
  48.3 0.0 copy-start.2
  48.3 9.8 %all-to-all-start.1 = ((f32[4,136,128]{2,1,0:T(8,128)}), f32[4,136,128]{2,1,0:T(8,128)S(1)}, u32[]{:S(2)}, u32[]{:S(2)}) async-start(f32[4,136,128]{2,1,0:T(8,128)} %sums.1), calls=%async_computation.1 | async-start | bytes 557056 | tf_op jit(solution)/shard_map/all_to_all | solution.py:164
  58.1 0.0 collective-permute-done.2
  58.1 1.9 %collective-permute-start.3 = (bf16[1024,1024]{1,0:T(8,128)(2,1)S(1)}, bf16[1024,1024]{1,0:T(8,128)(2,1)}, u32[]{:S(2)}, u32[]{:S(2)}) collective-permute-start(bf16[1024,1024]{1,0:T(8,128)(2,1)S(1)} %constant_dynamic-update-slice_fusion.own_ref), channel_id=1, source_target_pairs={{0,1},{1,0},{2,3},{3,2},{4,5},{5,4},{6,7},{7,6},{8,9},{9,8},{10,11... | collective-permute-start | bytes 6291464 | tf_op jit(solution)/shard_map/ppermute | solution.py:177
  60.0 4.4 %all-to-all-done.1.in_ref = f32[4,136,128]{2,1,0:T(8,128)S(1)} async-done(((f32[4,136,128]{2,1,0:T(8,128)}), f32[4,136,128]{2,1,0:T(8,128)S(1)}, u32[]{:S(2)}, u32[]{:S(2)}) %all-to-all-start.1) | async-done | bytes 278560 | tf_op jit(solution)/shard_map/all_to_all | solution.py:164
  64.4 0.7 regroup.1
  65.1 25.5 %all-to-all-start.2 = ((f32[32,5,1,128]{3,2,1,0:T(1,128)}), f32[32,5,1,128]{3,2,1,0:T(1,128)S(1)}, u32[]{:S(2)}, u32[]{:S(2)}) async-start(f32[32,5,1,128]{3,2,1,0:T(1,128)} %bitcast.2), calls=%async_computation.2 | async-start | bytes 163840 | tf_op jit(solution)/shard_map/all_to_all | solution.py:175
  90.6 0.0 copy-done.3
  90.6 0.1 copy.9.rows_ref
  90.8 0.1 pad_add_fusion.place_ref
  90.9 0.0 copy-start
  90.9 0.0 collective-permute-done.3.other_ref
  90.9 0.0 copy-done.2
  90.9 3.8 %match.1 = f32[2,128]{1,0:T(2,128)} custom-call(s32[2]{0:T(128)S(1)} %pad_add_fusion.place_ref, s32[2]{0:T(128)S(1)} %copy-done.2, s32[256,1]{1,0:T(8,128)S(1)} %copy.9.rows_ref, bf16[1024,1024]{1,0:T(8,128)(2,1)S(1)} %constant_dynamic-update-slice_fusion.own_ref, bf16[1024,1024]{1,0:T(8,128)(2,1)} %collective-permute-done.3.other_ref), custom_call_target="tpu_custom_call" | custom-call | flops 2147483648 | bytes 5242880 | tf_op jit(solution)/shard_map/match/pallas_call | solution.py:179
  94.6 22.6 %all-to-all-done.2 = f32[32,5,1,128]{3,2,1,0:T(1,128)S(1)} async-done(((f32[32,5,1,128]{3,2,1,0:T(1,128)}), f32[32,5,1,128]{3,2,1,0:T(1,128)S(1)}, u32[]{:S(2)}, u32[]{:S(2)}) %all-to-all-start.2) | async-done | bytes 81952 | tf_op jit(solution)/shard_map/all_to_all | solution.py:175
  117.2 0.0 copy-done
  117.2 0.7 finish.1
  (1 shorter events, 0.0 us)
Async XLA Ops:
  0.6 0.7 copy-start.1
  3.4 19.1 %collective-permute-start = (bf16[256,1024]{1,0:T(8,128)(2,1)}, bf16[256,1024]{1,0:T(8,128)(2,1)}, u32[]{:S(2)}, u32[]{:S(2)}) collective-permute-start(bf16[256,1024]{1,0:T(8,128)(2,1)} %emb_ref.1), channel_id=1, source_target_pairs={{0,2},{2,0},{4,6},{6,4},{1,3},{3,1},{5,7},{7,5},{8,10},{10,8},{12,... | collective-permute-start | bytes 1572872 | tf_op jit(solution)/shard_map/ppermute | solution.py:147
  6.9 34.6 %collective-permute-start.1 = (bf16[256,1024]{1,0:T(8,128)(2,1)}, bf16[256,1024]{1,0:T(8,128)(2,1)}, u32[]{:S(2)}, u32[]{:S(2)}) collective-permute-start(bf16[256,1024]{1,0:T(8,128)(2,1)} %emb_ref.1), channel_id=1, source_target_pairs={{0,6},{2,4},{4,2},{6,0},{1,7},{3,5},{5,3},{7,1},{8,14},{10,12},{12... | collective-permute-start | bytes 1572872 | tf_op jit(solution)/shard_map/ppermute | solution.py:147
  11.0 31.6 %all-to-all-start = ((bf16[32,80,128]{2,1,0:T(8,128)(2,1)}), bf16[32,80,128]{2,1,0:T(8,128)(2,1)S(1)}, u32[]{:S(2)}, u32[]{:S(2)}) async-start(bf16[32,80,128]{2,1,0:T(8,128)(2,1)} %pack.1), calls=%async_computation | async-start | bytes 1310720 | tf_op jit(solution)/shard_map/all_to_all | solution.py:148
  16.2 41.9 %collective-permute-start.2 = (bf16[256,1024]{1,0:T(8,128)(2,1)}, bf16[256,1024]{1,0:T(8,128)(2,1)S(1)}, u32[]{:S(2)}, u32[]{:S(2)}) collective-permute-start(bf16[256,1024]{1,0:T(8,128)(2,1)} %emb_ref.1), channel_id=1, source_target_pairs={{0,4},{2,6},{4,0},{6,2},{1,5},{3,7},{5,1},{7,3},{8,12},{10,14},{12... | collective-permute-start | bytes 1572872 | tf_op jit(solution)/shard_map/ppermute | solution.py:147
  48.3 42.3 %copy-start.3 = (s32[2,128]{1,0:T(2,128)S(1)}, s32[2,128]{1,0:T(2,128)}, u32[]{:S(2)}) copy-start(s32[2,128]{1,0:T(2,128)} %param.8) | copy-start | bytes 3076
  48.3 42.6 %copy-start.2 = (s32[2]{0:T(128)S(1)}, s32[2]{0:T(128)}, u32[]{:S(2)}) copy-start(s32[2]{0:T(128)} %len_ref.1) | copy-start | bytes 28
  48.3 16.1 %all-to-all-start.1 = ((f32[4,136,128]{2,1,0:T(8,128)}), f32[4,136,128]{2,1,0:T(8,128)S(1)}, u32[]{:S(2)}, u32[]{:S(2)}) async-start(f32[4,136,128]{2,1,0:T(8,128)} %sums.1), calls=%async_computation.1 | async-start | bytes 557056 | tf_op jit(solution)/shard_map/all_to_all | solution.py:164
  58.1 32.8 %collective-permute-start.3 = (bf16[1024,1024]{1,0:T(8,128)(2,1)S(1)}, bf16[1024,1024]{1,0:T(8,128)(2,1)}, u32[]{:S(2)}, u32[]{:S(2)}) collective-permute-start(bf16[1024,1024]{1,0:T(8,128)(2,1)S(1)} %constant_dynamic-update-slice_fusion.own_ref), channel_id=1, source_target_pairs={{0,1},{1,0},{2,3},{3,2},{4,5},{5,4},{6,7},{7,6},{8,9},{9,8},{10,11... | collective-permute-start | bytes 6291464 | tf_op jit(solution)/shard_map/ppermute | solution.py:177
  65.1 52.1 %all-to-all-start.2 = ((f32[32,5,1,128]{3,2,1,0:T(1,128)}), f32[32,5,1,128]{3,2,1,0:T(1,128)S(1)}, u32[]{:S(2)}, u32[]{:S(2)}) async-start(f32[32,5,1,128]{3,2,1,0:T(1,128)} %bitcast.2), calls=%async_computation.2 | async-start | bytes 163840 | tf_op jit(solution)/shard_map/all_to_all | solution.py:175
  90.9 26.4 %copy-start = (f32[16,128]{1,0:T(8,128)S(1)}, f32[16,128]{1,0:T(8,128)}, u32[]{:S(2)}) copy-start(f32[16,128]{1,0:T(8,128)} %old_ref.1) | copy-start | bytes 24580

commit v3 on v2

--- a/solution.py
+++ b/solution.py
@@ -104,16 +104,16 @@
         out_ref[j, :] = (rows + old_ref[j, :]) / (counts[j] + 1.0)
 
 
-def match_kernel(place_ref, len_ref, rows_ref, own_ref, other_ref, out_ref):
+def match_kernel(place_ref, len_ref, rows_ref, *refs):
+    *line_refs, out_ref = refs
     r = rows_ref[...]
     away = (r >> 9) ^ place_ref[1]
-    away = jnp.where(away == 2, 3, jnp.where(away == 3, 2, away))
-    at = (((r >> 8) & 1) ^ place_ref[0]) * 1024 + away * 256 + (r & 255)
-    lane = lax.broadcasted_iota(I32, (256, 1024), 1)
-    pick = jnp.where(lane == at, 1.0, 0.0).astype(BF16)
-    members = jnp.dot(pick, own_ref[...], preferred_element_type=F32)
-    pick = jnp.where(lane + 1024 == at, 1.0, 0.0).astype(BF16)
-    members = members + jnp.dot(pick, other_ref[...], preferred_element_type=F32)
+    at = (away << 9) + ((((r >> 8) & 1) ^ place_ref[0]) << 8) + (r & 255)
+    lane = lax.broadcasted_iota(I32, (256, 512), 1)
+    members = jnp.zeros((256, 1024), F32)
+    for away, line_ref in zip((0, 1, 3, 2), line_refs):
+        pick = jnp.where(lane + 512 * away == at, 1.0, 0.0).astype(BF16)
+        members = members + jnp.dot(pick, line_ref[...], preferred_element_type=F32)
     members = members.astype(BF16)
     i = lax.broadcasted_iota(I32, (128, 128), 0)
     j = lax.broadcasted_iota(I32, (128, 128), 1)
@@ -143,8 +143,7 @@
         cost_estimate=cost(1 << 20, 3 << 19),
         name="pack",
     )(embeddings, assignments.reshape(2, 128))
-    line, messages = lax.optimization_barrier((embeddings, messages))
-    line = [line] + [lax.ppermute(line, "y", [(i, i ^ d) for i in range(4)]) for d in (1, 3, 2)]
+    pair = jnp.concatenate([embeddings, lax.ppermute(embeddings, "c", [(0, 1), (1, 0)])])
     messages = lax.all_to_all(messages, ("x", "y", "c"), 0, 0, tiled=True)
     parts = pl.pallas_call(
         sum_kernel,
@@ -161,6 +160,8 @@
         cost_estimate=cost(1 << 31, 1 << 20),
         name="sums",
     )(messages)
+    pair, parts = lax.optimization_barrier((pair, parts))
+    line = [pair] + [lax.ppermute(pair, "y", [(i, i ^ d) for i in range(4)]) for d in (1, 3, 2)]
     parts = lax.all_to_all(parts, "zl", 0, 0, tiled=True)
     parts = pl.pallas_call(
         regroup_kernel,
@@ -173,18 +174,16 @@
         name="regroup",
     )(parts)
     parts = lax.all_to_all(parts.reshape(32, 5, 1, 128), ("zh", "x"), 0, 0, tiled=True)
-    own = jnp.concatenate(line)
-    other = lax.ppermute(own, "c", [(0, 1), (1, 0)])
     place = jnp.stack([lax.axis_index("c"), lax.axis_index("y")]).astype(I32)
     best_cosine = pl.pallas_call(
         match_kernel,
         out_shape=jax.ShapeDtypeStruct((2, 128), F32),
-        in_specs=[SMEM, SMEM, VMEM, VMEM, VMEM],
+        in_specs=[SMEM, SMEM] + [VMEM] * 5,
         out_specs=VMEM,
         compiler_params=params(16),
         cost_estimate=cost(1 << 31, 5 << 20),
         name="match",
-    )(place, slab_len, slab_rows.reshape(256, 1), own, other)
+    )(place, slab_len, slab_rows.reshape(256, 1), *line)
     parts, best_cosine = lax.optimization_barrier((parts, best_cosine))
     first = ((lax.axis_index("zh") % 2) * 4 + lax.axis_index("x")) * 16
     centroids = pl.pallas_call(

time: 119 us -> 104 us (0.87)
  the two profiles are of different devices: /device:TPU:32 before, /device:TPU:8 now
where the time goes in v3:
time: 104 us; the launch traced here: 103 us
  starting transfers between devices  52.8 us (51%)
  waiting for transfers between devices  35.8 us (34%)
  Pallas kernels  11.8 us (11%)
  local copies, waits for them, and re-layouts  1.86 us (2%)
    all_to_all x1, starting transfers between devices, local(): lax.all_to_all(parts.reshape(32, 5, 1, 128), ('zh', 'x'), 0, 0, tiled=True)  20.2 us
    ppermute x3, waiting for transfers between devices, local(): lax.ppermute(pair, 'y', [(i, i ^ d) for i in range(4)])  19.6 us
    all_to_all x1, starting transfers between devices, local(): messages = lax.all_to_all(messages, ('x', 'y', 'c'), 0, 0, tiled=True)  16.7 us
    all_to_all x1, waiting for transfers between devices, local(): messages = lax.all_to_all(messages, ('x', 'y', 'c'), 0, 0, tiled=True)  11.4 us
    ppermute x3, starting transfers between devices, local(): lax.ppermute(pair, 'y', [(i, i ^ d) for i in range(4)])  10.4 us
    pallas_call x1, Pallas kernels, local(): pl.pallas_call(sum_kernel, out_shape=jax.ShapeDtypeStruct((4, 136, 128),...  5.7 us
    all_to_all x1, waiting for transfers between devices, local(): lax.all_to_all(parts.reshape(32, 5, 1, 128), ('zh', 'x'), 0, 0, tiled=True)  4.83 us
    pallas_call x1, Pallas kernels, local(): pl.pallas_call(match_kernel, out_shape=jax.ShapeDtypeStruct((2, 128), F32...  3.71 us
  transfers between devices with their start and end apart: 7, of which 3 were waited for; matrix products, arithmetic and copies ran while one was open for 0% of the time, Pallas kernels for 5%

profile of v3, /device:TPU:8, one launch (start us, length us, event | category | flops | bytes accessed | tf_op | source)
XLA Modules:
  0.0 103.3 jit_solution(14034620374950506096)
XLA Ops:
  0.6 1.9 %collective-permute-start = (bf16[256,1024]{1,0:T(8,128)(2,1)}, bf16[256,1024]{1,0:T(8,128)(2,1)S(1)}, u32[]{:S(2)}, u32[]{:S(2)}) collective-permute-start(bf16[256,1024]{1,0:T(8,128)(2,1)} %emb_ref.1), channel_id=1, source_target_pairs={{0,1},{1,0},{2,3},{3,2},{4,5},{5,4},{6,7},{7,6},{8,9},{9,8},{10,11... | collective-permute-start | bytes 1572872 | tf_op jit(solution)/shard_map/ppermute | solution.py:146
  2.6 0.0 copy-start
  2.6 1.0 %copy-done = bf16[256,1024]{1,0:T(8,128)(2,1)S(1)} copy-done((bf16[256,1024]{1,0:T(8,128)(2,1)S(1)}, bf16[256,1024]{1,0:T(8,128)(2,1)}, u32[]{:S(2)}) %copy-start) | copy-done | bytes 524312
  3.6 0.0 copy-start.3
  3.6 0.7 copy-done.3
  4.3 0.0 copy-start.1
  4.3 1.0 %pack.1 = bf16[32,80,128]{2,1,0:T(8,128)(2,1)} custom-call(bf16[256,1024]{1,0:T(8,128)(2,1)S(1)} %copy-done, s32[2,128]{1,0:T(2,128)S(1)} %bitcast.8), custom_call_target="tpu_custom_call" | custom-call | flops 1048576 | bytes 1572864 | tf_op jit(solution)/shard_map/pack/pallas_call | solution.py:137
  5.3 16.7 %all-to-all-start = ((bf16[32,80,128]{2,1,0:T(8,128)(2,1)}), bf16[32,80,128]{2,1,0:T(8,128)(2,1)S(1)}, u32[]{:S(2)}, u32[]{:S(2)}) async-start(bf16[32,80,128]{2,1,0:T(8,128)(2,1)} %pack.1), calls=%async_computation | async-start | bytes 1310720 | tf_op jit(solution)/shard_map/all_to_all | solution.py:147
  22.0 0.0 collective-permute-done
  22.0 0.0 copy-done.1
  22.0 0.1 pad_maximum_fusion.refs_0_
  22.1 11.4 %all-to-all-done.msg_ref = bf16[32,80,128]{2,1,0:T(8,128)(2,1)S(1)} async-done(((bf16[32,80,128]{2,1,0:T(8,128)(2,1)}), bf16[32,80,128]{2,1,0:T(8,128)(2,1)S(1)}, u32[]{:S(2)}, u32[]{:S(2)}) %all-to-all-start) | async-done | bytes 655392 | tf_op jit(solution)/shard_map/all_to_all | solution.py:147
  33.5 5.7 %sums.1 = f32[4,136,128]{2,1,0:T(8,128)} custom-call(bf16[32,80,128]{2,1,0:T(8,128)(2,1)S(1)} %all-to-all-done.msg_ref), custom_call_target="tpu_custom_call" | custom-call | flops 2147483648 | bytes 1048576 | tf_op jit(solution)/shard_map/sums/pallas_call | solution.py:148
  39.2 0.0 copy-start.5
  39.2 0.0 copy-start.4
  39.2 3.6 %all-to-all-start.1 = ((f32[4,136,128]{2,1,0:T(8,128)}), f32[4,136,128]{2,1,0:T(8,128)S(1)}, u32[]{:S(2)}, u32[]{:S(2)}) async-start(f32[4,136,128]{2,1,0:T(8,128)} %sums.1), calls=%async_computation.1 | async-start | bytes 557056 | tf_op jit(solution)/shard_map/all_to_all | solution.py:165
  42.8 3.7 %collective-permute-start.3 = (bf16[512,1024]{1,0:T(8,128)(2,1)S(1)}, bf16[512,1024]{1,0:T(8,128)(2,1)S(1)}, u32[]{:S(2)}, u32[]{:S(2)}) collective-permute-start(bf16[512,1024]{1,0:T(8,128)(2,1)S(1)} %pad_maximum_fusion.refs_0_), channel_id=1, source_target_pairs={{0,4},{2,6},{4,0},{6,2},{1,5},{3,7},{5,1},{7,3},{8,12},{10,14},{12... | collective-permute-start | bytes 3145736 | tf_op jit(solution)/shard_map/ppermute | solution.py:164
  46.5 2.9 %collective-permute-start.2 = (bf16[512,1024]{1,0:T(8,128)(2,1)S(1)}, bf16[512,1024]{1,0:T(8,128)(2,1)}, u32[]{:S(2)}, u32[]{:S(2)}) collective-permute-start(bf16[512,1024]{1,0:T(8,128)(2,1)S(1)} %pad_maximum_fusion.refs_0_), channel_id=1, source_target_pairs={{0,6},{2,4},{4,2},{6,0},{1,7},{3,5},{5,3},{7,1},{8,14},{10,12},{12... | collective-permute-start | bytes 3145736 | tf_op jit(solution)/shard_map/ppermute | solution.py:164
  49.4 3.8 %collective-permute-start.1 = (bf16[512,1024]{1,0:T(8,128)(2,1)S(1)}, bf16[512,1024]{1,0:T(8,128)(2,1)}, u32[]{:S(2)}, u32[]{:S(2)}) collective-permute-start(bf16[512,1024]{1,0:T(8,128)(2,1)S(1)} %pad_maximum_fusion.refs_0_), channel_id=1, source_target_pairs={{0,2},{2,0},{4,6},{6,4},{1,3},{3,1},{5,7},{7,5},{8,10},{10,8},{12,... | collective-permute-start | bytes 3145736 | tf_op jit(solution)/shard_map/ppermute | solution.py:164
  53.3 0.0 all-to-all-done.1.in_ref
  53.3 0.7 regroup.1
  53.9 20.2 %all-to-all-start.2 = ((f32[32,5,1,128]{3,2,1,0:T(1,128)}), f32[32,5,1,128]{3,2,1,0:T(1,128)S(1)}, u32[]{:S(2)}, u32[]{:S(2)}) async-start(f32[32,5,1,128]{3,2,1,0:T(1,128)} %bitcast.2), calls=%async_computation.2 | async-start | bytes 163840 | tf_op jit(solution)/shard_map/all_to_all | solution.py:176
  74.2 0.0 copy-done.5
  74.2 0.1 copy.9.rows_ref
  74.4 0.1 pad_add_fusion.place_ref
  74.4 0.0 copy-start.2
  74.4 0.0 collective-permute-done.3.refs_3_
  74.4 19.6 %collective-permute-done.2.refs_2_ = bf16[512,1024]{1,0:T(8,128)(2,1)} collective-permute-done((bf16[512,1024]{1,0:T(8,128)(2,1)S(1)}, bf16[512,1024]{1,0:T(8,128)(2,1)}, u32[]{:S(2)}, u32[]{:S(2)}) %collective-permute-start.2) | collective-permute-done | bytes 1048608 | tf_op jit(solution)/shard_map/ppermute | solution.py:164
  94.0 0.0 collective-permute-done.1.refs_1_
  94.0 0.0 copy-done.4
  94.0 3.7 %match.1 = f32[2,128]{1,0:T(2,128)} custom-call(s32[2]{0:T(128)S(1)} %pad_add_fusion.place_ref, s32[2]{0:T(128)S(1)} %copy-done.4, s32[256,1]{1,0:T(8,128)S(1)} %copy.9.rows_ref, bf16[512,1024]{1,0:T(8,128)(2,1)S(1)} %pad_maximum_fusion.refs_0_, bf16[512,1024]{1,0:T(8,128)(2,1)} %collective-permute-done.1.refs_1_, ...), custom_call_target="tpu_custom_call" | custom-call | flops 2147483648 | bytes 5242880 | tf_op jit(solution)/shard_map/match/pallas_call | solution.py:178
  97.7 4.8 %all-to-all-done.2 = f32[32,5,1,128]{3,2,1,0:T(1,128)S(1)} async-done(((f32[32,5,1,128]{3,2,1,0:T(1,128)}), f32[32,5,1,128]{3,2,1,0:T(1,128)S(1)}, u32[]{:S(2)}, u32[]{:S(2)}) %all-to-all-start.2) | async-done | bytes 81952 | tf_op jit(solution)/shard_map/all_to_all | solution.py:176
  102.6 0.0 copy-done.2
  102.6 0.7 finish.1
Async XLA Ops:
  0.6 21.4 %collective-permute-start = (bf16[256,1024]{1,0:T(8,128)(2,1)}, bf16[256,1024]{1,0:T(8,128)(2,1)S(1)}, u32[]{:S(2)}, u32[]{:S(2)}) collective-permute-start(bf16[256,1024]{1,0:T(8,128)(2,1)} %emb_ref.1), channel_id=1, source_target_pairs={{0,1},{1,0},{2,3},{3,2},{4,5},{5,4},{6,7},{7,6},{8,9},{9,8},{10,11... | collective-permute-start | bytes 1572872 | tf_op jit(solution)/shard_map/ppermute | solution.py:146
  2.6 1.0 %copy-start = (bf16[256,1024]{1,0:T(8,128)(2,1)S(1)}, bf16[256,1024]{1,0:T(8,128)(2,1)}, u32[]{:S(2)}) copy-start(bf16[256,1024]{1,0:T(8,128)(2,1)} %emb_ref.1) | copy-start | bytes 1572868
  3.6 0.7 copy-start.3
  4.3 17.7 %copy-start.1 = (bf16[256,1024]{1,0:T(8,128)(2,1)S(1)}, bf16[256,1024]{1,0:T(8,128)(2,1)}, u32[]{:S(2)}) copy-start(bf16[256,1024]{1,0:T(8,128)(2,1)} %emb_ref.1) | copy-start | bytes 1572868
  5.3 28.2 %all-to-all-start = ((bf16[32,80,128]{2,1,0:T(8,128)(2,1)}), bf16[32,80,128]{2,1,0:T(8,128)(2,1)S(1)}, u32[]{:S(2)}, u32[]{:S(2)}) async-start(bf16[32,80,128]{2,1,0:T(8,128)(2,1)} %pack.1), calls=%async_computation | async-start | bytes 1310720 | tf_op jit(solution)/shard_map/all_to_all | solution.py:147
  39.2 35.0 %copy-start.5 = (s32[2,128]{1,0:T(2,128)S(1)}, s32[2,128]{1,0:T(2,128)}, u32[]{:S(2)}) copy-start(s32[2,128]{1,0:T(2,128)} %param.8) | copy-start | bytes 3076
  39.2 54.8 %copy-start.4 = (s32[2]{0:T(128)S(1)}, s32[2]{0:T(128)}, u32[]{:S(2)}) copy-start(s32[2]{0:T(128)} %len_ref.1) | copy-start | bytes 28
  39.2 14.0 %all-to-all-start.1 = ((f32[4,136,128]{2,1,0:T(8,128)}), f32[4,136,128]{2,1,0:T(8,128)S(1)}, u32[]{:S(2)}, u32[]{:S(2)}) async-start(f32[4,136,128]{2,1,0:T(8,128)} %sums.1), calls=%async_computation.1 | async-start | bytes 557056 | tf_op jit(solution)/shard_map/all_to_all | solution.py:165
  42.8 31.6 %collective-permute-start.3 = (bf16[512,1024]{1,0:T(8,128)(2,1)S(1)}, bf16[512,1024]{1,0:T(8,128)(2,1)S(1)}, u32[]{:S(2)}, u32[]{:S(2)}) collective-permute-start(bf16[512,1024]{1,0:T(8,128)(2,1)S(1)} %pad_maximum_fusion.refs_0_), channel_id=1, source_target_pairs={{0,4},{2,6},{4,0},{6,2},{1,5},{3,7},{5,1},{7,3},{8,12},{10,14},{12... | collective-permute-start | bytes 3145736 | tf_op jit(solution)/shard_map/ppermute | solution.py:164
  46.5 47.5 %collective-permute-start.2 = (bf16[512,1024]{1,0:T(8,128)(2,1)S(1)}, bf16[512,1024]{1,0:T(8,128)(2,1)}, u32[]{:S(2)}, u32[]{:S(2)}) collective-permute-start(bf16[512,1024]{1,0:T(8,128)(2,1)S(1)} %pad_maximum_fusion.refs_0_), channel_id=1, source_target_pairs={{0,6},{2,4},{4,2},{6,0},{1,7},{3,5},{5,3},{7,1},{8,14},{10,12},{12... | collective-permute-start | bytes 3145736 | tf_op jit(solution)/shard_map/ppermute | solution.py:164
  49.4 44.6 %collective-permute-start.1 = (bf16[512,1024]{1,0:T(8,128)(2,1)S(1)}, bf16[512,1024]{1,0:T(8,128)(2,1)}, u32[]{:S(2)}, u32[]{:S(2)}) collective-permute-start(bf16[512,1024]{1,0:T(8,128)(2,1)S(1)} %pad_maximum_fusion.refs_0_), channel_id=1, source_target_pairs={{0,2},{2,0},{4,6},{6,4},{1,3},{3,1},{5,7},{7,5},{8,10},{10,8},{12,... | collective-permute-start | bytes 3145736 | tf_op jit(solution)/shard_map/ppermute | solution.py:164
  53.9 48.6 %all-to-all-start.2 = ((f32[32,5,1,128]{3,2,1,0:T(1,128)}), f32[32,5,1,128]{3,2,1,0:T(1,128)S(1)}, u32[]{:S(2)}, u32[]{:S(2)}) async-start(f32[32,5,1,128]{3,2,1,0:T(1,128)} %bitcast.2), calls=%async_computation.2 | async-start | bytes 163840 | tf_op jit(solution)/shard_map/all_to_all | solution.py:176
  74.4 28.1 %copy-start.2 = (f32[16,128]{1,0:T(8,128)S(1)}, f32[16,128]{1,0:T(8,128)}, u32[]{:S(2)}) copy-start(f32[16,128]{1,0:T(8,128)} %old_ref.1) | copy-start | bytes 24580

commit v4 on v3

v4 whole, which is shorter than its diff:
```python
import jax
import jax.numpy as jnp
from jax import lax
from jax.experimental import pallas as pl
from jax.experimental.pallas import tpu as pltpu
from jax.sharding import Mesh, PartitionSpec as P

F32, BF16, I32 = jnp.float32, jnp.bfloat16, jnp.int32
SIZES = (8, 4, 4, 4, 2)
NAMES = ("zh", "zl", "x", "y", "c")
BLOCK = 32
ROWS = 256
FEATS = 32
MSG = 80
MIB = 1 << 20


def params(mib):
    return pltpu.CompilerParams(vmem_limit_bytes=mib * MIB)


def cost(flops, moved):
    return pl.CostEstimate(flops=flops, bytes_accessed=moved, transcendentals=0)


def pack_kernel(emb_hbm, label_hbm, rows_hbm, out_ref, emb_ref, label_ref, rows_ref, sems):
    pairs = ((emb_hbm, emb_ref), (label_hbm, label_ref), (rows_hbm, rows_ref))
    copies = [pltpu.make_async_copy(a, b, sems.at[k]) for k, (a, b) in enumerate(pairs)]
    for copy in copies:
        copy.start()
    for copy in copies:
        copy.wait()
    turned = emb_ref[...].T
    c, r = label_ref[...], rows_ref[...]
    high = ((c >> 6) & 3) * 64 + (c >> 8) * 8 + ((c >> 4) & 3) * 2 + (c & 1)
    low = ((c >> 1) & 1) * 4 + ((c >> 2) & 3)
    row = lax.broadcasted_iota(I32, (16, 128), 0)
    codes = jnp.zeros((16, 128), I32)
    for k, pair in enumerate((high, low, r >> 3, r & 7)):
        codes = jnp.where(row == 2 * k, pair[0:1], codes)
        codes = jnp.where(row == 2 * k + 1, pair[1:2], codes)
    codes = codes.astype(F32).astype(BF16)
    for x in range(4):
        for mp in range(8):
            d, f = x * 8 + mp, (mp * 4 + x) * FEATS
            out_ref[d, 0:32, :] = turned[f : f + FEATS, 0:128]
            out_ref[d, 32:64, :] = turned[f : f + FEATS, 128:256]
            out_ref[d, 64:80, :] = codes


def lanes(n):
    return lax.broadcasted_iota(I32, (n, 128), 0).astype(F32).astype(BF16)


def sum_kernel(from_ref, msg_ref, out_ref, rows_ref):
    cluster = lanes(256)
    one, zero = jnp.ones((), BF16), jnp.zeros((), BF16)
    contract = (((1,), (1,)), ((), ()))
    sums = jnp.zeros((256, 256), F32)
    counts = jnp.zeros((16, 128), F32)
    for first in range(0, BLOCK, 4):
        a, b, p, q = [], [], [], []
        for s in range(first, first + 4):
            codes = msg_ref[s, 64:80, :]
            for t in range(2):
                high, low = codes[t : t + 1], codes[2 + t : 3 + t]
                part = msg_ref[s, 32 * t : 32 * t + 32, :]
                a.append(jnp.where(cluster == high, one, zero))
                b.append(jnp.concatenate([jnp.where(low == jnp.asarray(g, BF16), part, zero) for g in range(8)], 0))
                h, g = high.astype(F32).astype(I32), low.astype(F32).astype(I32)
                within = ((h >> 1) & 7) * 16 + (g & 3) * 4 + (g >> 2) * 2 + (h & 1)
                p.append(jnp.where(cluster[0:16] == (h >> 4).astype(F32).astype(BF16), one, zero))
                q.append(jnp.where(cluster[0:128] == within.astype(F32).astype(BF16), one, zero))
        a, b, p, q = (jnp.concatenate(blocks, 1) for blocks in (a, b, p, q))
        sums = sums + lax.dot_general(a, b, contract, preferred_element_type=F32)
        counts = counts + lax.dot_general(p, q, contract, preferred_element_type=F32)
    for zl in range(4):
        out_ref[zl, 0:64, :] = sums[zl * 64 : zl * 64 + 64, 0:128]
        out_ref[zl, 64:128, :] = sums[zl * 64 : zl * 64 + 64, 128:256]
        out_ref[zl, 128:132, :] = counts[zl * 4 : zl * 4 + 4, :]
        out_ref[zl, 132:136, :] = jnp.zeros((4, 128), F32)
    codes = msg_ref[from_ref[0], 64:80, :].astype(F32).astype(I32)
    rows_ref[...] = codes[4:6] * 8 + codes[6:8]


def regroup_kernel(in_ref, out_ref, s_ref):
    s_ref[...] = (in_ref[0] + in_ref[1]) + (in_ref[2] + in_ref[3])
    for m in range(32):
        out_ref[5 * m : 5 * m + 2, :] = s_ref[2 * m : 2 * m + 2, :]
        out_ref[5 * m + 2 : 5 * m + 4, :] = s_ref[64 + 2 * m : 66 + 2 * m, :]
        out_ref[5 * m + 4 : 5 * m + 5, :] = s_ref[128 + m // 8 : 129 + m // 8, :]


def finish_kernel(at_ref, in_ref, old_ref, out_ref):
    slot = lax.broadcasted_iota(I32, (4, 128), 1) // FEATS
    parts = []
    for x in range(4):
        total = in_ref[5 * x : 5 * x + 4, :]
        for zh in range(1, 8):
            m = zh * 4 + x
            total = total + in_ref[5 * m : 5 * m + 4, :]
        parts.append(total)
    count_row = in_ref[4:5, :]
    for zh in range(1, 8):
        count_row = count_row + in_ref[20 * zh + 4 : 20 * zh + 5, :]
    lane = lax.broadcasted_iota(I32, (16, 128), 1)
    own = lane == at_ref[0] + lax.broadcasted_iota(I32, (16, 128), 0)
    counts = jnp.sum(jnp.where(own, count_row, 0.0), axis=1, keepdims=True)
    for low in range(4):
        rows = jnp.zeros((4, 128), F32)
        for x in range(4):
            shift = ((x - low) * FEATS) % 128
            moved = pltpu.roll(parts[x], shift, 1) if shift else parts[x]
            rows = jnp.where(slot == x, moved, rows)
        j = slice(4 * low, 4 * low + 4)
        out_ref[j, :] = (rows + old_ref[j, :]) / (counts[j] + 1.0)


def member_kernel(place_ref, mine_ref, theirs_ref, *refs):
    *line_refs, own_ref, other_ref = refs
    core, y = place_ref[0], place_ref[1]
    lane = lax.broadcasted_iota(I32, (128, ROWS), 1)
    for out, r in ((own_ref, mine_ref[...]), (other_ref, theirs_ref[...])):
        at = jnp.where(((r >> 8) & 1) == core, (((r >> 9) ^ y) << 8) + (r & 255), -1)
        at = jnp.concatenate([at, jnp.zeros((6, 128), I32)], 0).astype(F32).T.astype(I32)
        for s in range(2):
            total = jnp.zeros((128, 1024), F32)
            for away, line_ref in zip((0, 1, 3, 2), line_refs):
                pick = jnp.where(lane + 256 * away == at[:, s : s + 1], 1.0, 0.0).astype(BF16)
                total = total + jnp.dot(pick, line_ref[...], preferred_element_type=F32)
            out[128 * s : 128 * s + 128, :] = total.astype(BF16)


def match_kernel(len_ref, own_ref, other_ref, out_ref):
    members = own_ref[...] + other_ref[...]
    i = lax.broadcasted_iota(I32, (128, 128), 0)
    j = lax.broadcasted_iota(I32, (128, 128), 1)
    for s in range(2):
        one = members[128 * s : 128 * s + 128]
        gram = lax.dot_general(one, one, (((1,), (1,)), ((), ())), preferred_element_type=F32)
        diagonal = jnp.where(i == j, gram, 0.0)
        down = lax.rsqrt(jnp.sum(diagonal, axis=1, keepdims=True) + 1e-06)
        across = lax.rsqrt(jnp.sum(diagonal, axis=0, keepdims=True) + 1e-06)
        cosine = gram * down * across
        length = len_ref[s]
        largest = jnp.max(jnp.where((i < length) & (i != j), cosine, -2.0), axis=0, keepdims=True)
        out_ref[s : s + 1, :] = jnp.where(j[0:1] < length, largest, 0.0)


VMEM = pl.BlockSpec(memory_space=pltpu.VMEM)
HBM = pl.BlockSpec(memory_space=pltpu.HBM)
SMEM = pl.BlockSpec(memory_space=pltpu.SMEM)


def local(embeddings, assignments, old_centroids, slab_rows, slab_len):
    zh, x, y, core = (lax.axis_index(name).astype(I32) for name in ("zh", "x", "y", "c"))
    messages = pl.pallas_call(
        pack_kernel,
        out_shape=pltpu.VMEM((BLOCK, MSG, 128), BF16),
        in_specs=[HBM] * 3,
        out_specs=VMEM,
        scratch_shapes=[
            pltpu.VMEM((ROWS, 1024), BF16),
            pltpu.VMEM((2, 128), I32),
            pltpu.VMEM((2, 128), I32),
            pltpu.SemaphoreType.DMA((3,)),
        ],
        compiler_params=params(8),
        cost_estimate=cost(1 << 20, 3 << 19),
        name="pack",
    )(*(pltpu.with_memory_space_constraint(a, pltpu.HBM) for a in (embeddings, assignments.reshape(2, 128), slab_rows)))
    messages = lax.all_to_all(messages, ("x", "y", "c"), 0, 0, tiled=True)
    parts, other_rows = pl.pallas_call(
        sum_kernel,
        out_shape=(pltpu.VMEM((4, 136, 128), F32), pltpu.VMEM((2, 128), I32)),
        in_specs=[SMEM, VMEM],
        out_specs=(VMEM, VMEM),
        compiler_params=params(20),
        cost_estimate=cost(1 << 31, 1 << 20),
        name="sums",
    )((x * 8 + y * 2 + 1 - core).reshape(1), messages)
    embeddings, parts = lax.optimization_barrier((embeddings, parts))
    line = [embeddings] + [lax.ppermute(embeddings, "y", [(i, i ^ d) for i in range(4)]) for d in (1, 3, 2)]
    parts = lax.all_to_all(parts, "zl", 0, 0, tiled=True)
    parts = pl.pallas_call(
        regroup_kernel,
        out_shape=pltpu.VMEM((160, 128), F32),
        in_specs=[VMEM],
        out_specs=VMEM,
        scratch_shapes=[pltpu.VMEM((136, 128), F32)],
        compiler_params=params(4),
        cost_estimate=cost(1 << 18, 1 << 19),
        name="regroup",
    )(parts)
    parts = lax.all_to_all(parts.reshape(32, 5, 1, 128), ("zh", "x"), 0, 0, tiled=True)
    members = jax.ShapeDtypeStruct((256, 1024), BF16)
    own, other = pl.pallas_call(
        member_kernel,
        out_shape=(members, members),
        in_specs=[SMEM] + [VMEM] * 6,
        out_specs=(VMEM, VMEM),
        compiler_params=params(16),
        cost_estimate=cost(1 << 31, 3 << 20),
        name="members",
    )(jnp.stack([core, y]), slab_rows, other_rows, *line)
    other = lax.ppermute(other, "c", [(0, 1), (1, 0)])
    best_cosine = pl.pallas_call(
        match_kernel,
        out_shape=jax.ShapeDtypeStruct((2, 128), F32),
        in_specs=[SMEM, VMEM, VMEM],
        out_specs=VMEM,
        compiler_params=params(8),
        cost_estimate=cost(1 << 20, 1 << 20),
        name="match",
    )(slab_len, own, other)
    parts, best_cosine = lax.optimization_barrier((parts, best_cosine))
    centroids = pl.pallas_call(
        finish_kernel,
        out_shape=jax.ShapeDtypeStruct((16, 128), F32),
        in_specs=[SMEM, VMEM, VMEM],
        out_specs=VMEM,
        compiler_params=params(4),
        cost_estimate=cost(1 << 18, 1 << 18),
        name="finish",
    )((((zh & 1) * 4 + x) * 16).reshape(1), parts.reshape(160, 128), old_centroids)
    return (centroids, best_cosine)


def solution(mesh):
    fine = Mesh(mesh.devices.reshape(SIZES), NAMES)
    dp, mp = ("zh", "zl", "x"), ("y", "c")
    placed = (
        P(dp + mp, None),
        P(dp + mp),
        P(dp, mp),
        P(dp + mp, None),
        P(dp + mp),
    )
    return jax.shard_map(
        local,
        mesh=fine,
        in_specs=placed,
        out_specs=(P(dp, mp), P(dp + mp, None)),
        check_vma=False,
    )
```

time: 104 us -> 98 us (0.942)
  Pallas kernels: 11.8 us -> 9.54 us
  waiting for transfers between devices: 35.8 us -> 33.7 us
  local copies, waits for them, and re-layouts: 1.86 us -> 0.66 us
    ppermute x4, waiting for transfers between devices: 19.6 us -> 1.86 us  [the longest x1 1.85 us: local(): other = lax.ppermute(other, 'c', [(0, 1), (1, 0)])]
    all_to_all x1, waiting for transfers between devices: 4.83 us -> 20.4 us  [local(): lax.all_to_all(parts.reshape(32, 5, 1, 128), ('zh', 'x'), 0, 0, tiled=True)]
    pallas_call x1, Pallas kernels: 3.71 us -> 1.52 us  [local(): pl.pallas_call(match_kernel, out_shape=jax.ShapeDtypeStruct((2, 128), F32...]
    unnamed x12 -> x8, local copies, waits for them, and re-layouts: 1.73 us -> 0.66 us
    pallas_call x3 -> x4, Pallas kernels: 7.41 us -> 7.32 us  [the longest x1 2.54 us: local(): pl.pallas_call(sum_kernel, out_shape=(pltpu.VMEM((4, 136, 128), F32), plt...]
  transfers between devices with their start and end apart: 7 -> 7, of which waited for: 3 -> 3; matrix products, arithmetic and copies ran while one was open for 0% -> 0% of each run, Pallas kernels for 5% -> 4%
where the time goes in v4:
time: 98 us; the launch traced here: 97.5 us
  starting transfers between devices  52.7 us (54%)
  waiting for transfers between devices  33.7 us (34%)
  Pallas kernels  9.54 us (10%)
    all_to_all x1, waiting for transfers between devices, local(): lax.all_to_all(parts.reshape(32, 5, 1, 128), ('zh', 'x'), 0, 0, tiled=True)  20.4 us
    all_to_all x1, starting transfers between devices, local(): lax.all_to_all(parts.reshape(32, 5, 1, 128), ('zh', 'x'), 0, 0, tiled=True)  20.1 us
    all_to_all x1, starting transfers between devices, local(): messages = lax.all_to_all(messages, ('x', 'y', 'c'), 0, 0, tiled=True)  16.7 us
    all_to_all x1, waiting for transfers between devices, local(): messages = lax.all_to_all(messages, ('x', 'y', 'c'), 0, 0, tiled=True)  11.5 us
    ppermute x3, starting transfers between devices, local(): lax.ppermute(embeddings, 'y', [(i, i ^ d) for i in range(4)])  10.4 us
    all_to_all x1, starting transfers between devices, local(): parts = lax.all_to_all(parts, 'zl', 0, 0, tiled=True)  3.58 us
    pallas_call x1, Pallas kernels, local(): pl.pallas_call(sum_kernel, out_shape=(pltpu.VMEM((4, 136, 128), F32), plt...  2.54 us
    pallas_call x1, Pallas kernels, local(): pl.pallas_call(pack_kernel, out_shape=pltpu.VMEM((BLOCK, MSG, 128), BF16)...  2.11 us
  transfers between devices with their start and end apart: 7, of which 3 were waited for; matrix products, arithmetic and copies ran while one was open for 0% of the time, Pallas kernels for 4%

profile of v4, /device:TPU:8, one launch (start us, length us, event | category | flops | bytes accessed | tf_op | source)
XLA Modules:
  0.0 97.5 jit_solution(10813374720260726691)
XLA Ops:
  0.6 2.1 %pack.1 = bf16[32,80,128]{2,1,0:T(8,128)(2,1)} custom-call(bf16[256,1024]{1,0:T(8,128)(2,1)} %refs_0_, s32[2,128]{1,0:T(2,128)} %bitcast.8, s32[2,128]{1,0:T(2,128)} %mine_ref.1), custom_call_target="tpu_custom_call" | custom-call | flops 1048576 | bytes 1572864 | tf_op jit(solution)/shard_map/pack/pallas_call | solution.py:157
  2.7 16.7 %all-to-all-start = ((bf16[32,80,128]{2,1,0:T(8,128)(2,1)}), bf16[32,80,128]{2,1,0:T(8,128)(2,1)S(1)}, u32[]{:S(2)}, u32[]{:S(2)}) async-start(bf16[32,80,128]{2,1,0:T(8,128)(2,1)} %pack.1), calls=%async_computation | async-start | bytes 1310720 | tf_op jit(solution)/shard_map/all_to_all | solution.py:172
  19.4 11.5 %all-to-all-done.msg_ref = bf16[32,80,128]{2,1,0:T(8,128)(2,1)S(1)} async-done(((bf16[32,80,128]{2,1,0:T(8,128)(2,1)}), bf16[32,80,128]{2,1,0:T(8,128)(2,1)S(1)}, u32[]{:S(2)}, u32[]{:S(2)}) %all-to-all-start) | async-done | bytes 655392 | tf_op jit(solution)/shard_map/all_to_all | solution.py:172
  30.9 2.5 %sums.1 = (f32[4,136,128]{2,1,0:T(8,128)}, s32[2,128]{1,0:T(2,128)S(1)}) custom-call(s32[1]{0:T(128)} %bitcast.1.from_ref, bf16[32,80,128]{2,1,0:T(8,128)(2,1)S(1)} %all-to-all-done.msg_ref), custom_call_target="tpu_custom_call" | custom-call | flops 2147483648 | bytes 1048576 | tf_op jit(solution)/shard_map/sums/pallas_call | solution.py:173
  33.5 0.0 copy-start
  33.5 3.6 %all-to-all-start.1 = ((f32[4,136,128]{2,1,0:T(8,128)}), f32[4,136,128]{2,1,0:T(8,128)S(1)}, u32[]{:S(2)}, u32[]{:S(2)}) async-start(f32[4,136,128]{2,1,0:T(8,128)} %get-tuple-element.11), calls=%async_computation.1 | async-start | bytes 557056 | tf_op jit(solution)/shard_map/all_to_all | solution.py:184
  37.1 0.0 copy-done
  37.1 3.7 %collective-permute-start.2 = (bf16[256,1024]{1,0:T(8,128)(2,1)S(1)}, bf16[256,1024]{1,0:T(8,128)(2,1)S(1)}, u32[]{:S(2)}, u32[]{:S(2)}) collective-permute-start(bf16[256,1024]{1,0:T(8,128)(2,1)S(1)} %copy-done), channel_id=1, source_target_pairs={{0,4},{2,6},{4,0},{6,2},{1,5},{3,7},{5,1},{7,3},{8,12},{10,14},{12... | collective-permute-start | bytes 1572872 | tf_op jit(solution)/shard_map/ppermute | solution.py:183
  40.8 2.9 %collective-permute-start.1 = (bf16[256,1024]{1,0:T(8,128)(2,1)S(1)}, bf16[256,1024]{1,0:T(8,128)(2,1)S(1)}, u32[]{:S(2)}, u32[]{:S(2)}) collective-permute-start(bf16[256,1024]{1,0:T(8,128)(2,1)S(1)} %copy-done), channel_id=1, source_target_pairs={{0,6},{2,4},{4,2},{6,0},{1,7},{3,5},{5,3},{7,1},{8,14},{10,12},{12... | collective-permute-start | bytes 1572872 | tf_op jit(solution)/shard_map/ppermute | solution.py:183
  43.7 3.8 %collective-permute-start = (bf16[256,1024]{1,0:T(8,128)(2,1)S(1)}, bf16[256,1024]{1,0:T(8,128)(2,1)S(1)}, u32[]{:S(2)}, u32[]{:S(2)}) collective-permute-start(bf16[256,1024]{1,0:T(8,128)(2,1)S(1)} %copy-done), channel_id=1, source_target_pairs={{0,2},{2,0},{4,6},{6,4},{1,3},{3,1},{5,7},{7,5},{8,10},{10,8},{12,... | collective-permute-start | bytes 1572872 | tf_op jit(solution)/shard_map/ppermute | solution.py:183
  47.5 0.1 pad_add_fusion.place_ref
  47.6 0.0 all-to-all-done.1.in_ref
  47.6 0.7 regroup.1
  48.3 20.1 %all-to-all-start.2 = ((f32[32,5,1,128]{3,2,1,0:T(1,128)}), f32[32,5,1,128]{3,2,1,0:T(1,128)S(1)}, u32[]{:S(2)}, u32[]{:S(2)}) async-start(f32[32,5,1,128]{3,2,1,0:T(1,128)} %bitcast.3), calls=%async_computation.2 | async-start | bytes 163840 | tf_op jit(solution)/shard_map/all_to_all | solution.py:195
  68.4 0.0 copy-start.2
  68.4 0.0 collective-permute-done.2.refs_3_
  68.4 0.0 collective-permute-done.1.refs_2_
  68.4 0.0 collective-permute-done.refs_1_
  68.4 0.6 copy-done.2
  69.0 2.0 %members.1 = (bf16[256,1024]{1,0:T(8,128)(2,1)S(1)}, bf16[256,1024]{1,0:T(8,128)(2,1)S(1)}) custom-call(s32[2]{0:T(128)S(1)} %pad_add_fusion.place_ref, s32[2,128]{1,0:T(2,128)S(1)} %copy-done.2, s32[2,128]{1,0:T(2,128)S(1)} %get-tuple-element.12.theirs_ref, bf16[256,1024]{1,0:T(8,128)(2,1)S(1)} %copy-done, ...), custom_call_target="tpu_custom_call" | custom-call | flops 2147483648 | bytes 3145728 | tf_op jit(solution)/shard_map/members/pallas_call | solution.py:197
  71.1 1.9 %collective-permute-start.3 = (bf16[256,1024]{1,0:T(8,128)(2,1)S(1)}, bf16[256,1024]{1,0:T(8,128)(2,1)S(1)}, u32[]{:S(2)}, u32[]{:S(2)}) collective-permute-start(bf16[256,1024]{1,0:T(8,128)(2,1)S(1)} %get-tuple-element.15), channel_id=1, source_target_pairs={{0,1},{1,0},{2,3},{3,2},{4,5},{5,4},{6,7},{7,6},{8,9},{9,8},{10,11... | collective-permute-start | bytes 1572872 | tf_op jit(solution)/shard_map/ppermute | solution.py:206
  73.0 0.0 copy-start.3
  73.0 1.9 %collective-permute-done.3.other_ref = bf16[256,1024]{1,0:T(8,128)(2,1)S(1)} collective-permute-done((bf16[256,1024]{1,0:T(8,128)(2,1)S(1)}, bf16[256,1024]{1,0:T(8,128)(2,1)S(1)}, u32[]{:S(2)}, u32[]{:S(2)}) %collective-permute-start.3) | collective-permute-done | bytes 524320 | tf_op jit(solution)/shard_map/ppermute | solution.py:206
  74.9 0.0 copy-done.3
  74.9 0.0 copy-start.1
  74.9 1.5 %match.1 = f32[2,128]{1,0:T(2,128)} custom-call(s32[2]{0:T(128)S(1)} %copy-done.3, bf16[256,1024]{1,0:T(8,128)(2,1)S(1)} %get-tuple-element.14.own_ref, bf16[256,1024]{1,0:T(8,128)(2,1)S(1)} %collective-permute-done.3.other_ref), custom_call_target="tpu_custom_call" | custom-call | flops 1048576 | bytes 1048576 | tf_op jit(solution)/shard_map/match/pallas_call | solution.py:207
  76.4 20.4 %all-to-all-done.2 = f32[32,5,1,128]{3,2,1,0:T(1,128)S(1)} async-done(((f32[32,5,1,128]{3,2,1,0:T(1,128)}), f32[32,5,1,128]{3,2,1,0:T(1,128)S(1)}, u32[]{:S(2)}, u32[]{:S(2)}) %all-to-all-start.2) | async-done | bytes 81952 | tf_op jit(solution)/shard_map/all_to_all | solution.py:195
  96.8 0.0 copy-done.1
  96.8 0.7 finish.1
Async XLA Ops:
  2.7 28.2 %all-to-all-start = ((bf16[32,80,128]{2,1,0:T(8,128)(2,1)}), bf16[32,80,128]{2,1,0:T(8,128)(2,1)S(1)}, u32[]{:S(2)}, u32[]{:S(2)}) async-start(bf16[32,80,128]{2,1,0:T(8,128)(2,1)} %pack.1), calls=%async_computation | async-start | bytes 1310720 | tf_op jit(solution)/shard_map/all_to_all | solution.py:172
  33.5 3.6 %copy-start = (bf16[256,1024]{1,0:T(8,128)(2,1)S(1)}, bf16[256,1024]{1,0:T(8,128)(2,1)}, u32[]{:S(2)}) copy-start(bf16[256,1024]{1,0:T(8,128)(2,1)} %refs_0_) | copy-start | bytes 1572868
  33.5 14.1 %all-to-all-start.1 = ((f32[4,136,128]{2,1,0:T(8,128)}), f32[4,136,128]{2,1,0:T(8,128)S(1)}, u32[]{:S(2)}, u32[]{:S(2)}) async-start(f32[4,136,128]{2,1,0:T(8,128)} %get-tuple-element.11), calls=%async_computation.1 | async-start | bytes 557056 | tf_op jit(solution)/shard_map/all_to_all | solution.py:184
  37.1 31.3 %collective-permute-start.2 = (bf16[256,1024]{1,0:T(8,128)(2,1)S(1)}, bf16[256,1024]{1,0:T(8,128)(2,1)S(1)}, u32[]{:S(2)}, u32[]{:S(2)}) collective-permute-start(bf16[256,1024]{1,0:T(8,128)(2,1)S(1)} %copy-done), channel_id=1, source_target_pairs={{0,4},{2,6},{4,0},{6,2},{1,5},{3,7},{5,1},{7,3},{8,12},{10,14},{12... | collective-permute-start | bytes 1572872 | tf_op jit(solution)/shard_map/ppermute | solution.py:183
  40.8 27.6 %collective-permute-start.1 = (bf16[256,1024]{1,0:T(8,128)(2,1)S(1)}, bf16[256,1024]{1,0:T(8,128)(2,1)S(1)}, u32[]{:S(2)}, u32[]{:S(2)}) collective-permute-start(bf16[256,1024]{1,0:T(8,128)(2,1)S(1)} %copy-done), channel_id=1, source_target_pairs={{0,6},{2,4},{4,2},{6,0},{1,7},{3,5},{5,3},{7,1},{8,14},{10,12},{12... | collective-permute-start | bytes 1572872 | tf_op jit(solution)/shard_map/ppermute | solution.py:183
  43.7 24.7 %collective-permute-start = (bf16[256,1024]{1,0:T(8,128)(2,1)S(1)}, bf16[256,1024]{1,0:T(8,128)(2,1)S(1)}, u32[]{:S(2)}, u32[]{:S(2)}) collective-permute-start(bf16[256,1024]{1,0:T(8,128)(2,1)S(1)} %copy-done), channel_id=1, source_target_pairs={{0,2},{2,0},{4,6},{6,4},{1,3},{3,1},{5,7},{7,5},{8,10},{10,8},{12,... | collective-permute-start | bytes 1572872 | tf_op jit(solution)/shard_map/ppermute | solution.py:183
  48.3 48.5 %all-to-all-start.2 = ((f32[32,5,1,128]{3,2,1,0:T(1,128)}), f32[32,5,1,128]{3,2,1,0:T(1,128)S(1)}, u32[]{:S(2)}, u32[]{:S(2)}) async-start(f32[32,5,1,128]{3,2,1,0:T(1,128)} %bitcast.3), calls=%async_computation.2 | async-start | bytes 163840 | tf_op jit(solution)/shard_map/all_to_all | solution.py:195
  68.4 0.7 copy-start.2
  71.1 3.8 %collective-permute-start.3 = (bf16[256,1024]{1,0:T(8,128)(2,1)S(1)}, bf16[256,1024]{1,0:T(8,128)(2,1)S(1)}, u32[]{:S(2)}, u32[]{:S(2)}) collective-permute-start(bf16[256,1024]{1,0:T(8,128)(2,1)S(1)} %get-tuple-element.15), channel_id=1, source_target_pairs={{0,1},{1,0},{2,3},{3,2},{4,5},{5,4},{6,7},{7,6},{8,9},{9,8},{10,11... | collective-permute-start | bytes 1572872 | tf_op jit(solution)/shard_map/ppermute | solution.py:206
  73.0 1.9 %copy-start.3 = (s32[2]{0:T(128)S(1)}, s32[2]{0:T(128)}, u32[]{:S(2)}) copy-start(s32[2]{0:T(128)} %len_ref.1) | copy-start | bytes 28
  74.9 21.9 %copy-start.1 = (f32[16,128]{1,0:T(8,128)S(1)}, f32[16,128]{1,0:T(8,128)}, u32[]{:S(2)}) copy-start(f32[16,128]{1,0:T(8,128)} %old_ref.1) | copy-start | bytes 24580

commit v5 on v4

v5 whole, which is shorter than its diff:
```python
import jax
import jax.numpy as jnp
from jax import lax
from jax.experimental import pallas as pl
from jax.experimental.pallas import tpu as pltpu
from jax.sharding import Mesh, PartitionSpec as P

F32, BF16, I32 = jnp.float32, jnp.bfloat16, jnp.int32
SIZES = (8, 4, 4, 4, 2)
NAMES = ("zh", "zl", "x", "y", "c")
BLOCK = 32
ROWS = 256
FEATS = 32
MSG = 80
MIB = 1 << 20


def params(mib):
    return pltpu.CompilerParams(vmem_limit_bytes=mib * MIB)


def cost(flops, moved):
    return pl.CostEstimate(flops=flops, bytes_accessed=moved, transcendentals=0)


def pack_kernel(emb_hbm, label_hbm, rows_hbm, out_hbm, emb_ref, label_ref, rows_ref, msg_ref, in_sems, out_sems, sems):
    small = [
        pltpu.make_async_copy(label_hbm, label_ref, sems.at[0]),
        pltpu.make_async_copy(rows_hbm, rows_ref, sems.at[1]),
    ]
    blocks = [
        pltpu.make_async_copy(emb_hbm.at[:, pl.ds(128 * mp, 128)], emb_ref.at[mp], in_sems.at[mp]) for mp in range(8)
    ]
    for copy in small + blocks:
        copy.start()
    for copy in small:
        copy.wait()
    c, r = label_ref[...], rows_ref[...]
    high = ((c >> 6) & 3) * 64 + ((c >> 4) & 3) * 16 + (c >> 8) * 2 + (c & 1)
    low = ((c >> 1) & 1) * 4 + ((c >> 2) & 3)
    row = lax.broadcasted_iota(I32, (16, 128), 0)
    codes = jnp.zeros((16, 128), I32)
    for k, pair in enumerate((high, low, r >> 3, r & 7)):
        codes = jnp.where(row == 2 * k, pair[0:1], codes)
        codes = jnp.where(row == 2 * k + 1, pair[1:2], codes)
    codes = codes.astype(F32).astype(BF16)
    sent = []
    for mp in range(8):
        blocks[mp].wait()
        turned = emb_ref[mp].T
        for x in range(4):
            part = turned[x * FEATS : x * FEATS + FEATS]
            msg_ref[mp, x, 0:32, :] = part[:, 0:128]
            msg_ref[mp, x, 32:64, :] = part[:, 128:256]
            msg_ref[mp, x, 64:80, :] = codes
        sent.append(pltpu.make_async_copy(msg_ref.at[mp], out_hbm.at[:, mp], out_sems.at[mp]))
        sent[mp].start()
    for copy in sent:
        copy.wait()


def lanes(n):
    return lax.broadcasted_iota(I32, (n, 128), 0).astype(F32).astype(BF16)


def sum_kernel(from_ref, msg_ref, out_ref, rows_ref):
    cluster = lanes(256)
    one, zero = jnp.ones((), BF16), jnp.zeros((), BF16)
    contract = (((1,), (1,)), ((), ()))
    sums = jnp.zeros((256, 256), F32)
    counts = jnp.zeros((16, 128), F32)
    for first in range(0, BLOCK, 4):
        a, b, p, q = [], [], [], []
        for s in range(first, first + 4):
            codes = msg_ref[s, 64:80, :]
            for t in range(2):
                high, low = codes[t : t + 1], codes[2 + t : 3 + t]
                part = msg_ref[s, 32 * t : 32 * t + 32, :]
                a.append(jnp.where(cluster == high, one, zero))
                b.append(jnp.concatenate([jnp.where(low == jnp.asarray(g, BF16), part, zero) for g in range(8)], 0))
                h, g = high.astype(F32).astype(I32), low.astype(F32).astype(I32)
                within = ((h >> 1) & 7) * 16 + (g & 3) * 4 + (g >> 2) * 2 + (h & 1)
                p.append(jnp.where(cluster[0:16] == (h >> 4).astype(F32).astype(BF16), one, zero))
                q.append(jnp.where(cluster[0:128] == within.astype(F32).astype(BF16), one, zero))
        a, b, p, q = (jnp.concatenate(blocks, 1) for blocks in (a, b, p, q))
        sums = sums + lax.dot_general(a, b, contract, preferred_element_type=F32)
        counts = counts + lax.dot_general(p, q, contract, preferred_element_type=F32)
    for m in range(16):
        out_ref[33 * m : 33 * m + 16, :] = sums[16 * m : 16 * m + 16, 0:128]
        out_ref[33 * m + 16 : 33 * m + 32, :] = sums[16 * m : 16 * m + 16, 128:256]
        out_ref[33 * m + 32 : 33 * m + 33, :] = counts[m : m + 1, :]
    codes = msg_ref[from_ref[0], 64:80, :].astype(F32).astype(I32)
    rows_ref[...] = codes[4:6] * 8 + codes[6:8]


def regroup_kernel(in_ref, out_ref, s_ref):
    slot = lax.broadcasted_iota(I32, (32, 128), 1) // FEATS
    parts = []
    for x in range(4):
        first, *others = (in_ref[33 * (4 * zl + x) : 33 * (4 * zl + x) + 32, :] for zl in range(4))
        parts.append((first + others[0]) + (others[1] + others[2]))
    first, *others = (in_ref[33 * 4 * zl + 32 : 33 * 4 * zl + 33, :] for zl in range(4))
    counts = (first + others[0]) + (others[1] + others[2])
    for low in range(4):
        rows = jnp.zeros((32, 128), F32)
        for x in range(4):
            shift = ((x - low) * FEATS) % 128
            moved = pltpu.roll(parts[x], shift, 1) if shift else parts[x]
            rows = jnp.where(slot == x, moved, rows)
        s_ref[...] = rows
        for zh in range(8):
            for r1 in range(2):
                at = 17 * zh + 4 * low + 2 * r1
                out_ref[at : at + 2, :] = s_ref[16 * r1 + 2 * zh : 16 * r1 + 2 * zh + 2, :]
    for zh in range(8):
        out_ref[17 * zh + 16 : 17 * zh + 17, :] = counts


def finish_kernel(at_ref, in_ref, old_ref, out_ref):
    sums, count_row = in_ref[0:16, :], in_ref[16:17, :]
    for zh in range(1, 8):
        sums = sums + in_ref[17 * zh : 17 * zh + 16, :]
        count_row = count_row + in_ref[17 * zh + 16 : 17 * zh + 17, :]
    lane = lax.broadcasted_iota(I32, (16, 128), 1)
    own = lane == at_ref[0] + lax.broadcasted_iota(I32, (16, 128), 0)
    counts = jnp.sum(jnp.where(own, count_row, 0.0), axis=1, keepdims=True)
    out_ref[...] = (sums + old_ref[...]) / (counts + 1.0)


def member_kernel(after_ref, place_ref, mine_ref, theirs_ref, *refs):
    *line_refs, own_ref, first_ref, second_ref = refs
    core, y = place_ref[0], place_ref[1]
    lane = lax.broadcasted_iota(I32, (128, ROWS), 1)
    outs = (own_ref.at[0:128], own_ref.at[128:256], first_ref, second_ref)
    for k, r in enumerate((mine_ref[...], theirs_ref[...])):
        at = jnp.where(((r >> 8) & 1) == core, (((r >> 9) ^ y) << 8) + (r & 255), -1)
        at = jnp.concatenate([at, jnp.zeros((6, 128), I32)], 0).astype(F32).T.astype(I32)
        for s in range(2):
            total = jnp.zeros((128, 1024), F32)
            for away, line_ref in zip((0, 1, 3, 2), line_refs):
                pick = jnp.where(lane + 256 * away == at[:, s : s + 1], 1.0, 0.0).astype(BF16)
                total = total + jnp.dot(pick, line_ref[...], preferred_element_type=F32)
            outs[2 * k + s][...] = total.astype(BF16)


def match_kernel(len_ref, own_ref, first_ref, second_ref, out_ref):
    i = lax.broadcasted_iota(I32, (128, 128), 0)
    j = lax.broadcasted_iota(I32, (128, 128), 1)
    for s, other_ref in enumerate((first_ref, second_ref)):
        one = own_ref[128 * s : 128 * s + 128, :] + other_ref[...]
        gram = lax.dot_general(one, one, (((1,), (1,)), ((), ())), preferred_element_type=F32)
        diagonal = jnp.where(i == j, gram, 0.0)
        down = lax.rsqrt(jnp.sum(diagonal, axis=1, keepdims=True) + 1e-06)
        across = lax.rsqrt(jnp.sum(diagonal, axis=0, keepdims=True) + 1e-06)
        cosine = gram * down * across
        length = len_ref[s]
        largest = jnp.max(jnp.where((i < length) & (i != j), cosine, -2.0), axis=0, keepdims=True)
        out_ref[s : s + 1, :] = jnp.where(j[0:1] < length, largest, 0.0)


VMEM = pl.BlockSpec(memory_space=pltpu.VMEM)
HBM = pl.BlockSpec(memory_space=pltpu.HBM)
SMEM = pl.BlockSpec(memory_space=pltpu.SMEM)


def local(embeddings, assignments, old_centroids, slab_rows, slab_len):
    zh, x, y, core = (lax.axis_index(name).astype(I32) for name in ("zh", "x", "y", "c"))
    messages = pl.pallas_call(
        pack_kernel,
        out_shape=pltpu.HBM((4, 8, MSG, 128), BF16),
        in_specs=[HBM] * 3,
        out_specs=HBM,
        scratch_shapes=[
            pltpu.VMEM((8, ROWS, 128), BF16),
            pltpu.VMEM((2, 128), I32),
            pltpu.VMEM((2, 128), I32),
            pltpu.VMEM((8, 4, MSG, 128), BF16),
            pltpu.SemaphoreType.DMA((8,)),
            pltpu.SemaphoreType.DMA((8,)),
            pltpu.SemaphoreType.DMA((2,)),
        ],
        compiler_params=params(8),
        cost_estimate=cost(1 << 20, 3 << 19),
        name="pack",
    )(*(pltpu.with_memory_space_constraint(a, pltpu.HBM) for a in (embeddings, assignments.reshape(2, 128), slab_rows)))
    messages = lax.all_to_all(messages.reshape(BLOCK, MSG, 128), ("x", "y", "c"), 0, 0, tiled=True)
    parts, other_rows = pl.pallas_call(
        sum_kernel,
        out_shape=(pltpu.VMEM((528, 128), F32), pltpu.VMEM((2, 128), I32)),
        in_specs=[SMEM, VMEM],
        out_specs=(VMEM, VMEM),
        compiler_params=params(20),
        cost_estimate=cost(1 << 31, 1 << 20),
        name="sums",
    )((x * 8 + y * 2 + 1 - core).reshape(1), messages)
    embeddings, parts = lax.optimization_barrier((embeddings, parts))
    line = [embeddings] + [lax.ppermute(embeddings, "y", [(i, i ^ d) for i in range(4)]) for d in (1, 3, 2)]
    parts = lax.all_to_all(parts.reshape(16, 33, 1, 128), ("zl", "x"), 0, 0, tiled=True)
    parts = pl.pallas_call(
        regroup_kernel,
        out_shape=pltpu.VMEM((136, 128), F32),
        in_specs=[VMEM],
        out_specs=VMEM,
        scratch_shapes=[pltpu.VMEM((32, 128), F32)],
        compiler_params=params(4),
        cost_estimate=cost(1 << 18, 1 << 19),
        name="regroup",
    )(parts.reshape(528, 128))
    after = parts
    parts = lax.all_to_all(parts.reshape(8, 17, 1, 128), "zh", 0, 0, tiled=True)
    members = [jax.ShapeDtypeStruct((n, 1024), BF16) for n in (256, 128, 128)]
    own, *others = pl.pallas_call(
        member_kernel,
        out_shape=members,
        in_specs=[pl.BlockSpec(memory_space=pl.ANY), SMEM] + [VMEM] * 6,
        out_specs=[VMEM] * 3,
        compiler_params=params(16),
        cost_estimate=cost(0, 0),
        name="members",
    )(after, jnp.stack([core, y]), slab_rows, other_rows, *line)
    others = [lax.ppermute(other, "c", [(0, 1), (1, 0)]) for other in others]
    best_cosine = pl.pallas_call(
        match_kernel,
        out_shape=jax.ShapeDtypeStruct((2, 128), F32),
        in_specs=[SMEM] + [VMEM] * 3,
        out_specs=VMEM,
        compiler_params=params(8),
        cost_estimate=cost(0, 0),
        name="match",
    )(slab_len, own, *others)
    parts, best_cosine = lax.optimization_barrier((parts, best_cosine))
    centroids = pl.pallas_call(
        finish_kernel,
        out_shape=jax.ShapeDtypeStruct((16, 128), F32),
        in_specs=[SMEM, VMEM, VMEM],
        out_specs=VMEM,
        compiler_params=params(4),
        cost_estimate=cost(1 << 18, 1 << 18),
        name="finish",
    )((zh * 16).reshape(1), parts.reshape(136, 128), old_centroids)
    return (centroids, best_cosine)


def solution(mesh):
    fine = Mesh(mesh.devices.reshape(SIZES), NAMES)
    dp, mp = ("zh", "zl", "x"), ("y", "c")
    placed = (
        P(dp + mp, None),
        P(dp + mp),
        P(dp, mp),
        P(dp + mp, None),
        P(dp + mp),
    )
    return jax.shard_map(
        local,
        mesh=fine,
        in_specs=placed,
        out_specs=(P(dp, mp), P(dp + mp, None)),
        check_vma=False,
    )
```

time: 98 us -> 96.6 us (0.986)
  the two profiles are of different devices: /device:TPU:8 before, /device:TPU:2 now
where the time goes in v5:
time: 96.6 us; the launch traced here: 96 us
  starting transfers between devices  55.8 us (58%)
  waiting for transfers between devices  28.8 us (30%)
  Pallas kernels  9.84 us (10%)
    all_to_all x1, starting transfers between devices, local(): parts = lax.all_to_all(parts.reshape(8, 17, 1, 128), 'zh', 0, 0, tiled=True)  19.5 us
    all_to_all x1, starting transfers between devices, local(): lax.all_to_all(messages.reshape(BLOCK, MSG, 128), ('x', 'y', 'c'), 0, 0,...  16.8 us
    all_to_all x1, waiting for transfers between devices, local(): parts = lax.all_to_all(parts.reshape(8, 17, 1, 128), 'zh', 0, 0, tiled=True)  16 us
    all_to_all x1, waiting for transfers between devices, local(): lax.all_to_all(messages.reshape(BLOCK, MSG, 128), ('x', 'y', 'c'), 0, 0,...  10.9 us
    ppermute x3, starting transfers between devices, local(): lax.ppermute(embeddings, 'y', [(i, i ^ d) for i in range(4)])  9.82 us
    all_to_all x1, starting transfers between devices, local(): lax.all_to_all(parts.reshape(16, 33, 1, 128), ('zl', 'x'), 0, 0, tiled=True)  5.34 us
    ppermute x2, starting transfers between devices, local(): others = [lax.ppermute(other, 'c', [(0, 1), (1, 0)]) for other in others]  4.33 us
    pallas_call x1, Pallas kernels, local(): pl.pallas_call(sum_kernel, out_shape=(pltpu.VMEM((528, 128), F32), pltpu....  2.53 us
  transfers between devices with their start and end apart: 8, of which 4 were waited for; matrix products, arithmetic and copies ran while one was open for 0% of the time, Pallas kernels for 4%

profile of v5, /device:TPU:2, one launch (start us, length us, event | category | flops | bytes accessed | tf_op | source)
XLA Modules:
  0.0 96.0 jit_solution(237799720224319851)
XLA Ops:
  0.6 2.3 %pack.1 = bf16[4,8,80,128]{3,2,1,0:T(8,128)(2,1)} custom-call(bf16[256,1024]{1,0:T(8,128)(2,1)} %refs_0_, s32[2,128]{1,0:T(2,128)} %bitcast.13, s32[2,128]{1,0:T(2,128)} %mine_ref.1), custom_call_target="tpu_custom_call" | custom-call | flops 1048576 | bytes 1572864 | tf_op jit(solution)/shard_map/pack/pallas_call | solution.py:168
  3.0 16.8 %all-to-all-start = ((bf16[32,80,128]{2,1,0:T(8,128)(2,1)}), bf16[32,80,128]{2,1,0:T(8,128)(2,1)S(1)}, u32[]{:S(2)}, u32[]{:S(2)}) async-start(bf16[32,80,128]{2,1,0:T(8,128)(2,1)} %bitcast.12), calls=%async_computation | async-start | bytes 1310720 | tf_op jit(solution)/shard_map/all_to_all | solution.py:186
  19.8 10.9 %all-to-all-done.msg_ref = bf16[32,80,128]{2,1,0:T(8,128)(2,1)S(1)} async-done(((bf16[32,80,128]{2,1,0:T(8,128)(2,1)}), bf16[32,80,128]{2,1,0:T(8,128)(2,1)S(1)}, u32[]{:S(2)}, u32[]{:S(2)}) %all-to-all-start) | async-done | bytes 655392 | tf_op jit(solution)/shard_map/all_to_all | solution.py:186
  30.7 2.5 %sums.1 = (f32[528,128]{1,0:T(8,128)}, s32[2,128]{1,0:T(2,128)S(1)}) custom-call(s32[1]{0:T(128)} %bitcast.1.from_ref, bf16[32,80,128]{2,1,0:T(8,128)(2,1)S(1)} %all-to-all-done.msg_ref), custom_call_target="tpu_custom_call" | custom-call | flops 2147483648 | bytes 1048576 | tf_op jit(solution)/shard_map/sums/pallas_call | solution.py:187
  33.2 0.0 copy-start
  33.2 5.3 %all-to-all-start.1 = ((f32[16,33,1,128]{3,2,1,0:T(1,128)}), f32[16,33,1,128]{3,2,1,0:T(1,128)S(1)}, u32[]{:S(2)}, u32[]{:S(2)}) async-start(f32[16,33,1,128]{3,2,1,0:T(1,128)} %bitcast.4), calls=%async_computation.1 | async-start | bytes 540672 | tf_op jit(solution)/shard_map/all_to_all | solution.py:198
  38.5 0.0 copy-done
  38.5 2.6 %collective-permute-start = (bf16[256,1024]{1,0:T(8,128)(2,1)S(1)}, bf16[256,1024]{1,0:T(8,128)(2,1)S(1)}, u32[]{:S(2)}, u32[]{:S(2)}) collective-permute-start(bf16[256,1024]{1,0:T(8,128)(2,1)S(1)} %copy-done), channel_id=1, source_target_pairs={{0,2},{2,0},{4,6},{6,4},{1,3},{3,1},{5,7},{7,5},{8,10},{10,8},{12,... | collective-permute-start | bytes 1572872 | tf_op jit(solution)/shard_map/ppermute | solution.py:197
  41.2 3.7 %collective-permute-start.1 = (bf16[256,1024]{1,0:T(8,128)(2,1)S(1)}, bf16[256,1024]{1,0:T(8,128)(2,1)S(1)}, u32[]{:S(2)}, u32[]{:S(2)}) collective-permute-start(bf16[256,1024]{1,0:T(8,128)(2,1)S(1)} %copy-done), channel_id=1, source_target_pairs={{0,6},{2,4},{4,2},{6,0},{1,7},{3,5},{5,3},{7,1},{8,14},{10,12},{12... | collective-permute-start | bytes 1572872 | tf_op jit(solution)/shard_map/ppermute | solution.py:197
  44.8 3.5 %collective-permute-start.2 = (bf16[256,1024]{1,0:T(8,128)(2,1)S(1)}, bf16[256,1024]{1,0:T(8,128)(2,1)S(1)}, u32[]{:S(2)}, u32[]{:S(2)}) collective-permute-start(bf16[256,1024]{1,0:T(8,128)(2,1)S(1)} %copy-done), channel_id=1, source_target_pairs={{0,4},{2,6},{4,0},{6,2},{1,5},{3,7},{5,1},{7,3},{8,12},{10,14},{12... | collective-permute-start | bytes 1572872 | tf_op jit(solution)/shard_map/ppermute | solution.py:197
  48.4 0.8 all-to-all-done.1
  49.2 0.8 regroup.1.after_ref
  50.0 19.5 %all-to-all-start.2 = ((f32[8,17,1,128]{3,2,1,0:T(1,128)}), f32[8,17,1,128]{3,2,1,0:T(1,128)S(1)}, u32[]{:S(2)}, u32[]{:S(2)}) async-start(f32[8,17,1,128]{3,2,1,0:T(1,128)} %bitcast.6), calls=%async_computation.2 | async-start | bytes 139264 | tf_op jit(solution)/shard_map/all_to_all | solution.py:210
  69.5 0.1 pad_add_fusion.place_ref
  69.6 0.0 copy-start.2
  69.6 0.0 collective-permute-done.refs_1_
  69.6 0.0 collective-permute-done.1.refs_2_
  69.6 0.0 collective-permute-done.2.refs_3_
  69.6 0.7 copy-done.2
  70.3 2.0 %members.1 = (bf16[256,1024]{1,0:T(8,128)(2,1)S(1)}, bf16[128,1024]{1,0:T(8,128)(2,1)S(1)}, bf16[128,1024]{1,0:T(8,128)(2,1)S(1)}) custom-call(f32[136,128]{1,0:T(8,128)} %regroup.1.after_ref, s32[2]{0:T(128)S(1)} %pad_add_fusion.place_ref, s32[2,128]{1,0:T(2,128)S(1)} %copy-done.2, s32[2,128]{1,0:T(2,128)S(1)} %get-tuple-element.13.theirs_ref, ...), custom_call_target="tpu_custom_call" | custom-call | tf_op jit(solution)/shard_map/members/pallas_call | solution.py:212
  72.3 1.9 %collective-permute-start.3 = (bf16[128,1024]{1,0:T(8,128)(2,1)S(1)}, bf16[128,1024]{1,0:T(8,128)(2,1)S(1)}, u32[]{:S(2)}, u32[]{:S(2)}) collective-permute-start(bf16[128,1024]{1,0:T(8,128)(2,1)S(1)} %get-tuple-element.16), channel_id=1, source_target_pairs={{0,1},{1,0},{2,3},{3,2},{4,5},{5,4},{6,7},{7,6},{8,9},{9,8},{10,11... | collective-permute-start | bytes 786440 | tf_op jit(solution)/shard_map/ppermute | solution.py:221
  74.2 2.4 %collective-permute-start.4 = (bf16[128,1024]{1,0:T(8,128)(2,1)S(1)}, bf16[128,1024]{1,0:T(8,128)(2,1)S(1)}, u32[]{:S(2)}, u32[]{:S(2)}) collective-permute-start(bf16[128,1024]{1,0:T(8,128)(2,1)S(1)} %get-tuple-element.17), channel_id=1, source_target_pairs={{0,1},{1,0},{2,3},{3,2},{4,5},{5,4},{6,7},{7,6},{8,9},{9,8},{10,11... | collective-permute-start | bytes 786440 | tf_op jit(solution)/shard_map/ppermute | solution.py:221
  76.6 0.0 copy-start.3
  76.7 0.0 collective-permute-done.3.first_ref
  76.7 1.1 %collective-permute-done.4.second_ref = bf16[128,1024]{1,0:T(8,128)(2,1)S(1)} collective-permute-done((bf16[128,1024]{1,0:T(8,128)(2,1)S(1)}, bf16[128,1024]{1,0:T(8,128)(2,1)S(1)}, u32[]{:S(2)}, u32[]{:S(2)}) %collective-permute-start.4) | collective-permute-done | bytes 262176 | tf_op jit(solution)/shard_map/ppermute | solution.py:221
  77.8 0.0 copy-done.3
  77.8 0.0 copy-start.1
  77.8 1.5 %match.1 = f32[2,128]{1,0:T(2,128)} custom-call(s32[2]{0:T(128)S(1)} %copy-done.3, bf16[256,1024]{1,0:T(8,128)(2,1)S(1)} %get-tuple-element.15.own_ref, bf16[128,1024]{1,0:T(8,128)(2,1)S(1)} %collective-permute-done.3.first_ref, bf16[128,1024]{1,0:T(8,128)(2,1)S(1)} %collective-permute-done.4.second_ref), custom_call_target="tpu_custom_call" | custom-call | tf_op jit(solution)/shard_map/match/pallas_call | solution.py:222
  79.3 16.0 %all-to-all-done.2 = f32[8,17,1,128]{3,2,1,0:T(1,128)S(1)} async-done(((f32[8,17,1,128]{3,2,1,0:T(1,128)}), f32[8,17,1,128]{3,2,1,0:T(1,128)S(1)}, u32[]{:S(2)}, u32[]{:S(2)}) %all-to-all-start.2) | async-done | bytes 69664 | tf_op jit(solution)/shard_map/all_to_all | solution.py:210
  95.3 0.0 copy-done.1
  95.3 0.7 finish.1
Async XLA Ops:
  3.0 27.7 %all-to-all-start = ((bf16[32,80,128]{2,1,0:T(8,128)(2,1)}), bf16[32,80,128]{2,1,0:T(8,128)(2,1)S(1)}, u32[]{:S(2)}, u32[]{:S(2)}) async-start(bf16[32,80,128]{2,1,0:T(8,128)(2,1)} %bitcast.12), calls=%async_computation | async-start | bytes 1310720 | tf_op jit(solution)/shard_map/all_to_all | solution.py:186
  33.2 5.3 %copy-start = (bf16[256,1024]{1,0:T(8,128)(2,1)S(1)}, bf16[256,1024]{1,0:T(8,128)(2,1)}, u32[]{:S(2)}) copy-start(bf16[256,1024]{1,0:T(8,128)(2,1)} %refs_0_) | copy-start | bytes 1572868
  33.2 16.0 %all-to-all-start.1 = ((f32[16,33,1,128]{3,2,1,0:T(1,128)}), f32[16,33,1,128]{3,2,1,0:T(1,128)S(1)}, u32[]{:S(2)}, u32[]{:S(2)}) async-start(f32[16,33,1,128]{3,2,1,0:T(1,128)} %bitcast.4), calls=%async_computation.1 | async-start | bytes 540672 | tf_op jit(solution)/shard_map/all_to_all | solution.py:198
  38.5 31.1 %collective-permute-start = (bf16[256,1024]{1,0:T(8,128)(2,1)S(1)}, bf16[256,1024]{1,0:T(8,128)(2,1)S(1)}, u32[]{:S(2)}, u32[]{:S(2)}) collective-permute-start(bf16[256,1024]{1,0:T(8,128)(2,1)S(1)} %copy-done), channel_id=1, source_target_pairs={{0,2},{2,0},{4,6},{6,4},{1,3},{3,1},{5,7},{7,5},{8,10},{10,8},{12,... | collective-permute-start | bytes 1572872 | tf_op jit(solution)/shard_map/ppermute | solution.py:197
  41.2 28.4 %collective-permute-start.1 = (bf16[256,1024]{1,0:T(8,128)(2,1)S(1)}, bf16[256,1024]{1,0:T(8,128)(2,1)S(1)}, u32[]{:S(2)}, u32[]{:S(2)}) collective-permute-start(bf16[256,1024]{1,0:T(8,128)(2,1)S(1)} %copy-done), channel_id=1, source_target_pairs={{0,6},{2,4},{4,2},{6,0},{1,7},{3,5},{5,3},{7,1},{8,14},{10,12},{12... | collective-permute-start | bytes 1572872 | tf_op jit(solution)/shard_map/ppermute | solution.py:197
  44.8 24.8 %collective-permute-start.2 = (bf16[256,1024]{1,0:T(8,128)(2,1)S(1)}, bf16[256,1024]{1,0:T(8,128)(2,1)S(1)}, u32[]{:S(2)}, u32[]{:S(2)}) collective-permute-start(bf16[256,1024]{1,0:T(8,128)(2,1)S(1)} %copy-done), channel_id=1, source_target_pairs={{0,4},{2,6},{4,0},{6,2},{1,5},{3,7},{5,1},{7,3},{8,12},{10,14},{12... | collective-permute-start | bytes 1572872 | tf_op jit(solution)/shard_map/ppermute | solution.py:197
  50.0 45.3 %all-to-all-start.2 = ((f32[8,17,1,128]{3,2,1,0:T(1,128)}), f32[8,17,1,128]{3,2,1,0:T(1,128)S(1)}, u32[]{:S(2)}, u32[]{:S(2)}) async-start(f32[8,17,1,128]{3,2,1,0:T(1,128)} %bitcast.6), calls=%async_computation.2 | async-start | bytes 139264 | tf_op jit(solution)/shard_map/all_to_all | solution.py:210
  69.6 0.7 copy-start.2
  72.3 4.4 %collective-permute-start.3 = (bf16[128,1024]{1,0:T(8,128)(2,1)S(1)}, bf16[128,1024]{1,0:T(8,128)(2,1)S(1)}, u32[]{:S(2)}, u32[]{:S(2)}) collective-permute-start(bf16[128,1024]{1,0:T(8,128)(2,1)S(1)} %get-tuple-element.16), channel_id=1, source_target_pairs={{0,1},{1,0},{2,3},{3,2},{4,5},{5,4},{6,7},{7,6},{8,9},{9,8},{10,11... | collective-permute-start | bytes 786440 | tf_op jit(solution)/shard_map/ppermute | solution.py:221
  74.2 3.6 %collective-permute-start.4 = (bf16[128,1024]{1,0:T(8,128)(2,1)S(1)}, bf16[128,1024]{1,0:T(8,128)(2,1)S(1)}, u32[]{:S(2)}, u32[]{:S(2)}) collective-permute-start(bf16[128,1024]{1,0:T(8,128)(2,1)S(1)} %get-tuple-element.17), channel_id=1, source_target_pairs={{0,1},{1,0},{2,3},{3,2},{4,5},{5,4},{6,7},{7,6},{8,9},{9,8},{10,11... | collective-permute-start | bytes 786440 | tf_op jit(solution)/shard_map/ppermute | solution.py:221
  76.6 1.1 %copy-start.3 = (s32[2]{0:T(128)S(1)}, s32[2]{0:T(128)}, u32[]{:S(2)}) copy-start(s32[2]{0:T(128)} %len_ref.1) | copy-start | bytes 28
  77.8 17.5 %copy-start.1 = (f32[16,128]{1,0:T(8,128)S(1)}, f32[16,128]{1,0:T(8,128)}, u32[]{:S(2)}) copy-start(f32[16,128]{1,0:T(8,128)} %old_ref.1) | copy-start | bytes 24580

commit v6 on v5

--- a/solution.py
+++ b/solution.py
@@ -13,6 +13,7 @@
 FEATS = 32
 MSG = 80
 MIB = 1 << 20
+RING = [4, 5, 6, 7, 0, 1, 2, 3]
 
 
 def params(mib):
@@ -110,10 +111,11 @@
         s_ref[...] = rows
         for zh in range(8):
             for r1 in range(2):
-                at = 17 * zh + 4 * low + 2 * r1
+                at = 17 * RING.index(zh) + 4 * low + 2 * r1
                 out_ref[at : at + 2, :] = s_ref[16 * r1 + 2 * zh : 16 * r1 + 2 * zh + 2, :]
     for zh in range(8):
-        out_ref[17 * zh + 16 : 17 * zh + 17, :] = counts
+        at = 17 * zh + 16
+        out_ref[at : at + 1, :] = counts
 
 
 def finish_kernel(at_ref, in_ref, old_ref, out_ref):
@@ -207,7 +209,7 @@
         name="regroup",
     )(parts.reshape(528, 128))
     after = parts
-    parts = lax.all_to_all(parts.reshape(8, 17, 1, 128), "zh", 0, 0, tiled=True)
+    parts = lax.all_to_all(parts.reshape(8, 17, 1, 128), "zh", 0, 0, axis_index_groups=[RING], tiled=True)
     members = [jax.ShapeDtypeStruct((n, 1024), BF16) for n in (256, 128, 128)]
     own, *others = pl.pallas_call(
         member_kernel,

time: 96.6 us -> 88.9 us (0.920)
  the two profiles are of different devices: /device:TPU:2 before, /device:TPU:1 now
where the time goes in v6:
time: 88.9 us; the launch traced here: 88.3 us
  starting transfers between devices  60.7 us (68%)
  waiting for transfers between devices  16.3 us (18%)
  Pallas kernels  9.82 us (11%)
    all_to_all x1, starting transfers between devices, local(): lax.all_to_all(parts.reshape(8, 17, 1, 128), 'zh', 0, 0, axis_index_group...  24.5 us
    all_to_all x1, starting transfers between devices, local(): lax.all_to_all(messages.reshape(BLOCK, MSG, 128), ('x', 'y', 'c'), 0, 0,...  17.7 us
    all_to_all x1, waiting for transfers between devices, local(): lax.all_to_all(messages.reshape(BLOCK, MSG, 128), ('x', 'y', 'c'), 0, 0,...  13 us
    ppermute x3, starting transfers between devices, local(): lax.ppermute(embeddings, 'y', [(i, i ^ d) for i in range(4)])  8.98 us
    ppermute x2, starting transfers between devices, local(): others = [lax.ppermute(other, 'c', [(0, 1), (1, 0)]) for other in others]  5.86 us
    all_to_all x1, starting transfers between devices, local(): lax.all_to_all(parts.reshape(16, 33, 1, 128), ('zl', 'x'), 0, 0, tiled=True)  3.66 us
    pallas_call x1, Pallas kernels, local(): pl.pallas_call(sum_kernel, out_shape=(pltpu.VMEM((528, 128), F32), pltpu....  2.53 us
    pallas_call x1, Pallas kernels, local(): pl.pallas_call(pack_kernel, out_shape=pltpu.HBM((4, 8, MSG, 128), BF16),...  2.32 us
  transfers between devices with their start and end apart: 8, of which 3 were waited for; matrix products, arithmetic and copies ran while one was open for 0% of the time, Pallas kernels for 5%

profile of v6, /device:TPU:1, one launch (start us, length us, event | category | flops | bytes accessed | tf_op | source)
XLA Modules:
  0.0 88.3 jit_solution(9326987198895289001)
XLA Ops:
  0.6 2.3 %pack.1 = bf16[4,8,80,128]{3,2,1,0:T(8,128)(2,1)} custom-call(bf16[256,1024]{1,0:T(8,128)(2,1)} %refs_0_, s32[2,128]{1,0:T(2,128)} %bitcast.13, s32[2,128]{1,0:T(2,128)} %mine_ref.1), custom_call_target="tpu_custom_call" | custom-call | flops 1048576 | bytes 1572864 | tf_op jit(solution)/shard_map/pack/pallas_call | solution.py:170
  3.0 17.7 %all-to-all-start = ((bf16[32,80,128]{2,1,0:T(8,128)(2,1)}), bf16[32,80,128]{2,1,0:T(8,128)(2,1)S(1)}, u32[]{:S(2)}, u32[]{:S(2)}) async-start(bf16[32,80,128]{2,1,0:T(8,128)(2,1)} %bitcast.12), calls=%async_computation | async-start | bytes 1310720 | tf_op jit(solution)/shard_map/all_to_all | solution.py:188
  20.7 13.0 %all-to-all-done.msg_ref = bf16[32,80,128]{2,1,0:T(8,128)(2,1)S(1)} async-done(((bf16[32,80,128]{2,1,0:T(8,128)(2,1)}), bf16[32,80,128]{2,1,0:T(8,128)(2,1)S(1)}, u32[]{:S(2)}, u32[]{:S(2)}) %all-to-all-start) | async-done | bytes 655392 | tf_op jit(solution)/shard_map/all_to_all | solution.py:188
  33.7 2.5 %sums.1 = (f32[528,128]{1,0:T(8,128)}, s32[2,128]{1,0:T(2,128)S(1)}) custom-call(s32[1]{0:T(128)} %bitcast.1.from_ref, bf16[32,80,128]{2,1,0:T(8,128)(2,1)S(1)} %all-to-all-done.msg_ref), custom_call_target="tpu_custom_call" | custom-call | flops 2147483648 | bytes 1048576 | tf_op jit(solution)/shard_map/sums/pallas_call | solution.py:189
  36.3 0.0 copy-start
  36.3 3.7 %all-to-all-start.1 = ((f32[16,33,1,128]{3,2,1,0:T(1,128)}), f32[16,33,1,128]{3,2,1,0:T(1,128)S(1)}, u32[]{:S(2)}, u32[]{:S(2)}) async-start(f32[16,33,1,128]{3,2,1,0:T(1,128)} %bitcast.4), calls=%async_computation.1 | async-start | bytes 540672 | tf_op jit(solution)/shard_map/all_to_all | solution.py:200
  39.9 0.0 copy-done
  39.9 1.9 %collective-permute-start = (bf16[256,1024]{1,0:T(8,128)(2,1)S(1)}, bf16[256,1024]{1,0:T(8,128)(2,1)S(1)}, u32[]{:S(2)}, u32[]{:S(2)}) collective-permute-start(bf16[256,1024]{1,0:T(8,128)(2,1)S(1)} %copy-done), channel_id=1, source_target_pairs={{0,2},{2,0},{4,6},{6,4},{1,3},{3,1},{5,7},{7,5},{8,10},{10,8},{12,... | collective-permute-start | bytes 1572872 | tf_op jit(solution)/shard_map/ppermute | solution.py:199
  41.9 3.0 %collective-permute-start.1 = (bf16[256,1024]{1,0:T(8,128)(2,1)S(1)}, bf16[256,1024]{1,0:T(8,128)(2,1)S(1)}, u32[]{:S(2)}, u32[]{:S(2)}) collective-permute-start(bf16[256,1024]{1,0:T(8,128)(2,1)S(1)} %copy-done), channel_id=1, source_target_pairs={{0,6},{2,4},{4,2},{6,0},{1,7},{3,5},{5,3},{7,1},{8,14},{10,12},{12... | collective-permute-start | bytes 1572872 | tf_op jit(solution)/shard_map/ppermute | solution.py:199
  44.9 4.1 %collective-permute-start.2 = (bf16[256,1024]{1,0:T(8,128)(2,1)S(1)}, bf16[256,1024]{1,0:T(8,128)(2,1)S(1)}, u32[]{:S(2)}, u32[]{:S(2)}) collective-permute-start(bf16[256,1024]{1,0:T(8,128)(2,1)S(1)} %copy-done), channel_id=1, source_target_pairs={{0,4},{2,6},{4,0},{6,2},{1,5},{3,7},{5,1},{7,3},{8,12},{10,14},{12... | collective-permute-start | bytes 1572872 | tf_op jit(solution)/shard_map/ppermute | solution.py:199
  48.9 1.8 %all-to-all-done.1 = f32[16,33,1,128]{3,2,1,0:T(1,128)S(1)} async-done(((f32[16,33,1,128]{3,2,1,0:T(1,128)}), f32[16,33,1,128]{3,2,1,0:T(1,128)S(1)}, u32[]{:S(2)}, u32[]{:S(2)}) %all-to-all-start.1) | async-done | bytes 270368 | tf_op jit(solution)/shard_map/all_to_all | solution.py:200
  50.7 0.8 regroup.1.after_ref
  51.5 24.5 %all-to-all-start.2 = ((f32[8,17,1,128]{3,2,1,0:T(1,128)}), f32[8,17,1,128]{3,2,1,0:T(1,128)S(1)}, u32[]{:S(2)}, u32[]{:S(2)}) async-start(f32[8,17,1,128]{3,2,1,0:T(1,128)} %bitcast.6), calls=%async_computation.2 | async-start | bytes 139264 | tf_op jit(solution)/shard_map/all_to_all | solution.py:212
  76.0 0.1 pad_add_fusion.place_ref
  76.1 0.0 copy-start.2
  76.1 0.0 collective-permute-done.refs_1_
  76.1 0.0 collective-permute-done.1.refs_2_
  76.1 0.0 collective-permute-done.2.refs_3_
  76.1 0.7 copy-done.2
  76.7 2.0 %members.1 = (bf16[256,1024]{1,0:T(8,128)(2,1)S(1)}, bf16[128,1024]{1,0:T(8,128)(2,1)S(1)}, bf16[128,1024]{1,0:T(8,128)(2,1)S(1)}) custom-call(f32[136,128]{1,0:T(8,128)} %regroup.1.after_ref, s32[2]{0:T(128)S(1)} %pad_add_fusion.place_ref, s32[2,128]{1,0:T(2,128)S(1)} %copy-done.2, s32[2,128]{1,0:T(2,128)S(1)} %get-tuple-element.13.theirs_ref, ...), custom_call_target="tpu_custom_call" | custom-call | tf_op jit(solution)/shard_map/members/pallas_call | solution.py:214
  78.7 3.9 %collective-permute-start.3 = (bf16[128,1024]{1,0:T(8,128)(2,1)S(1)}, bf16[128,1024]{1,0:T(8,128)(2,1)S(1)}, u32[]{:S(2)}, u32[]{:S(2)}) collective-permute-start(bf16[128,1024]{1,0:T(8,128)(2,1)S(1)} %get-tuple-element.16), channel_id=1, source_target_pairs={{0,1},{1,0},{2,3},{3,2},{4,5},{5,4},{6,7},{7,6},{8,9},{9,8},{10,11... | collective-permute-start | bytes 786440 | tf_op jit(solution)/shard_map/ppermute | solution.py:223
  82.7 1.9 %collective-permute-start.4 = (bf16[128,1024]{1,0:T(8,128)(2,1)S(1)}, bf16[128,1024]{1,0:T(8,128)(2,1)S(1)}, u32[]{:S(2)}, u32[]{:S(2)}) collective-permute-start(bf16[128,1024]{1,0:T(8,128)(2,1)S(1)} %get-tuple-element.17), channel_id=1, source_target_pairs={{0,1},{1,0},{2,3},{3,2},{4,5},{5,4},{6,7},{7,6},{8,9},{9,8},{10,11... | collective-permute-start | bytes 786440 | tf_op jit(solution)/shard_map/ppermute | solution.py:223
  84.6 0.0 copy-start.3
  84.6 0.0 collective-permute-done.3.first_ref
  84.6 1.5 %collective-permute-done.4.second_ref = bf16[128,1024]{1,0:T(8,128)(2,1)S(1)} collective-permute-done((bf16[128,1024]{1,0:T(8,128)(2,1)S(1)}, bf16[128,1024]{1,0:T(8,128)(2,1)S(1)}, u32[]{:S(2)}, u32[]{:S(2)}) %collective-permute-start.4) | collective-permute-done | bytes 262176 | tf_op jit(solution)/shard_map/ppermute | solution.py:223
  86.1 0.0 copy-done.3
  86.1 0.0 copy-start.1
  86.1 1.5 %match.1 = f32[2,128]{1,0:T(2,128)} custom-call(s32[2]{0:T(128)S(1)} %copy-done.3, bf16[256,1024]{1,0:T(8,128)(2,1)S(1)} %get-tuple-element.15.own_ref, bf16[128,1024]{1,0:T(8,128)(2,1)S(1)} %collective-permute-done.3.first_ref, bf16[128,1024]{1,0:T(8,128)(2,1)S(1)} %collective-permute-done.4.second_ref), custom_call_target="tpu_custom_call" | custom-call | tf_op jit(solution)/shard_map/match/pallas_call | solution.py:224
  87.6 0.0 all-to-all-done.2
  87.6 0.0 copy-done.1
  87.6 0.7 finish.1
Async XLA Ops:
  3.0 30.8 %all-to-all-start = ((bf16[32,80,128]{2,1,0:T(8,128)(2,1)}), bf16[32,80,128]{2,1,0:T(8,128)(2,1)S(1)}, u32[]{:S(2)}, u32[]{:S(2)}) async-start(bf16[32,80,128]{2,1,0:T(8,128)(2,1)} %bitcast.12), calls=%async_computation | async-start | bytes 1310720 | tf_op jit(solution)/shard_map/all_to_all | solution.py:188
  36.3 3.7 %copy-start = (bf16[256,1024]{1,0:T(8,128)(2,1)S(1)}, bf16[256,1024]{1,0:T(8,128)(2,1)}, u32[]{:S(2)}) copy-start(bf16[256,1024]{1,0:T(8,128)(2,1)} %refs_0_) | copy-start | bytes 1572868
  36.3 14.5 %all-to-all-start.1 = ((f32[16,33,1,128]{3,2,1,0:T(1,128)}), f32[16,33,1,128]{3,2,1,0:T(1,128)S(1)}, u32[]{:S(2)}, u32[]{:S(2)}) async-start(f32[16,33,1,128]{3,2,1,0:T(1,128)} %bitcast.4), calls=%async_computation.1 | async-start | bytes 540672 | tf_op jit(solution)/shard_map/all_to_all | solution.py:200
  39.9 36.1 %collective-permute-start = (bf16[256,1024]{1,0:T(8,128)(2,1)S(1)}, bf16[256,1024]{1,0:T(8,128)(2,1)S(1)}, u32[]{:S(2)}, u32[]{:S(2)}) collective-permute-start(bf16[256,1024]{1,0:T(8,128)(2,1)S(1)} %copy-done), channel_id=1, source_target_pairs={{0,2},{2,0},{4,6},{6,4},{1,3},{3,1},{5,7},{7,5},{8,10},{10,8},{12,... | collective-permute-start | bytes 1572872 | tf_op jit(solution)/shard_map/ppermute | solution.py:199
  41.9 34.2 %collective-permute-start.1 = (bf16[256,1024]{1,0:T(8,128)(2,1)S(1)}, bf16[256,1024]{1,0:T(8,128)(2,1)S(1)}, u32[]{:S(2)}, u32[]{:S(2)}) collective-permute-start(bf16[256,1024]{1,0:T(8,128)(2,1)S(1)} %copy-done), channel_id=1, source_target_pairs={{0,6},{2,4},{4,2},{6,0},{1,7},{3,5},{5,3},{7,1},{8,14},{10,12},{12... | collective-permute-start | bytes 1572872 | tf_op jit(solution)/shard_map/ppermute | solution.py:199
  44.9 31.2 %collective-permute-start.2 = (bf16[256,1024]{1,0:T(8,128)(2,1)S(1)}, bf16[256,1024]{1,0:T(8,128)(2,1)S(1)}, u32[]{:S(2)}, u32[]{:S(2)}) collective-permute-start(bf16[256,1024]{1,0:T(8,128)(2,1)S(1)} %copy-done), channel_id=1, source_target_pairs={{0,4},{2,6},{4,0},{6,2},{1,5},{3,7},{5,1},{7,3},{8,12},{10,14},{12... | collective-permute-start | bytes 1572872 | tf_op jit(solution)/shard_map/ppermute | solution.py:199
  51.5 36.1 %all-to-all-start.2 = ((f32[8,17,1,128]{3,2,1,0:T(1,128)}), f32[8,17,1,128]{3,2,1,0:T(1,128)S(1)}, u32[]{:S(2)}, u32[]{:S(2)}) async-start(f32[8,17,1,128]{3,2,1,0:T(1,128)} %bitcast.6), calls=%async_computation.2 | async-start | bytes 139264 | tf_op jit(solution)/shard_map/all_to_all | solution.py:212
  76.1 0.7 copy-start.2
  78.7 5.9 %collective-permute-start.3 = (bf16[128,1024]{1,0:T(8,128)(2,1)S(1)}, bf16[128,1024]{1,0:T(8,128)(2,1)S(1)}, u32[]{:S(2)}, u32[]{:S(2)}) collective-permute-start(bf16[128,1024]{1,0:T(8,128)(2,1)S(1)} %get-tuple-element.16), channel_id=1, source_target_pairs={{0,1},{1,0},{2,3},{3,2},{4,5},{5,4},{6,7},{7,6},{8,9},{9,8},{10,11... | collective-permute-start | bytes 786440 | tf_op jit(solution)/shard_map/ppermute | solution.py:223
  82.7 3.4 %collective-permute-start.4 = (bf16[128,1024]{1,0:T(8,128)(2,1)S(1)}, bf16[128,1024]{1,0:T(8,128)(2,1)S(1)}, u32[]{:S(2)}, u32[]{:S(2)}) collective-permute-start(bf16[128,1024]{1,0:T(8,128)(2,1)S(1)} %get-tuple-element.17), channel_id=1, source_target_pairs={{0,1},{1,0},{2,3},{3,2},{4,5},{5,4},{6,7},{7,6},{8,9},{9,8},{10,11... | collective-permute-start | bytes 786440 | tf_op jit(solution)/shard_map/ppermute | solution.py:223
  84.6 1.5 %copy-start.3 = (s32[2]{0:T(128)S(1)}, s32[2]{0:T(128)}, u32[]{:S(2)}) copy-start(s32[2]{0:T(128)} %len_ref.1) | copy-start | bytes 28
  86.1 1.5 %copy-start.1 = (f32[16,128]{1,0:T(8,128)S(1)}, f32[16,128]{1,0:T(8,128)}, u32[]{:S(2)}) copy-start(f32[16,128]{1,0:T(8,128)} %old_ref.1) | copy-start | bytes 24580

commit v7 on v6

--- a/solution.py
+++ b/solution.py
@@ -1,3 +1,5 @@
+import functools
+
 import jax
 import jax.numpy as jnp
 from jax import lax
@@ -13,7 +15,12 @@
 FEATS = 32
 MSG = 80
 MIB = 1 << 20
-RING = [4, 5, 6, 7, 0, 1, 2, 3]
+FIRST = (2, 4)
+BLOCK_ORDER = [k ^ 20 for k in range(BLOCK)]
+FIRST_ZL = 1
+PLANE_ORDER = [k ^ (4 * FIRST_ZL) for k in range(16)]
+FIRST_ZH = 4
+RING_ORDER = [k ^ FIRST_ZH for k in range(8)]
 
 
 def params(mib):
@@ -29,10 +36,9 @@
         pltpu.make_async_copy(label_hbm, label_ref, sems.at[0]),
         pltpu.make_async_copy(rows_hbm, rows_ref, sems.at[1]),
     ]
-    blocks = [
-        pltpu.make_async_copy(emb_hbm.at[:, pl.ds(128 * mp, 128)], emb_ref.at[mp], in_sems.at[mp]) for mp in range(8)
-    ]
-    for copy in small + blocks:
+    halves = [pl.ds(0, 512), pl.ds(512, 512)]
+    blocks = [pltpu.make_async_copy(emb_hbm.at[:, at], emb_ref.at[:, at], in_sems.at[k]) for k, at in enumerate(halves)]
+    for copy in blocks + small:
         copy.start()
     for copy in small:
         copy.wait()
@@ -46,16 +52,18 @@
         codes = jnp.where(row == 2 * k + 1, pair[1:2], codes)
     codes = codes.astype(F32).astype(BF16)
     sent = []
-    for mp in range(8):
-        blocks[mp].wait()
-        turned = emb_ref[mp].T
-        for x in range(4):
-            part = turned[x * FEATS : x * FEATS + FEATS]
-            msg_ref[mp, x, 0:32, :] = part[:, 0:128]
-            msg_ref[mp, x, 32:64, :] = part[:, 128:256]
-            msg_ref[mp, x, 64:80, :] = codes
-        sent.append(pltpu.make_async_copy(msg_ref.at[mp], out_hbm.at[:, mp], out_sems.at[mp]))
-        sent[mp].start()
+    for k in range(2):
+        blocks[k].wait()
+        for mp in range(4 * k, 4 * k + 4):
+            turned = emb_ref[:, 128 * mp : 128 * mp + 128].T
+            for x in range(4):
+                part, at = turned[x * FEATS : x * FEATS + FEATS], (x ^ FIRST[0], mp ^ FIRST[1])
+                msg_ref[*at, 0:32, :] = part[:, 0:128]
+                msg_ref[*at, 32:64, :] = part[:, 128:256]
+                msg_ref[*at, 64:80, :] = codes
+        at = pl.ds((4 * k) ^ FIRST[1], 4)
+        sent.append(pltpu.make_async_copy(msg_ref.at[:, at], out_hbm.at[:, at], out_sems.at[k]))
+        sent[k].start()
     for copy in sent:
         copy.wait()
 
@@ -87,11 +95,13 @@
         sums = sums + lax.dot_general(a, b, contract, preferred_element_type=F32)
         counts = counts + lax.dot_general(p, q, contract, preferred_element_type=F32)
     for m in range(16):
-        out_ref[33 * m : 33 * m + 16, :] = sums[16 * m : 16 * m + 16, 0:128]
-        out_ref[33 * m + 16 : 33 * m + 32, :] = sums[16 * m : 16 * m + 16, 128:256]
-        out_ref[33 * m + 32 : 33 * m + 33, :] = counts[m : m + 1, :]
-    codes = msg_ref[from_ref[0], 64:80, :].astype(F32).astype(I32)
-    rows_ref[...] = codes[4:6] * 8 + codes[6:8]
+        at = 33 * PLANE_ORDER[m]
+        out_ref[at : at + 16, :] = sums[16 * m : 16 * m + 16, 0:128]
+        out_ref[at + 16 : at + 32, :] = sums[16 * m : 16 * m + 16, 128:256]
+        out_ref[at + 32 : at + 33, :] = counts[m : m + 1, :]
+    for k in range(2):
+        codes = msg_ref[from_ref[0] ^ k, 64:80, :].astype(F32).astype(I32)
+        rows_ref[2 * k : 2 * k + 2, :] = codes[4:6] * 8 + codes[6:8]
 
 
 def regroup_kernel(in_ref, out_ref, s_ref):
@@ -111,7 +121,7 @@
         s_ref[...] = rows
         for zh in range(8):
             for r1 in range(2):
-                at = 17 * RING.index(zh) + 4 * low + 2 * r1
+                at = 17 * (zh ^ FIRST_ZH) + 4 * low + 2 * r1
                 out_ref[at : at + 2, :] = s_ref[16 * r1 + 2 * zh : 16 * r1 + 2 * zh + 2, :]
     for zh in range(8):
         at = 17 * zh + 16
@@ -129,27 +139,27 @@
     out_ref[...] = (sums + old_ref[...]) / (counts + 1.0)
 
 
-def member_kernel(after_ref, place_ref, mine_ref, theirs_ref, *refs):
-    *line_refs, own_ref, first_ref, second_ref = refs
+def member_kernel(of, after_ref, place_ref, rows_ref, *refs):
+    line_refs, out_refs = refs[:4], refs[4:]
     core, y = place_ref[0], place_ref[1]
     lane = lax.broadcasted_iota(I32, (128, ROWS), 1)
-    outs = (own_ref.at[0:128], own_ref.at[128:256], first_ref, second_ref)
-    for k, r in enumerate((mine_ref[...], theirs_ref[...])):
-        at = jnp.where(((r >> 8) & 1) == core, (((r >> 9) ^ y) << 8) + (r & 255), -1)
-        at = jnp.concatenate([at, jnp.zeros((6, 128), I32)], 0).astype(F32).T.astype(I32)
-        for s in range(2):
-            total = jnp.zeros((128, 1024), F32)
-            for away, line_ref in zip((0, 1, 3, 2), line_refs):
-                pick = jnp.where(lane + 256 * away == at[:, s : s + 1], 1.0, 0.0).astype(BF16)
-                total = total + jnp.dot(pick, line_ref[...], preferred_element_type=F32)
-            outs[2 * k + s][...] = total.astype(BF16)
-
-
-def match_kernel(len_ref, own_ref, first_ref, second_ref, out_ref):
+    r = rows_ref[2 * of : 2 * of + 2, :]
+    at = jnp.where(((r >> 8) & 1) == core, (((r >> 9) ^ y) << 8) + (r & 255), -1)
+    at = jnp.concatenate([at, jnp.zeros((6, 128), I32)], 0).astype(F32).T.astype(I32)
+    for s, out_ref in enumerate(out_refs):
+        total = jnp.zeros((128, 1024), F32)
+        for away, line_ref in zip((0, 1, 3, 2), line_refs):
+            pick = jnp.where(lane + 256 * away == at[:, s : s + 1], 1.0, 0.0).astype(BF16)
+            total = total + jnp.dot(pick, line_ref[...], preferred_element_type=F32)
+        out_ref[...] = total.astype(BF16)
+
+
+def match_kernel(len_ref, *refs):
     i = lax.broadcasted_iota(I32, (128, 128), 0)
     j = lax.broadcasted_iota(I32, (128, 128), 1)
-    for s, other_ref in enumerate((first_ref, second_ref)):
-        one = own_ref[128 * s : 128 * s + 128, :] + other_ref[...]
+    own_refs, other_refs, out_ref = refs[0:2], refs[2:4], refs[4]
+    for s in range(2):
+        one = own_refs[s][...] + other_refs[s][...]
         gram = lax.dot_general(one, one, (((1,), (1,)), ((), ())), preferred_element_type=F32)
         diagonal = jnp.where(i == j, gram, 0.0)
         down = lax.rsqrt(jnp.sum(diagonal, axis=1, keepdims=True) + 1e-06)
@@ -173,31 +183,31 @@
         in_specs=[HBM] * 3,
         out_specs=HBM,
         scratch_shapes=[
-            pltpu.VMEM((8, ROWS, 128), BF16),
+            pltpu.VMEM((ROWS, 1024), BF16),
             pltpu.VMEM((2, 128), I32),
             pltpu.VMEM((2, 128), I32),
-            pltpu.VMEM((8, 4, MSG, 128), BF16),
-            pltpu.SemaphoreType.DMA((8,)),
-            pltpu.SemaphoreType.DMA((8,)),
+            pltpu.VMEM((4, 8, MSG, 128), BF16),
+            pltpu.SemaphoreType.DMA((2,)),
+            pltpu.SemaphoreType.DMA((2,)),
             pltpu.SemaphoreType.DMA((2,)),
         ],
         compiler_params=params(8),
         cost_estimate=cost(1 << 20, 3 << 19),
         name="pack",
     )(*(pltpu.with_memory_space_constraint(a, pltpu.HBM) for a in (embeddings, assignments.reshape(2, 128), slab_rows)))
-    messages = lax.all_to_all(messages.reshape(BLOCK, MSG, 128), ("x", "y", "c"), 0, 0, tiled=True)
-    parts, other_rows = pl.pallas_call(
+    messages = lax.all_to_all(messages.reshape(BLOCK, MSG, 128), ("x", "y", "c"), 0, 0, axis_index_groups=[BLOCK_ORDER], tiled=True)
+    parts, rows = pl.pallas_call(
         sum_kernel,
-        out_shape=(pltpu.VMEM((528, 128), F32), pltpu.VMEM((2, 128), I32)),
+        out_shape=(pltpu.VMEM((528, 128), F32), pltpu.VMEM((4, 128), I32)),
         in_specs=[SMEM, VMEM],
         out_specs=(VMEM, VMEM),
         compiler_params=params(20),
         cost_estimate=cost(1 << 31, 1 << 20),
         name="sums",
-    )((x * 8 + y * 2 + 1 - core).reshape(1), messages)
+    )(((x * 8 + y * 2 + core) ^ BLOCK_ORDER[0]).reshape(1), messages)
     embeddings, parts = lax.optimization_barrier((embeddings, parts))
     line = [embeddings] + [lax.ppermute(embeddings, "y", [(i, i ^ d) for i in range(4)]) for d in (1, 3, 2)]
-    parts = lax.all_to_all(parts.reshape(16, 33, 1, 128), ("zl", "x"), 0, 0, tiled=True)
+    parts = lax.all_to_all(parts.reshape(16, 33, 1, 128), ("zl", "x"), 0, 0, axis_index_groups=[PLANE_ORDER], tiled=True)
     parts = pl.pallas_call(
         regroup_kernel,
         out_shape=pltpu.VMEM((136, 128), F32),
@@ -209,27 +219,30 @@
         name="regroup",
     )(parts.reshape(528, 128))
     after = parts
-    parts = lax.all_to_all(parts.reshape(8, 17, 1, 128), "zh", 0, 0, axis_index_groups=[RING], tiled=True)
-    members = [jax.ShapeDtypeStruct((n, 1024), BF16) for n in (256, 128, 128)]
-    own, *others = pl.pallas_call(
-        member_kernel,
-        out_shape=members,
-        in_specs=[pl.BlockSpec(memory_space=pl.ANY), SMEM] + [VMEM] * 6,
-        out_specs=[VMEM] * 3,
-        compiler_params=params(16),
-        cost_estimate=cost(0, 0),
-        name="members",
-    )(after, jnp.stack([core, y]), slab_rows, other_rows, *line)
+    parts = lax.all_to_all(parts.reshape(8, 17, 1, 128), "zh", 0, 0, axis_index_groups=[RING_ORDER], tiled=True)
+    place = jnp.stack([core, y])
+    own, others = (
+        pl.pallas_call(
+            functools.partial(member_kernel, of),
+            out_shape=[jax.ShapeDtypeStruct((128, 1024), BF16)] * 2,
+            in_specs=[pl.BlockSpec(memory_space=pl.ANY), SMEM] + [VMEM] * 5,
+            out_specs=[VMEM] * 2,
+            compiler_params=params(16),
+            cost_estimate=cost(0, 0),
+            name="members",
+        )(after, place, rows, *line)
+        for of in range(2)
+    )
     others = [lax.ppermute(other, "c", [(0, 1), (1, 0)]) for other in others]
     best_cosine = pl.pallas_call(
         match_kernel,
         out_shape=jax.ShapeDtypeStruct((2, 128), F32),
-        in_specs=[SMEM] + [VMEM] * 3,
+        in_specs=[SMEM] + [VMEM] * 4,
         out_specs=VMEM,
         compiler_params=params(8),
         cost_estimate=cost(0, 0),
         name="match",
-    )(slab_len, own, *others)
+    )(slab_len, *own, *others)
     parts, best_cosine = lax.optimization_barrier((parts, best_cosine))
     centroids = pl.pallas_call(
         finish_kernel,

time: 88.9 us -> 86.3 us (0.971)
  waiting for transfers between devices: 16.3 us -> 8.68 us
  starting transfers between devices: 60.7 us -> 65.2 us
    all_to_all x1, waiting for transfers between devices: 13 us -> 8.6 us  [local(): lax.all_to_all(messages.reshape(BLOCK, MSG, 128), ('x', 'y', 'c'), 0, 0,...]
    all_to_all x1, starting transfers between devices: 17.7 us -> 21.2 us  [local(): lax.all_to_all(messages.reshape(BLOCK, MSG, 128), ('x', 'y', 'c'), 0, 0,...]
    all_to_all x1, waiting for transfers between devices: 1.77 us -> 0.01 us  [local(): lax.all_to_all(parts.reshape(16, 33, 1, 128), ('zl', 'x'), 0, 0, axis_ind...]
    ppermute x2, waiting for transfers between devices: 1.48 us -> 0.07 us  [local(): others = [lax.ppermute(other, 'c', [(0, 1), (1, 0)]) for other in others]]
    all_to_all x1, starting transfers between devices: 3.66 us -> 4.8 us  [local(): lax.all_to_all(parts.reshape(16, 33, 1, 128), ('zl', 'x'), 0, 0, axis_ind...]
    all_to_all x1, starting transfers between devices: 24.5 us -> 23.6 us  [local(): lax.all_to_all(parts.reshape(8, 17, 1, 128), 'zh', 0, 0, axis_index_group...]
    pallas_call x1 -> x2, Pallas kernels: 1.98 us -> 2.82 us  [local(): pl.pallas_call(functools.partial(member_kernel, of), out_shape=[jax.Shape...]
  transfers between devices with their start and end apart: 8 -> 8, of which waited for: 3 -> 2; matrix products, arithmetic and copies ran while one was open for 0% -> 0% of each run, Pallas kernels for 5% -> 6%
where the time goes in v7:
time: 86.3 us; the launch traced here: 85.7 us
  starting transfers between devices  65.2 us (76%)
  Pallas kernels  10.3 us (12%)
  waiting for transfers between devices  8.68 us (10%)
    all_to_all x1, starting transfers between devices, local(): lax.all_to_all(parts.reshape(8, 17, 1, 128), 'zh', 0, 0, axis_index_group...  23.6 us
    all_to_all x1, starting transfers between devices, local(): lax.all_to_all(messages.reshape(BLOCK, MSG, 128), ('x', 'y', 'c'), 0, 0,...  21.2 us
    ppermute x3, starting transfers between devices, local(): lax.ppermute(embeddings, 'y', [(i, i ^ d) for i in range(4)])  8.98 us
    all_to_all x1, waiting for transfers between devices, local(): lax.all_to_all(messages.reshape(BLOCK, MSG, 128), ('x', 'y', 'c'), 0, 0,...  8.6 us
    ppermute x2, starting transfers between devices, local(): others = [lax.ppermute(other, 'c', [(0, 1), (1, 0)]) for other in others]  6.73 us
    all_to_all x1, starting transfers between devices, local(): lax.all_to_all(parts.reshape(16, 33, 1, 128), ('zl', 'x'), 0, 0, axis_ind...  4.8 us
    pallas_call x2, Pallas kernels, local(): pl.pallas_call(functools.partial(member_kernel, of), out_shape=[jax.Shape...  2.82 us
    pallas_call x1, Pallas kernels, local(): pl.pallas_call(sum_kernel, out_shape=(pltpu.VMEM((528, 128), F32), pltpu....  2.53 us
  transfers between devices with their start and end apart: 8, of which 2 were waited for; matrix products, arithmetic and copies ran while one was open for 0% of the time, Pallas kernels for 6%

profile of v7, /device:TPU:1, one launch (start us, length us, event | category | flops | bytes accessed | tf_op | source)
XLA Modules:
  0.0 85.7 jit_solution(1095676178240241000)
XLA Ops:
  0.6 2.0 %pack.1 = bf16[4,8,80,128]{3,2,1,0:T(8,128)(2,1)} custom-call(bf16[256,1024]{1,0:T(8,128)(2,1)} %refs_0_.1, s32[2,128]{1,0:T(2,128)} %bitcast.13, s32[2,128]{1,0:T(2,128)} %rows_hbm.1), custom_call_target="tpu_custom_call" | custom-call | flops 1048576 | bytes 1572864 | tf_op jit(solution)/shard_map/pack/pallas_call | solution.py:180
  2.6 21.2 %all-to-all-start = ((bf16[32,80,128]{2,1,0:T(8,128)(2,1)}), bf16[32,80,128]{2,1,0:T(8,128)(2,1)S(1)}, u32[]{:S(2)}, u32[]{:S(2)}) async-start(bf16[32,80,128]{2,1,0:T(8,128)(2,1)} %bitcast.12), calls=%async_computation | async-start | bytes 1310720 | tf_op jit(solution)/shard_map/all_to_all | solution.py:198
  23.8 8.6 %all-to-all-done.msg_ref = bf16[32,80,128]{2,1,0:T(8,128)(2,1)S(1)} async-done(((bf16[32,80,128]{2,1,0:T(8,128)(2,1)}), bf16[32,80,128]{2,1,0:T(8,128)(2,1)S(1)}, u32[]{:S(2)}, u32[]{:S(2)}) %all-to-all-start) | async-done | bytes 655392 | tf_op jit(solution)/shard_map/all_to_all | solution.py:198
  32.4 2.5 %sums.1 = (f32[528,128]{1,0:T(8,128)}, s32[4,128]{1,0:T(4,128)S(1)}) custom-call(s32[1]{0:T(128)} %bitcast.1.from_ref, bf16[32,80,128]{2,1,0:T(8,128)(2,1)S(1)} %all-to-all-done.msg_ref), custom_call_target="tpu_custom_call" | custom-call | flops 2147483648 | bytes 1048576 | tf_op jit(solution)/shard_map/sums/pallas_call | solution.py:199
  34.9 0.0 copy-start
  35.0 4.8 %all-to-all-start.1 = ((f32[16,33,1,128]{3,2,1,0:T(1,128)}), f32[16,33,1,128]{3,2,1,0:T(1,128)S(1)}, u32[]{:S(2)}, u32[]{:S(2)}) async-start(f32[16,33,1,128]{3,2,1,0:T(1,128)} %bitcast.4), calls=%async_computation.1 | async-start | bytes 540672 | tf_op jit(solution)/shard_map/all_to_all | solution.py:210
  39.8 0.0 copy-done
  39.8 2.5 %collective-permute-start = (bf16[256,1024]{1,0:T(8,128)(2,1)S(1)}, bf16[256,1024]{1,0:T(8,128)(2,1)S(1)}, u32[]{:S(2)}, u32[]{:S(2)}) collective-permute-start(bf16[256,1024]{1,0:T(8,128)(2,1)S(1)} %copy-done), channel_id=1, source_target_pairs={{0,2},{2,0},{4,6},{6,4},{1,3},{3,1},{5,7},{7,5},{8,10},{10,8},{12,... | collective-permute-start | bytes 1572872 | tf_op jit(solution)/shard_map/ppermute | solution.py:209
  42.3 4.1 %collective-permute-start.1 = (bf16[256,1024]{1,0:T(8,128)(2,1)S(1)}, bf16[256,1024]{1,0:T(8,128)(2,1)S(1)}, u32[]{:S(2)}, u32[]{:S(2)}) collective-permute-start(bf16[256,1024]{1,0:T(8,128)(2,1)S(1)} %copy-done), channel_id=1, source_target_pairs={{0,6},{2,4},{4,2},{6,0},{1,7},{3,5},{5,3},{7,1},{8,14},{10,12},{12... | collective-permute-start | bytes 1572872 | tf_op jit(solution)/shard_map/ppermute | solution.py:209
  46.4 2.4 %collective-permute-start.2 = (bf16[256,1024]{1,0:T(8,128)(2,1)S(1)}, bf16[256,1024]{1,0:T(8,128)(2,1)S(1)}, u32[]{:S(2)}, u32[]{:S(2)}) collective-permute-start(bf16[256,1024]{1,0:T(8,128)(2,1)S(1)} %copy-done), channel_id=1, source_target_pairs={{0,4},{2,6},{4,0},{6,2},{1,5},{3,7},{5,1},{7,3},{8,12},{10,14},{12... | collective-permute-start | bytes 1572872 | tf_op jit(solution)/shard_map/ppermute | solution.py:209
  48.8 0.0 all-to-all-done.1
  48.8 0.8 regroup.1.after_ref
  49.5 23.6 %all-to-all-start.2 = ((f32[8,17,1,128]{3,2,1,0:T(1,128)}), f32[8,17,1,128]{3,2,1,0:T(1,128)S(1)}, u32[]{:S(2)}, u32[]{:S(2)}) async-start(f32[8,17,1,128]{3,2,1,0:T(1,128)} %bitcast.6), calls=%async_computation.2 | async-start | bytes 139264 | tf_op jit(solution)/shard_map/all_to_all | solution.py:222
  73.1 0.1 pad_add_fusion.place_ref
  73.2 0.0 collective-permute-done.refs_1_
  73.2 0.0 collective-permute-done.1.refs_2_
  73.2 0.0 collective-permute-done.2.refs_3_
  73.2 1.4 %members.3 = (bf16[128,1024]{1,0:T(8,128)(2,1)S(1)}, bf16[128,1024]{1,0:T(8,128)(2,1)S(1)}) custom-call(f32[136,128]{1,0:T(8,128)} %regroup.1.after_ref, s32[2]{0:T(128)S(1)} %pad_add_fusion.place_ref, s32[4,128]{1,0:T(4,128)S(1)} %get-tuple-element.14.rows_ref, bf16[256,1024]{1,0:T(8,128)(2,1)S(1)} %copy-done, ...), custom_call_target="tpu_custom_call" | custom-call | tf_op jit(solution)/shard_map/members/pallas_call | solution.py:225
  74.6 4.8 %collective-permute-start.3 = (bf16[128,1024]{1,0:T(8,128)(2,1)S(1)}, bf16[128,1024]{1,0:T(8,128)(2,1)S(1)}, u32[]{:S(2)}, u32[]{:S(2)}) collective-permute-start(bf16[128,1024]{1,0:T(8,128)(2,1)S(1)} %get-tuple-element.18), channel_id=1, source_target_pairs={{0,1},{1,0},{2,3},{3,2},{4,5},{5,4},{6,7},{7,6},{8,9},{9,8},{10,11... | collective-permute-start | bytes 786440 | tf_op jit(solution)/shard_map/ppermute | solution.py:236
  79.4 1.9 %collective-permute-start.4 = (bf16[128,1024]{1,0:T(8,128)(2,1)S(1)}, bf16[128,1024]{1,0:T(8,128)(2,1)S(1)}, u32[]{:S(2)}, u32[]{:S(2)}) collective-permute-start(bf16[128,1024]{1,0:T(8,128)(2,1)S(1)} %get-tuple-element.19), channel_id=1, source_target_pairs={{0,1},{1,0},{2,3},{3,2},{4,5},{5,4},{6,7},{7,6},{8,9},{9,8},{10,11... | collective-permute-start | bytes 786440 | tf_op jit(solution)/shard_map/ppermute | solution.py:236
  81.4 1.4 %members.2 = (bf16[128,1024]{1,0:T(8,128)(2,1)S(1)}, bf16[128,1024]{1,0:T(8,128)(2,1)S(1)}) custom-call(f32[136,128]{1,0:T(8,128)} %regroup.1.after_ref, s32[2]{0:T(128)S(1)} %pad_add_fusion.place_ref, s32[4,128]{1,0:T(4,128)S(1)} %get-tuple-element.14.rows_ref, bf16[256,1024]{1,0:T(8,128)(2,1)S(1)} %copy-done, ...), custom_call_target="tpu_custom_call" | custom-call | tf_op jit(solution)/shard_map/members/pallas_call | solution.py:225
  82.8 0.0 collective-permute-done.3.refs_2_
  82.8 0.1 collective-permute-done.4.refs_3_
  82.9 0.0 copy-start.2
  82.9 0.7 copy-done.2
  83.5 0.0 copy-start.1
  83.5 1.5 %match.1 = f32[2,128]{1,0:T(2,128)} custom-call(s32[2]{0:T(128)S(1)} %copy-done.2, bf16[128,1024]{1,0:T(8,128)(2,1)S(1)} %get-tuple-element.16.refs_0_, bf16[128,1024]{1,0:T(8,128)(2,1)S(1)} %get-tuple-element.17.refs_1_, bf16[128,1024]{1,0:T(8,128)(2,1)S(1)} %collective-permute-done.3.refs_2_, bf16[128,1024]{1,0:T(8,128)(2,1)S(1)} %collective-permute-done.4.refs_3_), custom_call_target="tpu_custom_call" | custom-call | tf_op jit(solution)/shard_map/match/pallas_call | solution.py:237
  85.0 0.0 all-to-all-done.2
  85.0 0.0 copy-done.1
  85.0 0.7 finish.1
Async XLA Ops:
  2.6 29.8 %all-to-all-start = ((bf16[32,80,128]{2,1,0:T(8,128)(2,1)}), bf16[32,80,128]{2,1,0:T(8,128)(2,1)S(1)}, u32[]{:S(2)}, u32[]{:S(2)}) async-start(bf16[32,80,128]{2,1,0:T(8,128)(2,1)} %bitcast.12), calls=%async_computation | async-start | bytes 1310720 | tf_op jit(solution)/shard_map/all_to_all | solution.py:198
  34.9 4.8 %copy-start = (bf16[256,1024]{1,0:T(8,128)(2,1)S(1)}, bf16[256,1024]{1,0:T(8,128)(2,1)}, u32[]{:S(2)}) copy-start(bf16[256,1024]{1,0:T(8,128)(2,1)} %refs_0_.1) | copy-start | bytes 1572868
  35.0 13.8 %all-to-all-start.1 = ((f32[16,33,1,128]{3,2,1,0:T(1,128)}), f32[16,33,1,128]{3,2,1,0:T(1,128)S(1)}, u32[]{:S(2)}, u32[]{:S(2)}) async-start(f32[16,33,1,128]{3,2,1,0:T(1,128)} %bitcast.4), calls=%async_computation.1 | async-start | bytes 540672 | tf_op jit(solution)/shard_map/all_to_all | solution.py:210
  39.8 33.4 %collective-permute-start = (bf16[256,1024]{1,0:T(8,128)(2,1)S(1)}, bf16[256,1024]{1,0:T(8,128)(2,1)S(1)}, u32[]{:S(2)}, u32[]{:S(2)}) collective-permute-start(bf16[256,1024]{1,0:T(8,128)(2,1)S(1)} %copy-done), channel_id=1, source_target_pairs={{0,2},{2,0},{4,6},{6,4},{1,3},{3,1},{5,7},{7,5},{8,10},{10,8},{12,... | collective-permute-start | bytes 1572872 | tf_op jit(solution)/shard_map/ppermute | solution.py:209
  42.3 30.9 %collective-permute-start.1 = (bf16[256,1024]{1,0:T(8,128)(2,1)S(1)}, bf16[256,1024]{1,0:T(8,128)(2,1)S(1)}, u32[]{:S(2)}, u32[]{:S(2)}) collective-permute-start(bf16[256,1024]{1,0:T(8,128)(2,1)S(1)} %copy-done), channel_id=1, source_target_pairs={{0,6},{2,4},{4,2},{6,0},{1,7},{3,5},{5,3},{7,1},{8,14},{10,12},{12... | collective-permute-start | bytes 1572872 | tf_op jit(solution)/shard_map/ppermute | solution.py:209
  46.4 26.8 %collective-permute-start.2 = (bf16[256,1024]{1,0:T(8,128)(2,1)S(1)}, bf16[256,1024]{1,0:T(8,128)(2,1)S(1)}, u32[]{:S(2)}, u32[]{:S(2)}) collective-permute-start(bf16[256,1024]{1,0:T(8,128)(2,1)S(1)} %copy-done), channel_id=1, source_target_pairs={{0,4},{2,6},{4,0},{6,2},{1,5},{3,7},{5,1},{7,3},{8,12},{10,14},{12... | collective-permute-start | bytes 1572872 | tf_op jit(solution)/shard_map/ppermute | solution.py:209
  49.5 35.5 %all-to-all-start.2 = ((f32[8,17,1,128]{3,2,1,0:T(1,128)}), f32[8,17,1,128]{3,2,1,0:T(1,128)S(1)}, u32[]{:S(2)}, u32[]{:S(2)}) async-start(f32[8,17,1,128]{3,2,1,0:T(1,128)} %bitcast.6), calls=%async_computation.2 | async-start | bytes 139264 | tf_op jit(solution)/shard_map/all_to_all | solution.py:222
  74.6 8.2 %collective-permute-start.3 = (bf16[128,1024]{1,0:T(8,128)(2,1)S(1)}, bf16[128,1024]{1,0:T(8,128)(2,1)S(1)}, u32[]{:S(2)}, u32[]{:S(2)}) collective-permute-start(bf16[128,1024]{1,0:T(8,128)(2,1)S(1)} %get-tuple-element.18), channel_id=1, source_target_pairs={{0,1},{1,0},{2,3},{3,2},{4,5},{5,4},{6,7},{7,6},{8,9},{9,8},{10,11... | collective-permute-start | bytes 786440 | tf_op jit(solution)/shard_map/ppermute | solution.py:236
  79.4 3.4 %collective-permute-start.4 = (bf16[128,1024]{1,0:T(8,128)(2,1)S(1)}, bf16[128,1024]{1,0:T(8,128)(2,1)S(1)}, u32[]{:S(2)}, u32[]{:S(2)}) collective-permute-start(bf16[128,1024]{1,0:T(8,128)(2,1)S(1)} %get-tuple-element.19), channel_id=1, source_target_pairs={{0,1},{1,0},{2,3},{3,2},{4,5},{5,4},{6,7},{7,6},{8,9},{9,8},{10,11... | collective-permute-start | bytes 786440 | tf_op jit(solution)/shard_map/ppermute | solution.py:236
  82.9 0.7 copy-start.2
  83.5 1.5 %copy-start.1 = (f32[16,128]{1,0:T(8,128)S(1)}, f32[16,128]{1,0:T(8,128)}, u32[]{:S(2)}) copy-start(f32[16,128]{1,0:T(8,128)} %old_ref.1) | copy-start | bytes 24580

commit v8 on v7

--- a/solution.py
+++ b/solution.py
@@ -19,7 +19,7 @@
 BLOCK_ORDER = [k ^ 20 for k in range(BLOCK)]
 FIRST_ZL = 1
 PLANE_ORDER = [k ^ (4 * FIRST_ZL) for k in range(16)]
-FIRST_ZH = 4
+FIRST_ZH = 5
 RING_ORDER = [k ^ FIRST_ZH for k in range(8)]
 
 
@@ -154,19 +154,26 @@
         out_ref[...] = total.astype(BF16)
 
 
-def match_kernel(len_ref, *refs):
+def match_kernel(len_hbm, *refs):
     i = lax.broadcasted_iota(I32, (128, 128), 0)
     j = lax.broadcasted_iota(I32, (128, 128), 1)
-    own_refs, other_refs, out_ref = refs[0:2], refs[2:4], refs[4]
+    own_refs, other_refs, (out_ref, len_ref, sem) = refs[0:2], refs[2:4], refs[4:7]
+    lengths = pltpu.make_async_copy(len_hbm, len_ref, sem)
+    lengths.start()
+    i = lax.broadcasted_iota(I32, (128, 128), 0)
+    j = lax.broadcasted_iota(I32, (128, 128), 1)
+    cosines = []
     for s in range(2):
         one = own_refs[s][...] + other_refs[s][...]
         gram = lax.dot_general(one, one, (((1,), (1,)), ((), ())), preferred_element_type=F32)
         diagonal = jnp.where(i == j, gram, 0.0)
         down = lax.rsqrt(jnp.sum(diagonal, axis=1, keepdims=True) + 1e-06)
         across = lax.rsqrt(jnp.sum(diagonal, axis=0, keepdims=True) + 1e-06)
-        cosine = gram * down * across
+        cosines.append(gram * down * across)
+    lengths.wait()
+    for s in range(2):
         length = len_ref[s]
-        largest = jnp.max(jnp.where((i < length) & (i != j), cosine, -2.0), axis=0, keepdims=True)
+        largest = jnp.max(jnp.where((i < length) & (i != j), cosines[s], -2.0), axis=0, keepdims=True)
         out_ref[s : s + 1, :] = jnp.where(j[0:1] < length, largest, 0.0)
 
 
@@ -237,12 +244,13 @@
     best_cosine = pl.pallas_call(
         match_kernel,
         out_shape=jax.ShapeDtypeStruct((2, 128), F32),
-        in_specs=[SMEM] + [VMEM] * 4,
+        in_specs=[HBM] + [VMEM] * 4,
         out_specs=VMEM,
+        scratch_shapes=[pltpu.SMEM((2,), I32), pltpu.SemaphoreType.DMA],
         compiler_params=params(8),
         cost_estimate=cost(0, 0),
         name="match",
-    )(slab_len, *own, *others)
+    )(pltpu.with_memory_space_constraint(slab_len, pltpu.HBM), *own, *others)
     parts, best_cosine = lax.optimization_barrier((parts, best_cosine))
     centroids = pl.pallas_call(
         finish_kernel,

time: 86.3 us -> 81.2 us (0.941)
  starting transfers between devices: 65.2 us -> 60.5 us
    all_to_all x1, starting transfers between devices: 23.6 us -> 19 us  [local(): lax.all_to_all(parts.reshape(8, 17, 1, 128), 'zh', 0, 0, axis_index_group...]
  transfers between devices with their start and end apart: 8 -> 8, of which waited for: 2 -> 3; matrix products, arithmetic and copies ran while one was open for 0% -> 0% of each run, Pallas kernels for 6% -> 6%
where the time goes in v8:
time: 81.2 us; the launch traced here: 80.4 us
  starting transfers between devices  60.5 us (75%)
  Pallas kernels  10.2 us (13%)
  waiting for transfers between devices  8.84 us (11%)
    all_to_all x1, starting transfers between devices, local(): lax.all_to_all(messages.reshape(BLOCK, MSG, 128), ('x', 'y', 'c'), 0, 0,...  21.2 us
    all_to_all x1, starting transfers between devices, local(): lax.all_to_all(parts.reshape(8, 17, 1, 128), 'zh', 0, 0, axis_index_group...  19 us
    ppermute x3, starting transfers between devices, local(): lax.ppermute(embeddings, 'y', [(i, i ^ d) for i in range(4)])  8.98 us
    all_to_all x1, waiting for transfers between devices, local(): lax.all_to_all(messages.reshape(BLOCK, MSG, 128), ('x', 'y', 'c'), 0, 0,...  8.6 us
    ppermute x2, starting transfers between devices, local(): others = [lax.ppermute(other, 'c', [(0, 1), (1, 0)]) for other in others]  6.6 us
    all_to_all x1, starting transfers between devices, local(): lax.all_to_all(parts.reshape(16, 33, 1, 128), ('zl', 'x'), 0, 0, axis_ind...  4.8 us
    pallas_call x2, Pallas kernels, local(): pl.pallas_call(functools.partial(member_kernel, of), out_shape=[jax.Shape...  2.8 us
    pallas_call x1, Pallas kernels, local(): pl.pallas_call(sum_kernel, out_shape=(pltpu.VMEM((528, 128), F32), pltpu....  2.53 us
  transfers between devices with their start and end apart: 8, of which 3 were waited for; matrix products, arithmetic and copies ran while one was open for 0% of the time, Pallas kernels for 6%

profile of v8, /device:TPU:1, one launch (start us, length us, event | category | flops | bytes accessed | tf_op | source)
XLA Modules:
  0.0 80.4 jit_solution(3640566236898533515)
XLA Ops:
  0.6 2.0 %pack.1 = bf16[4,8,80,128]{3,2,1,0:T(8,128)(2,1)} custom-call(bf16[256,1024]{1,0:T(8,128)(2,1)} %refs_0_.1, s32[2,128]{1,0:T(2,128)} %bitcast.13, s32[2,128]{1,0:T(2,128)} %rows_hbm.1), custom_call_target="tpu_custom_call" | custom-call | flops 1048576 | bytes 1572864 | tf_op jit(solution)/shard_map/pack/pallas_call | solution.py:187
  2.6 21.2 %all-to-all-start = ((bf16[32,80,128]{2,1,0:T(8,128)(2,1)}), bf16[32,80,128]{2,1,0:T(8,128)(2,1)S(1)}, u32[]{:S(2)}, u32[]{:S(2)}) async-start(bf16[32,80,128]{2,1,0:T(8,128)(2,1)} %bitcast.12), calls=%async_computation | async-start | bytes 1310720 | tf_op jit(solution)/shard_map/all_to_all | solution.py:205
  23.8 8.6 %all-to-all-done.msg_ref = bf16[32,80,128]{2,1,0:T(8,128)(2,1)S(1)} async-done(((bf16[32,80,128]{2,1,0:T(8,128)(2,1)}), bf16[32,80,128]{2,1,0:T(8,128)(2,1)S(1)}, u32[]{:S(2)}, u32[]{:S(2)}) %all-to-all-start) | async-done | bytes 655392 | tf_op jit(solution)/shard_map/all_to_all | solution.py:205
  32.4 2.5 %sums.1 = (f32[528,128]{1,0:T(8,128)}, s32[4,128]{1,0:T(4,128)S(1)}) custom-call(s32[1]{0:T(128)} %bitcast.1.from_ref, bf16[32,80,128]{2,1,0:T(8,128)(2,1)S(1)} %all-to-all-done.msg_ref), custom_call_target="tpu_custom_call" | custom-call | flops 2147483648 | bytes 1048576 | tf_op jit(solution)/shard_map/sums/pallas_call | solution.py:206
  35.0 0.0 copy-start
  35.0 4.8 %all-to-all-start.1 = ((f32[16,33,1,128]{3,2,1,0:T(1,128)}), f32[16,33,1,128]{3,2,1,0:T(1,128)S(1)}, u32[]{:S(2)}, u32[]{:S(2)}) async-start(f32[16,33,1,128]{3,2,1,0:T(1,128)} %bitcast.4), calls=%async_computation.1 | async-start | bytes 540672 | tf_op jit(solution)/shard_map/all_to_all | solution.py:217
  39.8 0.0 copy-done
  39.8 2.5 %collective-permute-start = (bf16[256,1024]{1,0:T(8,128)(2,1)S(1)}, bf16[256,1024]{1,0:T(8,128)(2,1)S(1)}, u32[]{:S(2)}, u32[]{:S(2)}) collective-permute-start(bf16[256,1024]{1,0:T(8,128)(2,1)S(1)} %copy-done), channel_id=1, source_target_pairs={{0,2},{2,0},{4,6},{6,4},{1,3},{3,1},{5,7},{7,5},{8,10},{10,8},{12,... | collective-permute-start | bytes 1572872 | tf_op jit(solution)/shard_map/ppermute | solution.py:216
  42.3 4.1 %collective-permute-start.1 = (bf16[256,1024]{1,0:T(8,128)(2,1)S(1)}, bf16[256,1024]{1,0:T(8,128)(2,1)S(1)}, u32[]{:S(2)}, u32[]{:S(2)}) collective-permute-start(bf16[256,1024]{1,0:T(8,128)(2,1)S(1)} %copy-done), channel_id=1, source_target_pairs={{0,6},{2,4},{4,2},{6,0},{1,7},{3,5},{5,3},{7,1},{8,14},{10,12},{12... | collective-permute-start | bytes 1572872 | tf_op jit(solution)/shard_map/ppermute | solution.py:216
  46.4 2.4 %collective-permute-start.2 = (bf16[256,1024]{1,0:T(8,128)(2,1)S(1)}, bf16[256,1024]{1,0:T(8,128)(2,1)S(1)}, u32[]{:S(2)}, u32[]{:S(2)}) collective-permute-start(bf16[256,1024]{1,0:T(8,128)(2,1)S(1)} %copy-done), channel_id=1, source_target_pairs={{0,4},{2,6},{4,0},{6,2},{1,5},{3,7},{5,1},{7,3},{8,12},{10,14},{12... | collective-permute-start | bytes 1572872 | tf_op jit(solution)/shard_map/ppermute | solution.py:216
  48.8 0.0 all-to-all-done.1
  48.8 0.8 regroup.1.after_ref
  49.5 19.0 %all-to-all-start.2 = ((f32[8,17,1,128]{3,2,1,0:T(1,128)}), f32[8,17,1,128]{3,2,1,0:T(1,128)S(1)}, u32[]{:S(2)}, u32[]{:S(2)}) async-start(f32[8,17,1,128]{3,2,1,0:T(1,128)} %bitcast.6), calls=%async_computation.2 | async-start | bytes 139264 | tf_op jit(solution)/shard_map/all_to_all | solution.py:229
  68.5 0.1 pad_add_fusion.place_ref
  68.6 0.0 collective-permute-done.refs_1_
  68.6 0.2 collective-permute-done.1.refs_2_
  68.8 0.0 collective-permute-done.2.refs_3_
  68.8 1.4 %members.3 = (bf16[128,1024]{1,0:T(8,128)(2,1)S(1)}, bf16[128,1024]{1,0:T(8,128)(2,1)S(1)}) custom-call(f32[136,128]{1,0:T(8,128)} %regroup.1.after_ref, s32[2]{0:T(128)S(1)} %pad_add_fusion.place_ref, s32[4,128]{1,0:T(4,128)S(1)} %get-tuple-element.14.rows_ref, bf16[256,1024]{1,0:T(8,128)(2,1)S(1)} %copy-done, ...), custom_call_target="tpu_custom_call" | custom-call | tf_op jit(solution)/shard_map/members/pallas_call | solution.py:232
  70.2 4.7 %collective-permute-start.3 = (bf16[128,1024]{1,0:T(8,128)(2,1)S(1)}, bf16[128,1024]{1,0:T(8,128)(2,1)S(1)}, u32[]{:S(2)}, u32[]{:S(2)}) collective-permute-start(bf16[128,1024]{1,0:T(8,128)(2,1)S(1)} %get-tuple-element.18), channel_id=1, source_target_pairs={{0,1},{1,0},{2,3},{3,2},{4,5},{5,4},{6,7},{7,6},{8,9},{9,8},{10,11... | collective-permute-start | bytes 786440 | tf_op jit(solution)/shard_map/ppermute | solution.py:243
  74.8 1.9 %collective-permute-start.4 = (bf16[128,1024]{1,0:T(8,128)(2,1)S(1)}, bf16[128,1024]{1,0:T(8,128)(2,1)S(1)}, u32[]{:S(2)}, u32[]{:S(2)}) collective-permute-start(bf16[128,1024]{1,0:T(8,128)(2,1)S(1)} %get-tuple-element.19), channel_id=1, source_target_pairs={{0,1},{1,0},{2,3},{3,2},{4,5},{5,4},{6,7},{7,6},{8,9},{9,8},{10,11... | collective-permute-start | bytes 786440 | tf_op jit(solution)/shard_map/ppermute | solution.py:243
  76.8 1.4 %members.2 = (bf16[128,1024]{1,0:T(8,128)(2,1)S(1)}, bf16[128,1024]{1,0:T(8,128)(2,1)S(1)}) custom-call(f32[136,128]{1,0:T(8,128)} %regroup.1.after_ref, s32[2]{0:T(128)S(1)} %pad_add_fusion.place_ref, s32[4,128]{1,0:T(4,128)S(1)} %get-tuple-element.14.rows_ref, bf16[256,1024]{1,0:T(8,128)(2,1)S(1)} %copy-done, ...), custom_call_target="tpu_custom_call" | custom-call | tf_op jit(solution)/shard_map/members/pallas_call | solution.py:232
  78.2 0.0 collective-permute-done.3.refs_2_
  78.2 0.1 collective-permute-done.4.refs_3_
  78.3 0.0 copy-start.1
  78.3 1.4 %match.1 = f32[2,128]{1,0:T(2,128)} custom-call(s32[2]{0:T(128)} %len_hbm.1, bf16[128,1024]{1,0:T(8,128)(2,1)S(1)} %get-tuple-element.16.refs_0_, bf16[128,1024]{1,0:T(8,128)(2,1)S(1)} %get-tuple-element.17.refs_1_, bf16[128,1024]{1,0:T(8,128)(2,1)S(1)} %collective-permute-done.3.refs_2_, bf16[128,1024]{1,0:T(8,128)(2,1)S(1)} %collective-permute-done.4.refs_3_), custom_call_target="tpu_custom_call" | custom-call | tf_op jit(solution)/shard_map/match/pallas_call | solution.py:244
  79.7 0.0 all-to-all-done.2
  79.7 0.0 copy-done.1
  79.7 0.7 finish.1
Async XLA Ops:
  2.6 29.8 %all-to-all-start = ((bf16[32,80,128]{2,1,0:T(8,128)(2,1)}), bf16[32,80,128]{2,1,0:T(8,128)(2,1)S(1)}, u32[]{:S(2)}, u32[]{:S(2)}) async-start(bf16[32,80,128]{2,1,0:T(8,128)(2,1)} %bitcast.12), calls=%async_computation | async-start | bytes 1310720 | tf_op jit(solution)/shard_map/all_to_all | solution.py:205
  35.0 4.8 %copy-start = (bf16[256,1024]{1,0:T(8,128)(2,1)S(1)}, bf16[256,1024]{1,0:T(8,128)(2,1)}, u32[]{:S(2)}) copy-start(bf16[256,1024]{1,0:T(8,128)(2,1)} %refs_0_.1) | copy-start | bytes 1572868
  35.0 13.8 %all-to-all-start.1 = ((f32[16,33,1,128]{3,2,1,0:T(1,128)}), f32[16,33,1,128]{3,2,1,0:T(1,128)S(1)}, u32[]{:S(2)}, u32[]{:S(2)}) async-start(f32[16,33,1,128]{3,2,1,0:T(1,128)} %bitcast.4), calls=%async_computation.1 | async-start | bytes 540672 | tf_op jit(solution)/shard_map/all_to_all | solution.py:217
  39.8 28.8 %collective-permute-start = (bf16[256,1024]{1,0:T(8,128)(2,1)S(1)}, bf16[256,1024]{1,0:T(8,128)(2,1)S(1)}, u32[]{:S(2)}, u32[]{:S(2)}) collective-permute-start(bf16[256,1024]{1,0:T(8,128)(2,1)S(1)} %copy-done), channel_id=1, source_target_pairs={{0,2},{2,0},{4,6},{6,4},{1,3},{3,1},{5,7},{7,5},{8,10},{10,8},{12,... | collective-permute-start | bytes 1572872 | tf_op jit(solution)/shard_map/ppermute | solution.py:216
  42.3 26.5 %collective-permute-start.1 = (bf16[256,1024]{1,0:T(8,128)(2,1)S(1)}, bf16[256,1024]{1,0:T(8,128)(2,1)S(1)}, u32[]{:S(2)}, u32[]{:S(2)}) collective-permute-start(bf16[256,1024]{1,0:T(8,128)(2,1)S(1)} %copy-done), channel_id=1, source_target_pairs={{0,6},{2,4},{4,2},{6,0},{1,7},{3,5},{5,3},{7,1},{8,14},{10,12},{12... | collective-permute-start | bytes 1572872 | tf_op jit(solution)/shard_map/ppermute | solution.py:216
  46.4 22.4 %collective-permute-start.2 = (bf16[256,1024]{1,0:T(8,128)(2,1)S(1)}, bf16[256,1024]{1,0:T(8,128)(2,1)S(1)}, u32[]{:S(2)}, u32[]{:S(2)}) collective-permute-start(bf16[256,1024]{1,0:T(8,128)(2,1)S(1)} %copy-done), channel_id=1, source_target_pairs={{0,4},{2,6},{4,0},{6,2},{1,5},{3,7},{5,1},{7,3},{8,12},{10,14},{12... | collective-permute-start | bytes 1572872 | tf_op jit(solution)/shard_map/ppermute | solution.py:216
  49.5 30.2 %all-to-all-start.2 = ((f32[8,17,1,128]{3,2,1,0:T(1,128)}), f32[8,17,1,128]{3,2,1,0:T(1,128)S(1)}, u32[]{:S(2)}, u32[]{:S(2)}) async-start(f32[8,17,1,128]{3,2,1,0:T(1,128)} %bitcast.6), calls=%async_computation.2 | async-start | bytes 139264 | tf_op jit(solution)/shard_map/all_to_all | solution.py:229
  70.2 8.0 %collective-permute-start.3 = (bf16[128,1024]{1,0:T(8,128)(2,1)S(1)}, bf16[128,1024]{1,0:T(8,128)(2,1)S(1)}, u32[]{:S(2)}, u32[]{:S(2)}) collective-permute-start(bf16[128,1024]{1,0:T(8,128)(2,1)S(1)} %get-tuple-element.18), channel_id=1, source_target_pairs={{0,1},{1,0},{2,3},{3,2},{4,5},{5,4},{6,7},{7,6},{8,9},{9,8},{10,11... | collective-permute-start | bytes 786440 | tf_op jit(solution)/shard_map/ppermute | solution.py:243
  74.8 3.4 %collective-permute-start.4 = (bf16[128,1024]{1,0:T(8,128)(2,1)S(1)}, bf16[128,1024]{1,0:T(8,128)(2,1)S(1)}, u32[]{:S(2)}, u32[]{:S(2)}) collective-permute-start(bf16[128,1024]{1,0:T(8,128)(2,1)S(1)} %get-tuple-element.19), channel_id=1, source_target_pairs={{0,1},{1,0},{2,3},{3,2},{4,5},{5,4},{6,7},{7,6},{8,9},{9,8},{10,11... | collective-permute-start | bytes 786440 | tf_op jit(solution)/shard_map/ppermute | solution.py:243
  78.3 1.5 %copy-start.1 = (f32[16,128]{1,0:T(8,128)S(1)}, f32[16,128]{1,0:T(8,128)}, u32[]{:S(2)}) copy-start(f32[16,128]{1,0:T(8,128)} %old_ref.1) | copy-start | bytes 24580

commit v9 on v8

--- a/solution.py
+++ b/solution.py
@@ -140,17 +140,21 @@
 
 
 def member_kernel(of, after_ref, place_ref, rows_ref, *refs):
-    line_refs, out_refs = refs[:4], refs[4:]
+    line_refs, out_refs = refs[:3], refs[3:]
     core, y = place_ref[0], place_ref[1]
     lane = lax.broadcasted_iota(I32, (128, ROWS), 1)
     r = rows_ref[2 * of : 2 * of + 2, :]
-    at = jnp.where(((r >> 8) & 1) == core, (((r >> 9) ^ y) << 8) + (r & 255), -1)
+    away, far = (r >> 9) ^ y, ((r >> 8) & 1) ^ core
+    block = jnp.where(away == 1 + 2 * core, 1 + far, jnp.where(far == 1, -1, jnp.where(away == 0, 0, jnp.where(away == 2, 3, -1))))
+    at = jnp.where(block < 0, -1, (block << 8) + (r & 255))
     at = jnp.concatenate([at, jnp.zeros((6, 128), I32)], 0).astype(F32).T.astype(I32)
     for s, out_ref in enumerate(out_refs):
         total = jnp.zeros((128, 1024), F32)
-        for away, line_ref in zip((0, 1, 3, 2), line_refs):
-            pick = jnp.where(lane + 256 * away == at[:, s : s + 1], 1.0, 0.0).astype(BF16)
-            total = total + jnp.dot(pick, line_ref[...], preferred_element_type=F32)
+        for first, line_ref in zip((0, 1, 3), line_refs):
+            for k in range(line_ref.shape[0] // ROWS):
+                pick = jnp.where(lane + ROWS * (first + k) == at[:, s : s + 1], 1.0, 0.0).astype(BF16)
+                rows = line_ref[ROWS * k : ROWS * k + ROWS, :]
+                total = total + jnp.dot(pick, rows, preferred_element_type=F32)
         out_ref[...] = total.astype(BF16)
 
 
@@ -212,8 +216,14 @@
         cost_estimate=cost(1 << 31, 1 << 20),
         name="sums",
     )(((x * 8 + y * 2 + core) ^ BLOCK_ORDER[0]).reshape(1), messages)
-    embeddings, parts = lax.optimization_barrier((embeddings, parts))
-    line = [embeddings] + [lax.ppermute(embeddings, "y", [(i, i ^ d) for i in range(4)]) for d in (1, 3, 2)]
+    partner = lax.ppermute(embeddings, "c", [(0, 1), (1, 0)])
+    embeddings, partner, parts = lax.optimization_barrier((embeddings, partner, parts))
+    near = [(2 * i + c, 2 * (i ^ (1 + 2 * c)) + c) for i in range(4) for c in range(2)]
+    line = [
+        embeddings,
+        lax.ppermute(jnp.concatenate([embeddings, partner]), ("y", "c"), near),
+        lax.ppermute(embeddings, "y", [(i, i ^ 2) for i in range(4)]),
+    ]
     parts = lax.all_to_all(parts.reshape(16, 33, 1, 128), ("zl", "x"), 0, 0, axis_index_groups=[PLANE_ORDER], tiled=True)
     parts = pl.pallas_call(
         regroup_kernel,
@@ -232,7 +242,7 @@
         pl.pallas_call(
             functools.partial(member_kernel, of),
             out_shape=[jax.ShapeDtypeStruct((128, 1024), BF16)] * 2,
-            in_specs=[pl.BlockSpec(memory_space=pl.ANY), SMEM] + [VMEM] * 5,
+            in_specs=[pl.BlockSpec(memory_space=pl.ANY), SMEM] + [VMEM] * 4,
             out_specs=[VMEM] * 2,
             compiler_params=params(16),
             cost_estimate=cost(0, 0),

time: 81.2 us -> 81 us (level)
  waiting for transfers between devices: 8.84 us -> 7.21 us
    all_to_all x1, waiting for transfers between devices: 8.6 us -> 6.31 us  [local(): lax.all_to_all(messages.reshape(BLOCK, MSG, 128), ('x', 'y', 'c'), 0, 0,...]
    ppermute x2, starting transfers between devices: 6.6 us -> 7.74 us  [local(): others = [lax.ppermute(other, 'c', [(0, 1), (1, 0)]) for other in others]]
    all_to_all x1, waiting for transfers between devices: 0.01 us -> 0.85 us  [local(): lax.all_to_all(parts.reshape(16, 33, 1, 128), ('zl', 'x'), 0, 0, axis_ind...]
  transfers between devices with their start and end apart: 8 -> 8, of which waited for: 3 -> 2; matrix products, arithmetic and copies ran while one was open for 0% -> 0% of each run, Pallas kernels for 6% -> 10%
where the time goes in v9:
time: 81 us; the launch traced here: 79.6 us
  starting transfers between devices  61.1 us (75%)
  Pallas kernels  10.3 us (13%)
  waiting for transfers between devices  7.21 us (9%)
    all_to_all x1, starting transfers between devices, local(): lax.all_to_all(messages.reshape(BLOCK, MSG, 128), ('x', 'y', 'c'), 0, 0,...  21.2 us
    all_to_all x1, starting transfers between devices, local(): lax.all_to_all(parts.reshape(8, 17, 1, 128), 'zh', 0, 0, axis_index_group...  19 us
    ppermute x2, starting transfers between devices, local(): others = [lax.ppermute(other, 'c', [(0, 1), (1, 0)]) for other in others]  7.74 us
    all_to_all x1, waiting for transfers between devices, local(): lax.all_to_all(messages.reshape(BLOCK, MSG, 128), ('x', 'y', 'c'), 0, 0,...  6.31 us
    all_to_all x1, starting transfers between devices, local(): lax.all_to_all(parts.reshape(16, 33, 1, 128), ('zl', 'x'), 0, 0, axis_ind...  4.67 us
    ppermute x1, starting transfers between devices, local(): lax.ppermute(jnp.concatenate([embeddings, partner]), ('y', 'c'), near)  3.57 us
    pallas_call x2, Pallas kernels, local(): pl.pallas_call(functools.partial(member_kernel, of), out_shape=[jax.Shape...  2.84 us
    ppermute x1, starting transfers between devices, local(): lax.ppermute(embeddings, 'y', [(i, i ^ 2) for i in range(4)])  2.74 us
  transfers between devices with their start and end apart: 8, of which 2 were waited for; matrix products, arithmetic and copies ran while one was open for 0% of the time, Pallas kernels for 10%

profile of v9, /device:TPU:1, one launch (start us, length us, event | category | flops | bytes accessed | tf_op | source)
XLA Modules:
  0.0 79.6 jit_solution(13342158703676191740)
XLA Ops:
  0.6 0.0 copy-start
  0.6 2.1 %pack.1 = bf16[4,8,80,128]{3,2,1,0:T(8,128)(2,1)} custom-call(bf16[256,1024]{1,0:T(8,128)(2,1)} %refs_0_.1, s32[2,128]{1,0:T(2,128)} %bitcast.13, s32[2,128]{1,0:T(2,128)} %rows_hbm.1), custom_call_target="tpu_custom_call" | custom-call | flops 1048576 | bytes 1572864 | tf_op jit(solution)/shard_map/pack/pallas_call | solution.py:191
  2.7 21.2 %all-to-all-start = ((bf16[32,80,128]{2,1,0:T(8,128)(2,1)}), bf16[32,80,128]{2,1,0:T(8,128)(2,1)S(1)}, u32[]{:S(2)}, u32[]{:S(2)}) async-start(bf16[32,80,128]{2,1,0:T(8,128)(2,1)} %bitcast.12), calls=%async_computation | async-start | bytes 1310720 | tf_op jit(solution)/shard_map/all_to_all | solution.py:209
  23.9 0.0 copy-done
  23.9 2.3 %collective-permute-start = (bf16[256,1024]{1,0:T(8,128)(2,1)S(1)}, bf16[256,1024]{1,0:T(8,128)(2,1)S(1)}, u32[]{:S(2)}, u32[]{:S(2)}) collective-permute-start(bf16[256,1024]{1,0:T(8,128)(2,1)S(1)} %copy-done), channel_id=1, source_target_pairs={{0,1},{1,0},{2,3},{3,2},{4,5},{5,4},{6,7},{7,6},{8,9},{9,8},{10,11... | collective-permute-start | bytes 1572872 | tf_op jit(solution)/shard_map/ppermute | solution.py:219
  26.2 6.3 %all-to-all-done.msg_ref = bf16[32,80,128]{2,1,0:T(8,128)(2,1)S(1)} async-done(((bf16[32,80,128]{2,1,0:T(8,128)(2,1)}), bf16[32,80,128]{2,1,0:T(8,128)(2,1)S(1)}, u32[]{:S(2)}, u32[]{:S(2)}) %all-to-all-start) | async-done | bytes 655392 | tf_op jit(solution)/shard_map/all_to_all | solution.py:209
  32.5 2.5 %sums.1 = (f32[528,128]{1,0:T(8,128)}, s32[4,128]{1,0:T(4,128)S(1)}) custom-call(s32[1]{0:T(128)} %bitcast.1.from_ref, bf16[32,80,128]{2,1,0:T(8,128)(2,1)S(1)} %all-to-all-done.msg_ref), custom_call_target="tpu_custom_call" | custom-call | flops 2147483648 | bytes 1048576 | tf_op jit(solution)/shard_map/sums/pallas_call | solution.py:210
  35.0 0.0 collective-permute-done
  35.0 4.7 %all-to-all-start.1 = ((f32[16,33,1,128]{3,2,1,0:T(1,128)}), f32[16,33,1,128]{3,2,1,0:T(1,128)S(1)}, u32[]{:S(2)}, u32[]{:S(2)}) async-start(f32[16,33,1,128]{3,2,1,0:T(1,128)} %bitcast.4), calls=%async_computation.1 | async-start | bytes 540672 | tf_op jit(solution)/shard_map/all_to_all | solution.py:227
  39.7 0.1 pad_maximum_fusion
  39.8 3.6 %collective-permute-start.1 = (bf16[512,1024]{1,0:T(8,128)(2,1)S(1)}, bf16[512,1024]{1,0:T(8,128)(2,1)S(1)}, u32[]{:S(2)}, u32[]{:S(2)}) collective-permute-start(bf16[512,1024]{1,0:T(8,128)(2,1)S(1)} %pad_maximum_fusion), channel_id=1, source_target_pairs={{0,2},{1,7},{2,0},{3,5},{4,6},{5,3},{6,4},{7,1},{8,10},{9,15},{10,... | collective-permute-start | bytes 3145736 | tf_op jit(solution)/shard_map/ppermute | solution.py:224
  43.4 2.7 %collective-permute-start.2 = (bf16[256,1024]{1,0:T(8,128)(2,1)S(1)}, bf16[256,1024]{1,0:T(8,128)(2,1)S(1)}, u32[]{:S(2)}, u32[]{:S(2)}) collective-permute-start(bf16[256,1024]{1,0:T(8,128)(2,1)S(1)} %copy-done), channel_id=1, source_target_pairs={{0,4},{2,6},{4,0},{6,2},{1,5},{3,7},{5,1},{7,3},{8,12},{10,14},{12... | collective-permute-start | bytes 1572872 | tf_op jit(solution)/shard_map/ppermute | solution.py:225
  46.1 0.8 %all-to-all-done.1 = f32[16,33,1,128]{3,2,1,0:T(1,128)S(1)} async-done(((f32[16,33,1,128]{3,2,1,0:T(1,128)}), f32[16,33,1,128]{3,2,1,0:T(1,128)S(1)}, u32[]{:S(2)}, u32[]{:S(2)}) %all-to-all-start.1) | async-done | bytes 270368 | tf_op jit(solution)/shard_map/all_to_all | solution.py:227
  47.0 0.8 regroup.1.after_ref
  47.7 19.0 %all-to-all-start.2 = ((f32[8,17,1,128]{3,2,1,0:T(1,128)}), f32[8,17,1,128]{3,2,1,0:T(1,128)S(1)}, u32[]{:S(2)}, u32[]{:S(2)}) async-start(f32[8,17,1,128]{3,2,1,0:T(1,128)} %bitcast.6), calls=%async_computation.2 | async-start | bytes 139264 | tf_op jit(solution)/shard_map/all_to_all | solution.py:239
  66.7 0.1 pad_add_fusion.place_ref
  66.7 0.0 collective-permute-done.2.refs_2_
  66.7 0.0 collective-permute-done.1.refs_1_
  66.8 1.4 %members.3 = (bf16[128,1024]{1,0:T(8,128)(2,1)S(1)}, bf16[128,1024]{1,0:T(8,128)(2,1)S(1)}) custom-call(f32[136,128]{1,0:T(8,128)} %regroup.1.after_ref, s32[2]{0:T(128)S(1)} %pad_add_fusion.place_ref, s32[4,128]{1,0:T(4,128)S(1)} %get-tuple-element.15.rows_ref, bf16[256,1024]{1,0:T(8,128)(2,1)S(1)} %copy-done, ...), custom_call_target="tpu_custom_call" | custom-call | tf_op jit(solution)/shard_map/members/pallas_call | solution.py:242
  68.2 5.8 %collective-permute-start.3 = (bf16[128,1024]{1,0:T(8,128)(2,1)S(1)}, bf16[128,1024]{1,0:T(8,128)(2,1)S(1)}, u32[]{:S(2)}, u32[]{:S(2)}) collective-permute-start(bf16[128,1024]{1,0:T(8,128)(2,1)S(1)} %get-tuple-element.20), channel_id=1, source_target_pairs={{0,1},{1,0},{2,3},{3,2},{4,5},{5,4},{6,7},{7,6},{8,9},{9,8},{10,11... | collective-permute-start | bytes 786440 | tf_op jit(solution)/shard_map/ppermute | solution.py:253
  74.0 1.9 %collective-permute-start.4 = (bf16[128,1024]{1,0:T(8,128)(2,1)S(1)}, bf16[128,1024]{1,0:T(8,128)(2,1)S(1)}, u32[]{:S(2)}, u32[]{:S(2)}) collective-permute-start(bf16[128,1024]{1,0:T(8,128)(2,1)S(1)} %get-tuple-element.21), channel_id=1, source_target_pairs={{0,1},{1,0},{2,3},{3,2},{4,5},{5,4},{6,7},{7,6},{8,9},{9,8},{10,11... | collective-permute-start | bytes 786440 | tf_op jit(solution)/shard_map/ppermute | solution.py:253
  75.9 1.4 %members.2 = (bf16[128,1024]{1,0:T(8,128)(2,1)S(1)}, bf16[128,1024]{1,0:T(8,128)(2,1)S(1)}) custom-call(f32[136,128]{1,0:T(8,128)} %regroup.1.after_ref, s32[2]{0:T(128)S(1)} %pad_add_fusion.place_ref, s32[4,128]{1,0:T(4,128)S(1)} %get-tuple-element.15.rows_ref, bf16[256,1024]{1,0:T(8,128)(2,1)S(1)} %copy-done, ...), custom_call_target="tpu_custom_call" | custom-call | tf_op jit(solution)/shard_map/members/pallas_call | solution.py:242
  77.4 0.0 copy-start.1
  77.4 0.0 collective-permute-done.3.refs_2_
  77.4 0.0 collective-permute-done.4.refs_3_
  77.4 1.4 %match.1 = f32[2,128]{1,0:T(2,128)} custom-call(s32[2]{0:T(128)} %len_hbm.1, bf16[128,1024]{1,0:T(8,128)(2,1)S(1)} %get-tuple-element.18.refs_0_, bf16[128,1024]{1,0:T(8,128)(2,1)S(1)} %get-tuple-element.19.refs_1_, bf16[128,1024]{1,0:T(8,128)(2,1)S(1)} %collective-permute-done.3.refs_2_, bf16[128,1024]{1,0:T(8,128)(2,1)S(1)} %collective-permute-done.4.refs_3_), custom_call_target="tpu_custom_call" | custom-call | tf_op jit(solution)/shard_map/match/pallas_call | solution.py:254
  78.9 0.0 all-to-all-done.2
  78.9 0.0 copy-done.1
  78.9 0.7 finish.1
Async XLA Ops:
  0.6 23.3 %copy-start = (bf16[256,1024]{1,0:T(8,128)(2,1)S(1)}, bf16[256,1024]{1,0:T(8,128)(2,1)}, u32[]{:S(2)}) copy-start(bf16[256,1024]{1,0:T(8,128)(2,1)} %refs_0_.1) | copy-start | bytes 1572868
  2.7 29.8 %all-to-all-start = ((bf16[32,80,128]{2,1,0:T(8,128)(2,1)}), bf16[32,80,128]{2,1,0:T(8,128)(2,1)S(1)}, u32[]{:S(2)}, u32[]{:S(2)}) async-start(bf16[32,80,128]{2,1,0:T(8,128)(2,1)} %bitcast.12), calls=%async_computation | async-start | bytes 1310720 | tf_op jit(solution)/shard_map/all_to_all | solution.py:209
  23.9 11.1 %collective-permute-start = (bf16[256,1024]{1,0:T(8,128)(2,1)S(1)}, bf16[256,1024]{1,0:T(8,128)(2,1)S(1)}, u32[]{:S(2)}, u32[]{:S(2)}) collective-permute-start(bf16[256,1024]{1,0:T(8,128)(2,1)S(1)} %copy-done), channel_id=1, source_target_pairs={{0,1},{1,0},{2,3},{3,2},{4,5},{5,4},{6,7},{7,6},{8,9},{9,8},{10,11... | collective-permute-start | bytes 1572872 | tf_op jit(solution)/shard_map/ppermute | solution.py:219
  35.0 11.9 %all-to-all-start.1 = ((f32[16,33,1,128]{3,2,1,0:T(1,128)}), f32[16,33,1,128]{3,2,1,0:T(1,128)S(1)}, u32[]{:S(2)}, u32[]{:S(2)}) async-start(f32[16,33,1,128]{3,2,1,0:T(1,128)} %bitcast.4), calls=%async_computation.1 | async-start | bytes 540672 | tf_op jit(solution)/shard_map/all_to_all | solution.py:227
  39.8 27.0 %collective-permute-start.1 = (bf16[512,1024]{1,0:T(8,128)(2,1)S(1)}, bf16[512,1024]{1,0:T(8,128)(2,1)S(1)}, u32[]{:S(2)}, u32[]{:S(2)}) collective-permute-start(bf16[512,1024]{1,0:T(8,128)(2,1)S(1)} %pad_maximum_fusion), channel_id=1, source_target_pairs={{0,2},{1,7},{2,0},{3,5},{4,6},{5,3},{6,4},{7,1},{8,10},{9,15},{10,... | collective-permute-start | bytes 3145736 | tf_op jit(solution)/shard_map/ppermute | solution.py:224
  43.4 23.4 %collective-permute-start.2 = (bf16[256,1024]{1,0:T(8,128)(2,1)S(1)}, bf16[256,1024]{1,0:T(8,128)(2,1)S(1)}, u32[]{:S(2)}, u32[]{:S(2)}) collective-permute-start(bf16[256,1024]{1,0:T(8,128)(2,1)S(1)} %copy-done), channel_id=1, source_target_pairs={{0,4},{2,6},{4,0},{6,2},{1,5},{3,7},{5,1},{7,3},{8,12},{10,14},{12... | collective-permute-start | bytes 1572872 | tf_op jit(solution)/shard_map/ppermute | solution.py:225
  47.7 31.2 %all-to-all-start.2 = ((f32[8,17,1,128]{3,2,1,0:T(1,128)}), f32[8,17,1,128]{3,2,1,0:T(1,128)S(1)}, u32[]{:S(2)}, u32[]{:S(2)}) async-start(f32[8,17,1,128]{3,2,1,0:T(1,128)} %bitcast.6), calls=%async_computation.2 | async-start | bytes 139264 | tf_op jit(solution)/shard_map/all_to_all | solution.py:239
  68.2 9.2 %collective-permute-start.3 = (bf16[128,1024]{1,0:T(8,128)(2,1)S(1)}, bf16[128,1024]{1,0:T(8,128)(2,1)S(1)}, u32[]{:S(2)}, u32[]{:S(2)}) collective-permute-start(bf16[128,1024]{1,0:T(8,128)(2,1)S(1)} %get-tuple-element.20), channel_id=1, source_target_pairs={{0,1},{1,0},{2,3},{3,2},{4,5},{5,4},{6,7},{7,6},{8,9},{9,8},{10,11... | collective-permute-start | bytes 786440 | tf_op jit(solution)/shard_map/ppermute | solution.py:253
  74.0 3.4 %collective-permute-start.4 = (bf16[128,1024]{1,0:T(8,128)(2,1)S(1)}, bf16[128,1024]{1,0:T(8,128)(2,1)S(1)}, u32[]{:S(2)}, u32[]{:S(2)}) collective-permute-start(bf16[128,1024]{1,0:T(8,128)(2,1)S(1)} %get-tuple-element.21), channel_id=1, source_target_pairs={{0,1},{1,0},{2,3},{3,2},{4,5},{5,4},{6,7},{7,6},{8,9},{9,8},{10,11... | collective-permute-start | bytes 786440 | tf_op jit(solution)/shard_map/ppermute | solution.py:253
  77.4 1.5 %copy-start.1 = (f32[16,128]{1,0:T(8,128)S(1)}, f32[16,128]{1,0:T(8,128)}, u32[]{:S(2)}) copy-start(f32[16,128]{1,0:T(8,128)} %old_ref.1) | copy-start | bytes 24580

commit v10 on v9

--- a/solution.py
+++ b/solution.py
@@ -17,8 +17,8 @@
 MIB = 1 << 20
 FIRST = (2, 4)
 BLOCK_ORDER = [k ^ 20 for k in range(BLOCK)]
-FIRST_ZL = 1
-PLANE_ORDER = [k ^ (4 * FIRST_ZL) for k in range(16)]
+PLANE_FIRST = (1, 2)
+PLANE_ORDER = [k ^ 6 for k in range(16)]
 FIRST_ZH = 5
 RING_ORDER = [k ^ FIRST_ZH for k in range(8)]
 
@@ -108,7 +108,7 @@
     slot = lax.broadcasted_iota(I32, (32, 128), 1) // FEATS
     parts = []
     for x in range(4):
-        first, *others = (in_ref[33 * (4 * zl + x) : 33 * (4 * zl + x) + 32, :] for zl in range(4))
+        first, *others = (in_ref[33 * at : 33 * at + 32, :] for at in range(x ^ PLANE_FIRST[1], 16, 4))
         parts.append((first + others[0]) + (others[1] + others[2]))
     first, *others = (in_ref[33 * 4 * zl + 32 : 33 * 4 * zl + 33, :] for zl in range(4))
     counts = (first + others[0]) + (others[1] + others[2])
@@ -142,20 +142,21 @@
 def member_kernel(of, after_ref, place_ref, rows_ref, *refs):
     line_refs, out_refs = refs[:3], refs[3:]
     core, y = place_ref[0], place_ref[1]
-    lane = lax.broadcasted_iota(I32, (128, ROWS), 1)
     r = rows_ref[2 * of : 2 * of + 2, :]
     away, far = (r >> 9) ^ y, ((r >> 8) & 1) ^ core
     block = jnp.where(away == 1 + 2 * core, 1 + far, jnp.where(far == 1, -1, jnp.where(away == 0, 0, jnp.where(away == 2, 3, -1))))
     at = jnp.where(block < 0, -1, (block << 8) + (r & 255))
     at = jnp.concatenate([at, jnp.zeros((6, 128), I32)], 0).astype(F32).T.astype(I32)
+    at = jnp.concatenate([at[:, 0:1], at[:, 1:2]], 0)
+    lane = lax.broadcasted_iota(I32, (256, ROWS), 1)
+    total = jnp.zeros((256, 1024), F32)
+    for first, line_ref in zip((0, 1, 3), line_refs):
+        for k in range(line_ref.shape[0] // ROWS):
+            pick = jnp.where(lane + ROWS * (first + k) == at, 1.0, 0.0).astype(BF16)
+            rows = line_ref[ROWS * k : ROWS * k + ROWS, :]
+            total = total + jnp.dot(pick, rows, preferred_element_type=F32)
     for s, out_ref in enumerate(out_refs):
-        total = jnp.zeros((128, 1024), F32)
-        for first, line_ref in zip((0, 1, 3), line_refs):
-            for k in range(line_ref.shape[0] // ROWS):
-                pick = jnp.where(lane + ROWS * (first + k) == at[:, s : s + 1], 1.0, 0.0).astype(BF16)
-                rows = line_ref[ROWS * k : ROWS * k + ROWS, :]
-                total = total + jnp.dot(pick, rows, preferred_element_type=F32)
-        out_ref[...] = total.astype(BF16)
+        out_ref[...] = total[128 * s : 128 * s + 128].astype(BF16)
 
 
 def match_kernel(len_hbm, *refs):

time: 81 us -> 80.8 us (level)
  starting transfers between devices: 61.1 us -> 62.5 us
  waiting for transfers between devices: 7.21 us -> 6.36 us
    all_to_all x1, waiting for transfers between devices: 0.85 us -> 0.01 us  [local(): lax.all_to_all(parts.reshape(16, 33, 1, 128), ('zl', 'x'), 0, 0, axis_ind...]
  transfers between devices with their start and end apart: 8 -> 8, of which waited for: 2 -> 1; matrix products, arithmetic and copies ran while one was open for 0% -> 0% of each run, Pallas kernels for 10% -> 9%
where the time goes in v10:
time: 80.8 us; the launch traced here: 80.2 us
  starting transfers between devices  62.5 us (77%)
  Pallas kernels  10.3 us (13%)
  waiting for transfers between devices  6.36 us (8%)
    all_to_all x1, starting transfers between devices, local(): lax.all_to_all(messages.reshape(BLOCK, MSG, 128), ('x', 'y', 'c'), 0, 0,...  21.2 us
    all_to_all x1, starting transfers between devices, local(): lax.all_to_all(parts.reshape(8, 17, 1, 128), 'zh', 0, 0, axis_index_group...  19 us
    ppermute x2, starting transfers between devices, local(): others = [lax.ppermute(other, 'c', [(0, 1), (1, 0)]) for other in others]  8.29 us
    all_to_all x1, waiting for transfers between devices, local(): lax.all_to_all(messages.reshape(BLOCK, MSG, 128), ('x', 'y', 'c'), 0, 0,...  6.31 us
    all_to_all x1, starting transfers between devices, local(): lax.all_to_all(parts.reshape(16, 33, 1, 128), ('zl', 'x'), 0, 0, axis_ind...  5.16 us
    ppermute x1, starting transfers between devices, local(): lax.ppermute(jnp.concatenate([embeddings, partner]), ('y', 'c'), near)  3.98 us
    pallas_call x2, Pallas kernels, local(): pl.pallas_call(functools.partial(member_kernel, of), out_shape=[jax.Shape...  2.86 us
    ppermute x1, starting transfers between devices, local(): lax.ppermute(embeddings, 'y', [(i, i ^ 2) for i in range(4)])  2.66 us
  transfers between devices with their start and end apart: 8, of which 1 were waited for; matrix products, arithmetic and copies ran while one was open for 0% of the time, Pallas kernels for 9%

profile of v10, /device:TPU:1, one launch (start us, length us, event | category | flops | bytes accessed | tf_op | source)
XLA Modules:
  0.0 80.2 jit_solution(2235687460062159681)
XLA Ops:
  0.6 0.0 copy-start
  0.6 2.1 %pack.1 = bf16[4,8,80,128]{3,2,1,0:T(8,128)(2,1)} custom-call(bf16[256,1024]{1,0:T(8,128)(2,1)} %refs_0_.1, s32[2,128]{1,0:T(2,128)} %bitcast.13, s32[2,128]{1,0:T(2,128)} %rows_hbm.1), custom_call_target="tpu_custom_call" | custom-call | flops 1048576 | bytes 1572864 | tf_op jit(solution)/shard_map/pack/pallas_call | solution.py:192
  2.7 21.2 %all-to-all-start = ((bf16[32,80,128]{2,1,0:T(8,128)(2,1)}), bf16[32,80,128]{2,1,0:T(8,128)(2,1)S(1)}, u32[]{:S(2)}, u32[]{:S(2)}) async-start(bf16[32,80,128]{2,1,0:T(8,128)(2,1)} %bitcast.12), calls=%async_computation | async-start | bytes 1310720 | tf_op jit(solution)/shard_map/all_to_all | solution.py:210
  23.9 0.0 copy-done
  23.9 2.3 %collective-permute-start = (bf16[256,1024]{1,0:T(8,128)(2,1)S(1)}, bf16[256,1024]{1,0:T(8,128)(2,1)S(1)}, u32[]{:S(2)}, u32[]{:S(2)}) collective-permute-start(bf16[256,1024]{1,0:T(8,128)(2,1)S(1)} %copy-done), channel_id=1, source_target_pairs={{0,1},{1,0},{2,3},{3,2},{4,5},{5,4},{6,7},{7,6},{8,9},{9,8},{10,11... | collective-permute-start | bytes 1572872 | tf_op jit(solution)/shard_map/ppermute | solution.py:220
  26.2 6.3 %all-to-all-done.msg_ref = bf16[32,80,128]{2,1,0:T(8,128)(2,1)S(1)} async-done(((bf16[32,80,128]{2,1,0:T(8,128)(2,1)}), bf16[32,80,128]{2,1,0:T(8,128)(2,1)S(1)}, u32[]{:S(2)}, u32[]{:S(2)}) %all-to-all-start) | async-done | bytes 655392 | tf_op jit(solution)/shard_map/all_to_all | solution.py:210
  32.5 2.5 %sums.1 = (f32[528,128]{1,0:T(8,128)}, s32[4,128]{1,0:T(4,128)S(1)}) custom-call(s32[1]{0:T(128)} %bitcast.1.from_ref, bf16[32,80,128]{2,1,0:T(8,128)(2,1)S(1)} %all-to-all-done.msg_ref), custom_call_target="tpu_custom_call" | custom-call | flops 2147483648 | bytes 1048576 | tf_op jit(solution)/shard_map/sums/pallas_call | solution.py:211
  35.0 0.0 collective-permute-done
  35.0 5.2 %all-to-all-start.1 = ((f32[16,33,1,128]{3,2,1,0:T(1,128)}), f32[16,33,1,128]{3,2,1,0:T(1,128)S(1)}, u32[]{:S(2)}, u32[]{:S(2)}) async-start(f32[16,33,1,128]{3,2,1,0:T(1,128)} %bitcast.4), calls=%async_computation.1 | async-start | bytes 540672 | tf_op jit(solution)/shard_map/all_to_all | solution.py:228
  40.2 0.1 pad_maximum_fusion
  40.3 4.0 %collective-permute-start.1 = (bf16[512,1024]{1,0:T(8,128)(2,1)S(1)}, bf16[512,1024]{1,0:T(8,128)(2,1)S(1)}, u32[]{:S(2)}, u32[]{:S(2)}) collective-permute-start(bf16[512,1024]{1,0:T(8,128)(2,1)S(1)} %pad_maximum_fusion), channel_id=1, source_target_pairs={{0,2},{1,7},{2,0},{3,5},{4,6},{5,3},{6,4},{7,1},{8,10},{9,15},{10,... | collective-permute-start | bytes 3145736 | tf_op jit(solution)/shard_map/ppermute | solution.py:225
  44.3 2.7 %collective-permute-start.2 = (bf16[256,1024]{1,0:T(8,128)(2,1)S(1)}, bf16[256,1024]{1,0:T(8,128)(2,1)S(1)}, u32[]{:S(2)}, u32[]{:S(2)}) collective-permute-start(bf16[256,1024]{1,0:T(8,128)(2,1)S(1)} %copy-done), channel_id=1, source_target_pairs={{0,4},{2,6},{4,0},{6,2},{1,5},{3,7},{5,1},{7,3},{8,12},{10,14},{12... | collective-permute-start | bytes 1572872 | tf_op jit(solution)/shard_map/ppermute | solution.py:226
  46.9 0.0 all-to-all-done.1
  46.9 0.8 regroup.1.after_ref
  47.7 19.0 %all-to-all-start.2 = ((f32[8,17,1,128]{3,2,1,0:T(1,128)}), f32[8,17,1,128]{3,2,1,0:T(1,128)S(1)}, u32[]{:S(2)}, u32[]{:S(2)}) async-start(f32[8,17,1,128]{3,2,1,0:T(1,128)} %bitcast.6), calls=%async_computation.2 | async-start | bytes 139264 | tf_op jit(solution)/shard_map/all_to_all | solution.py:240
  66.7 0.1 pad_add_fusion.place_ref
  66.8 0.0 collective-permute-done.2.refs_2_
  66.8 0.0 collective-permute-done.1.refs_1_
  66.8 1.4 %members.3 = (bf16[128,1024]{1,0:T(8,128)(2,1)S(1)}, bf16[128,1024]{1,0:T(8,128)(2,1)S(1)}) custom-call(f32[136,128]{1,0:T(8,128)} %regroup.1.after_ref, s32[2]{0:T(128)S(1)} %pad_add_fusion.place_ref, s32[4,128]{1,0:T(4,128)S(1)} %get-tuple-element.15.rows_ref, bf16[256,1024]{1,0:T(8,128)(2,1)S(1)} %copy-done, ...), custom_call_target="tpu_custom_call" | custom-call | tf_op jit(solution)/shard_map/members/pallas_call | solution.py:243
  68.2 6.4 %collective-permute-start.3 = (bf16[128,1024]{1,0:T(8,128)(2,1)S(1)}, bf16[128,1024]{1,0:T(8,128)(2,1)S(1)}, u32[]{:S(2)}, u32[]{:S(2)}) collective-permute-start(bf16[128,1024]{1,0:T(8,128)(2,1)S(1)} %get-tuple-element.20), channel_id=1, source_target_pairs={{0,1},{1,0},{2,3},{3,2},{4,5},{5,4},{6,7},{7,6},{8,9},{9,8},{10,11... | collective-permute-start | bytes 786440 | tf_op jit(solution)/shard_map/ppermute | solution.py:254
  74.6 1.9 %collective-permute-start.4 = (bf16[128,1024]{1,0:T(8,128)(2,1)S(1)}, bf16[128,1024]{1,0:T(8,128)(2,1)S(1)}, u32[]{:S(2)}, u32[]{:S(2)}) collective-permute-start(bf16[128,1024]{1,0:T(8,128)(2,1)S(1)} %get-tuple-element.21), channel_id=1, source_target_pairs={{0,1},{1,0},{2,3},{3,2},{4,5},{5,4},{6,7},{7,6},{8,9},{9,8},{10,11... | collective-permute-start | bytes 786440 | tf_op jit(solution)/shard_map/ppermute | solution.py:254
  76.5 1.4 %members.2 = (bf16[128,1024]{1,0:T(8,128)(2,1)S(1)}, bf16[128,1024]{1,0:T(8,128)(2,1)S(1)}) custom-call(f32[136,128]{1,0:T(8,128)} %regroup.1.after_ref, s32[2]{0:T(128)S(1)} %pad_add_fusion.place_ref, s32[4,128]{1,0:T(4,128)S(1)} %get-tuple-element.15.rows_ref, bf16[256,1024]{1,0:T(8,128)(2,1)S(1)} %copy-done, ...), custom_call_target="tpu_custom_call" | custom-call | tf_op jit(solution)/shard_map/members/pallas_call | solution.py:243
  78.0 0.0 copy-start.1
  78.0 0.0 collective-permute-done.3.refs_2_
  78.0 0.0 collective-permute-done.4.refs_3_
  78.0 1.4 %match.1 = f32[2,128]{1,0:T(2,128)} custom-call(s32[2]{0:T(128)} %len_hbm.1, bf16[128,1024]{1,0:T(8,128)(2,1)S(1)} %get-tuple-element.18.refs_0_, bf16[128,1024]{1,0:T(8,128)(2,1)S(1)} %get-tuple-element.19.refs_1_, bf16[128,1024]{1,0:T(8,128)(2,1)S(1)} %collective-permute-done.3.refs_2_, bf16[128,1024]{1,0:T(8,128)(2,1)S(1)} %collective-permute-done.4.refs_3_), custom_call_target="tpu_custom_call" | custom-call | tf_op jit(solution)/shard_map/match/pallas_call | solution.py:255
  79.5 0.0 all-to-all-done.2
  79.5 0.0 copy-done.1
  79.5 0.7 finish.1
Async XLA Ops:
  0.6 23.3 %copy-start = (bf16[256,1024]{1,0:T(8,128)(2,1)S(1)}, bf16[256,1024]{1,0:T(8,128)(2,1)}, u32[]{:S(2)}) copy-start(bf16[256,1024]{1,0:T(8,128)(2,1)} %refs_0_.1) | copy-start | bytes 1572868
  2.7 29.8 %all-to-all-start = ((bf16[32,80,128]{2,1,0:T(8,128)(2,1)}), bf16[32,80,128]{2,1,0:T(8,128)(2,1)S(1)}, u32[]{:S(2)}, u32[]{:S(2)}) async-start(bf16[32,80,128]{2,1,0:T(8,128)(2,1)} %bitcast.12), calls=%async_computation | async-start | bytes 1310720 | tf_op jit(solution)/shard_map/all_to_all | solution.py:210
  23.9 11.1 %collective-permute-start = (bf16[256,1024]{1,0:T(8,128)(2,1)S(1)}, bf16[256,1024]{1,0:T(8,128)(2,1)S(1)}, u32[]{:S(2)}, u32[]{:S(2)}) collective-permute-start(bf16[256,1024]{1,0:T(8,128)(2,1)S(1)} %copy-done), channel_id=1, source_target_pairs={{0,1},{1,0},{2,3},{3,2},{4,5},{5,4},{6,7},{7,6},{8,9},{9,8},{10,11... | collective-permute-start | bytes 1572872 | tf_op jit(solution)/shard_map/ppermute | solution.py:220
  35.0 11.9 %all-to-all-start.1 = ((f32[16,33,1,128]{3,2,1,0:T(1,128)}), f32[16,33,1,128]{3,2,1,0:T(1,128)S(1)}, u32[]{:S(2)}, u32[]{:S(2)}) async-start(f32[16,33,1,128]{3,2,1,0:T(1,128)} %bitcast.4), calls=%async_computation.1 | async-start | bytes 540672 | tf_op jit(solution)/shard_map/all_to_all | solution.py:228
  40.3 26.5 %collective-permute-start.1 = (bf16[512,1024]{1,0:T(8,128)(2,1)S(1)}, bf16[512,1024]{1,0:T(8,128)(2,1)S(1)}, u32[]{:S(2)}, u32[]{:S(2)}) collective-permute-start(bf16[512,1024]{1,0:T(8,128)(2,1)S(1)} %pad_maximum_fusion), channel_id=1, source_target_pairs={{0,2},{1,7},{2,0},{3,5},{4,6},{5,3},{6,4},{7,1},{8,10},{9,15},{10,... | collective-permute-start | bytes 3145736 | tf_op jit(solution)/shard_map/ppermute | solution.py:225
  44.3 22.5 %collective-permute-start.2 = (bf16[256,1024]{1,0:T(8,128)(2,1)S(1)}, bf16[256,1024]{1,0:T(8,128)(2,1)S(1)}, u32[]{:S(2)}, u32[]{:S(2)}) collective-permute-start(bf16[256,1024]{1,0:T(8,128)(2,1)S(1)} %copy-done), channel_id=1, source_target_pairs={{0,4},{2,6},{4,0},{6,2},{1,5},{3,7},{5,1},{7,3},{8,12},{10,14},{12... | collective-permute-start | bytes 1572872 | tf_op jit(solution)/shard_map/ppermute | solution.py:226
  47.7 31.8 %all-to-all-start.2 = ((f32[8,17,1,128]{3,2,1,0:T(1,128)}), f32[8,17,1,128]{3,2,1,0:T(1,128)S(1)}, u32[]{:S(2)}, u32[]{:S(2)}) async-start(f32[8,17,1,128]{3,2,1,0:T(1,128)} %bitcast.6), calls=%async_computation.2 | async-start | bytes 139264 | tf_op jit(solution)/shard_map/all_to_all | solution.py:240
  68.2 9.8 %collective-permute-start.3 = (bf16[128,1024]{1,0:T(8,128)(2,1)S(1)}, bf16[128,1024]{1,0:T(8,128)(2,1)S(1)}, u32[]{:S(2)}, u32[]{:S(2)}) collective-permute-start(bf16[128,1024]{1,0:T(8,128)(2,1)S(1)} %get-tuple-element.20), channel_id=1, source_target_pairs={{0,1},{1,0},{2,3},{3,2},{4,5},{5,4},{6,7},{7,6},{8,9},{9,8},{10,11... | collective-permute-start | bytes 786440 | tf_op jit(solution)/shard_map/ppermute | solution.py:254
  74.6 3.4 %collective-permute-start.4 = (bf16[128,1024]{1,0:T(8,128)(2,1)S(1)}, bf16[128,1024]{1,0:T(8,128)(2,1)S(1)}, u32[]{:S(2)}, u32[]{:S(2)}) collective-permute-start(bf16[128,1024]{1,0:T(8,128)(2,1)S(1)} %get-tuple-element.21), channel_id=1, source_target_pairs={{0,1},{1,0},{2,3},{3,2},{4,5},{5,4},{6,7},{7,6},{8,9},{9,8},{10,11... | collective-permute-start | bytes 786440 | tf_op jit(solution)/shard_map/ppermute | solution.py:254
  78.0 1.5 %copy-start.1 = (f32[16,128]{1,0:T(8,128)S(1)}, f32[16,128]{1,0:T(8,128)}, u32[]{:S(2)}) copy-start(f32[16,128]{1,0:T(8,128)} %old_ref.1) | copy-start | bytes 24580

commit v11 on v10

--- a/solution.py
+++ b/solution.py
@@ -77,9 +77,8 @@
     one, zero = jnp.ones((), BF16), jnp.zeros((), BF16)
     contract = (((1,), (1,)), ((), ()))
     sums = jnp.zeros((256, 256), F32)
-    counts = jnp.zeros((16, 128), F32)
     for first in range(0, BLOCK, 4):
-        a, b, p, q = [], [], [], []
+        a, b = [], []
         for s in range(first, first + 4):
             codes = msg_ref[s, 64:80, :]
             for t in range(2):
@@ -87,13 +86,18 @@
                 part = msg_ref[s, 32 * t : 32 * t + 32, :]
                 a.append(jnp.where(cluster == high, one, zero))
                 b.append(jnp.concatenate([jnp.where(low == jnp.asarray(g, BF16), part, zero) for g in range(8)], 0))
-                h, g = high.astype(F32).astype(I32), low.astype(F32).astype(I32)
-                within = ((h >> 1) & 7) * 16 + (g & 3) * 4 + (g >> 2) * 2 + (h & 1)
-                p.append(jnp.where(cluster[0:16] == (h >> 4).astype(F32).astype(BF16), one, zero))
-                q.append(jnp.where(cluster[0:128] == within.astype(F32).astype(BF16), one, zero))
-        a, b, p, q = (jnp.concatenate(blocks, 1) for blocks in (a, b, p, q))
+        a, b = (jnp.concatenate(blocks, 1) for blocks in (a, b))
         sums = sums + lax.dot_general(a, b, contract, preferred_element_type=F32)
-        counts = counts + lax.dot_general(p, q, contract, preferred_element_type=F32)
+    p, q = [], []
+    for k in range(8):
+        codes = msg_ref[(from_ref[0] & 24) + k, 64:80, :].astype(F32).astype(I32)
+        for t in range(2):
+            high, low = codes[t : t + 1], codes[2 + t : 3 + t]
+            within = ((high >> 1) & 7) * 16 + (low & 3) * 4 + (low >> 2) * 2 + (high & 1)
+            p.append(jnp.where(cluster[0:16] == (high >> 4).astype(F32).astype(BF16), one, zero))
+            q.append(jnp.where(cluster[0:128] == within.astype(F32).astype(BF16), one, zero))
+    p, q = (jnp.concatenate(blocks, 1) for blocks in (p, q))
+    counts = lax.dot_general(p, q, contract, preferred_element_type=F32)
     for m in range(16):
         at = 33 * PLANE_ORDER[m]
         out_ref[at : at + 16, :] = sums[16 * m : 16 * m + 16, 0:128]
@@ -110,8 +114,9 @@
     for x in range(4):
         first, *others = (in_ref[33 * at : 33 * at + 32, :] for at in range(x ^ PLANE_FIRST[1], 16, 4))
         parts.append((first + others[0]) + (others[1] + others[2]))
-    first, *others = (in_ref[33 * 4 * zl + 32 : 33 * 4 * zl + 33, :] for zl in range(4))
-    counts = (first + others[0]) + (others[1] + others[2])
+    counts = in_ref[32:33, :]
+    for k in range(1, 16):
+        counts = counts + in_ref[33 * k + 32 : 33 * k + 33, :]
     for low in range(4):
         rows = jnp.zeros((32, 128), F32)
         for x in range(4):

time: 80.8 us -> 80.3 us (level)
  no operation moved by 1% of the time
where the time goes in v11:
time: 80.3 us; the launch traced here: 79.8 us
  starting transfers between devices  62.5 us (78%)
  Pallas kernels  9.93 us (12%)
  waiting for transfers between devices  6.36 us (8%)
    all_to_all x1, starting transfers between devices, local(): lax.all_to_all(messages.reshape(BLOCK, MSG, 128), ('x', 'y', 'c'), 0, 0,...  21.2 us
    all_to_all x1, starting transfers between devices, local(): lax.all_to_all(parts.reshape(8, 17, 1, 128), 'zh', 0, 0, axis_index_group...  19 us
    ppermute x2, starting transfers between devices, local(): others = [lax.ppermute(other, 'c', [(0, 1), (1, 0)]) for other in others]  8.29 us
    all_to_all x1, waiting for transfers between devices, local(): lax.all_to_all(messages.reshape(BLOCK, MSG, 128), ('x', 'y', 'c'), 0, 0,...  6.31 us
    all_to_all x1, starting transfers between devices, local(): lax.all_to_all(parts.reshape(16, 33, 1, 128), ('zl', 'x'), 0, 0, axis_ind...  5.16 us
    ppermute x1, starting transfers between devices, local(): lax.ppermute(jnp.concatenate([embeddings, partner]), ('y', 'c'), near)  3.98 us
    pallas_call x2, Pallas kernels, local(): pl.pallas_call(functools.partial(member_kernel, of), out_shape=[jax.Shape...  2.86 us
    ppermute x1, starting transfers between devices, local(): lax.ppermute(embeddings, 'y', [(i, i ^ 2) for i in range(4)])  2.66 us
  transfers between devices with their start and end apart: 8, of which 1 were waited for; matrix products, arithmetic and copies ran while one was open for 0% of the time, Pallas kernels for 9%

profile of v11, /device:TPU:1, one launch (start us, length us, event | category | flops | bytes accessed | tf_op | source)
XLA Modules:
  0.0 79.8 jit_solution(8453207506489037718)
XLA Ops:
  0.6 0.0 copy-start
  0.6 2.1 %pack.1 = bf16[4,8,80,128]{3,2,1,0:T(8,128)(2,1)} custom-call(bf16[256,1024]{1,0:T(8,128)(2,1)} %refs_0_.1, s32[2,128]{1,0:T(2,128)} %bitcast.13, s32[2,128]{1,0:T(2,128)} %rows_hbm.1), custom_call_target="tpu_custom_call" | custom-call | flops 1048576 | bytes 1572864 | tf_op jit(solution)/shard_map/pack/pallas_call | solution.py:197
  2.7 21.2 %all-to-all-start = ((bf16[32,80,128]{2,1,0:T(8,128)(2,1)}), bf16[32,80,128]{2,1,0:T(8,128)(2,1)S(1)}, u32[]{:S(2)}, u32[]{:S(2)}) async-start(bf16[32,80,128]{2,1,0:T(8,128)(2,1)} %bitcast.12), calls=%async_computation | async-start | bytes 1310720 | tf_op jit(solution)/shard_map/all_to_all | solution.py:215
  23.9 0.0 copy-done
  23.9 2.3 %collective-permute-start = (bf16[256,1024]{1,0:T(8,128)(2,1)S(1)}, bf16[256,1024]{1,0:T(8,128)(2,1)S(1)}, u32[]{:S(2)}, u32[]{:S(2)}) collective-permute-start(bf16[256,1024]{1,0:T(8,128)(2,1)S(1)} %copy-done), channel_id=1, source_target_pairs={{0,1},{1,0},{2,3},{3,2},{4,5},{5,4},{6,7},{7,6},{8,9},{9,8},{10,11... | collective-permute-start | bytes 1572872 | tf_op jit(solution)/shard_map/ppermute | solution.py:225
  26.2 6.3 %all-to-all-done.msg_ref = bf16[32,80,128]{2,1,0:T(8,128)(2,1)S(1)} async-done(((bf16[32,80,128]{2,1,0:T(8,128)(2,1)}), bf16[32,80,128]{2,1,0:T(8,128)(2,1)S(1)}, u32[]{:S(2)}, u32[]{:S(2)}) %all-to-all-start) | async-done | bytes 655392 | tf_op jit(solution)/shard_map/all_to_all | solution.py:215
  32.5 2.1 %sums.1 = (f32[528,128]{1,0:T(8,128)}, s32[4,128]{1,0:T(4,128)S(1)}) custom-call(s32[1]{0:T(128)} %bitcast.1.from_ref, bf16[32,80,128]{2,1,0:T(8,128)(2,1)S(1)} %all-to-all-done.msg_ref), custom_call_target="tpu_custom_call" | custom-call | flops 2147483648 | bytes 1048576 | tf_op jit(solution)/shard_map/sums/pallas_call | solution.py:216
  34.6 0.0 collective-permute-done
  34.6 5.2 %all-to-all-start.1 = ((f32[16,33,1,128]{3,2,1,0:T(1,128)}), f32[16,33,1,128]{3,2,1,0:T(1,128)S(1)}, u32[]{:S(2)}, u32[]{:S(2)}) async-start(f32[16,33,1,128]{3,2,1,0:T(1,128)} %bitcast.4), calls=%async_computation.1 | async-start | bytes 540672 | tf_op jit(solution)/shard_map/all_to_all | solution.py:233
  39.8 0.1 pad_maximum_fusion
  39.9 4.0 %collective-permute-start.1 = (bf16[512,1024]{1,0:T(8,128)(2,1)S(1)}, bf16[512,1024]{1,0:T(8,128)(2,1)S(1)}, u32[]{:S(2)}, u32[]{:S(2)}) collective-permute-start(bf16[512,1024]{1,0:T(8,128)(2,1)S(1)} %pad_maximum_fusion), channel_id=1, source_target_pairs={{0,2},{1,7},{2,0},{3,5},{4,6},{5,3},{6,4},{7,1},{8,10},{9,15},{10,... | collective-permute-start | bytes 3145736 | tf_op jit(solution)/shard_map/ppermute | solution.py:230
  43.9 2.7 %collective-permute-start.2 = (bf16[256,1024]{1,0:T(8,128)(2,1)S(1)}, bf16[256,1024]{1,0:T(8,128)(2,1)S(1)}, u32[]{:S(2)}, u32[]{:S(2)}) collective-permute-start(bf16[256,1024]{1,0:T(8,128)(2,1)S(1)} %copy-done), channel_id=1, source_target_pairs={{0,4},{2,6},{4,0},{6,2},{1,5},{3,7},{5,1},{7,3},{8,12},{10,14},{12... | collective-permute-start | bytes 1572872 | tf_op jit(solution)/shard_map/ppermute | solution.py:231
  46.5 0.0 all-to-all-done.1
  46.5 0.8 regroup.1.after_ref
  47.3 19.0 %all-to-all-start.2 = ((f32[8,17,1,128]{3,2,1,0:T(1,128)}), f32[8,17,1,128]{3,2,1,0:T(1,128)S(1)}, u32[]{:S(2)}, u32[]{:S(2)}) async-start(f32[8,17,1,128]{3,2,1,0:T(1,128)} %bitcast.6), calls=%async_computation.2 | async-start | bytes 139264 | tf_op jit(solution)/shard_map/all_to_all | solution.py:245
  66.3 0.1 pad_add_fusion.place_ref
  66.4 0.0 collective-permute-done.2.refs_2_
  66.4 0.0 collective-permute-done.1.refs_1_
  66.4 1.4 %members.3 = (bf16[128,1024]{1,0:T(8,128)(2,1)S(1)}, bf16[128,1024]{1,0:T(8,128)(2,1)S(1)}) custom-call(f32[136,128]{1,0:T(8,128)} %regroup.1.after_ref, s32[2]{0:T(128)S(1)} %pad_add_fusion.place_ref, s32[4,128]{1,0:T(4,128)S(1)} %get-tuple-element.15.rows_ref, bf16[256,1024]{1,0:T(8,128)(2,1)S(1)} %copy-done, ...), custom_call_target="tpu_custom_call" | custom-call | tf_op jit(solution)/shard_map/members/pallas_call | solution.py:248
  67.8 6.4 %collective-permute-start.3 = (bf16[128,1024]{1,0:T(8,128)(2,1)S(1)}, bf16[128,1024]{1,0:T(8,128)(2,1)S(1)}, u32[]{:S(2)}, u32[]{:S(2)}) collective-permute-start(bf16[128,1024]{1,0:T(8,128)(2,1)S(1)} %get-tuple-element.20), channel_id=1, source_target_pairs={{0,1},{1,0},{2,3},{3,2},{4,5},{5,4},{6,7},{7,6},{8,9},{9,8},{10,11... | collective-permute-start | bytes 786440 | tf_op jit(solution)/shard_map/ppermute | solution.py:259
  74.2 1.9 %collective-permute-start.4 = (bf16[128,1024]{1,0:T(8,128)(2,1)S(1)}, bf16[128,1024]{1,0:T(8,128)(2,1)S(1)}, u32[]{:S(2)}, u32[]{:S(2)}) collective-permute-start(bf16[128,1024]{1,0:T(8,128)(2,1)S(1)} %get-tuple-element.21), channel_id=1, source_target_pairs={{0,1},{1,0},{2,3},{3,2},{4,5},{5,4},{6,7},{7,6},{8,9},{9,8},{10,11... | collective-permute-start | bytes 786440 | tf_op jit(solution)/shard_map/ppermute | solution.py:259
  76.1 1.4 %members.2 = (bf16[128,1024]{1,0:T(8,128)(2,1)S(1)}, bf16[128,1024]{1,0:T(8,128)(2,1)S(1)}) custom-call(f32[136,128]{1,0:T(8,128)} %regroup.1.after_ref, s32[2]{0:T(128)S(1)} %pad_add_fusion.place_ref, s32[4,128]{1,0:T(4,128)S(1)} %get-tuple-element.15.rows_ref, bf16[256,1024]{1,0:T(8,128)(2,1)S(1)} %copy-done, ...), custom_call_target="tpu_custom_call" | custom-call | tf_op jit(solution)/shard_map/members/pallas_call | solution.py:248
  77.6 0.0 copy-start.1
  77.6 0.0 collective-permute-done.3.refs_2_
  77.6 0.0 collective-permute-done.4.refs_3_
  77.6 1.4 %match.1 = f32[2,128]{1,0:T(2,128)} custom-call(s32[2]{0:T(128)} %len_hbm.1, bf16[128,1024]{1,0:T(8,128)(2,1)S(1)} %get-tuple-element.18.refs_0_, bf16[128,1024]{1,0:T(8,128)(2,1)S(1)} %get-tuple-element.19.refs_1_, bf16[128,1024]{1,0:T(8,128)(2,1)S(1)} %collective-permute-done.3.refs_2_, bf16[128,1024]{1,0:T(8,128)(2,1)S(1)} %collective-permute-done.4.refs_3_), custom_call_target="tpu_custom_call" | custom-call | tf_op jit(solution)/shard_map/match/pallas_call | solution.py:260
  79.1 0.0 all-to-all-done.2
  79.1 0.0 copy-done.1
  79.1 0.7 finish.1
Async XLA Ops:
  0.6 23.3 %copy-start = (bf16[256,1024]{1,0:T(8,128)(2,1)S(1)}, bf16[256,1024]{1,0:T(8,128)(2,1)}, u32[]{:S(2)}) copy-start(bf16[256,1024]{1,0:T(8,128)(2,1)} %refs_0_.1) | copy-start | bytes 1572868
  2.7 29.8 %all-to-all-start = ((bf16[32,80,128]{2,1,0:T(8,128)(2,1)}), bf16[32,80,128]{2,1,0:T(8,128)(2,1)S(1)}, u32[]{:S(2)}, u32[]{:S(2)}) async-start(bf16[32,80,128]{2,1,0:T(8,128)(2,1)} %bitcast.12), calls=%async_computation | async-start | bytes 1310720 | tf_op jit(solution)/shard_map/all_to_all | solution.py:215
  23.9 10.7 %collective-permute-start = (bf16[256,1024]{1,0:T(8,128)(2,1)S(1)}, bf16[256,1024]{1,0:T(8,128)(2,1)S(1)}, u32[]{:S(2)}, u32[]{:S(2)}) collective-permute-start(bf16[256,1024]{1,0:T(8,128)(2,1)S(1)} %copy-done), channel_id=1, source_target_pairs={{0,1},{1,0},{2,3},{3,2},{4,5},{5,4},{6,7},{7,6},{8,9},{9,8},{10,11... | collective-permute-start | bytes 1572872 | tf_op jit(solution)/shard_map/ppermute | solution.py:225
  34.6 11.9 %all-to-all-start.1 = ((f32[16,33,1,128]{3,2,1,0:T(1,128)}), f32[16,33,1,128]{3,2,1,0:T(1,128)S(1)}, u32[]{:S(2)}, u32[]{:S(2)}) async-start(f32[16,33,1,128]{3,2,1,0:T(1,128)} %bitcast.4), calls=%async_computation.1 | async-start | bytes 540672 | tf_op jit(solution)/shard_map/all_to_all | solution.py:233
  39.9 26.5 %collective-permute-start.1 = (bf16[512,1024]{1,0:T(8,128)(2,1)S(1)}, bf16[512,1024]{1,0:T(8,128)(2,1)S(1)}, u32[]{:S(2)}, u32[]{:S(2)}) collective-permute-start(bf16[512,1024]{1,0:T(8,128)(2,1)S(1)} %pad_maximum_fusion), channel_id=1, source_target_pairs={{0,2},{1,7},{2,0},{3,5},{4,6},{5,3},{6,4},{7,1},{8,10},{9,15},{10,... | collective-permute-start | bytes 3145736 | tf_op jit(solution)/shard_map/ppermute | solution.py:230
  43.9 22.5 %collective-permute-start.2 = (bf16[256,1024]{1,0:T(8,128)(2,1)S(1)}, bf16[256,1024]{1,0:T(8,128)(2,1)S(1)}, u32[]{:S(2)}, u32[]{:S(2)}) collective-permute-start(bf16[256,1024]{1,0:T(8,128)(2,1)S(1)} %copy-done), channel_id=1, source_target_pairs={{0,4},{2,6},{4,0},{6,2},{1,5},{3,7},{5,1},{7,3},{8,12},{10,14},{12... | collective-permute-start | bytes 1572872 | tf_op jit(solution)/shard_map/ppermute | solution.py:231
  47.3 31.8 %all-to-all-start.2 = ((f32[8,17,1,128]{3,2,1,0:T(1,128)}), f32[8,17,1,128]{3,2,1,0:T(1,128)S(1)}, u32[]{:S(2)}, u32[]{:S(2)}) async-start(f32[8,17,1,128]{3,2,1,0:T(1,128)} %bitcast.6), calls=%async_computation.2 | async-start | bytes 139264 | tf_op jit(solution)/shard_map/all_to_all | solution.py:245
  67.8 9.8 %collective-permute-start.3 = (bf16[128,1024]{1,0:T(8,128)(2,1)S(1)}, bf16[128,1024]{1,0:T(8,128)(2,1)S(1)}, u32[]{:S(2)}, u32[]{:S(2)}) collective-permute-start(bf16[128,1024]{1,0:T(8,128)(2,1)S(1)} %get-tuple-element.20), channel_id=1, source_target_pairs={{0,1},{1,0},{2,3},{3,2},{4,5},{5,4},{6,7},{7,6},{8,9},{9,8},{10,11... | collective-permute-start | bytes 786440 | tf_op jit(solution)/shard_map/ppermute | solution.py:259
  74.2 3.4 %collective-permute-start.4 = (bf16[128,1024]{1,0:T(8,128)(2,1)S(1)}, bf16[128,1024]{1,0:T(8,128)(2,1)S(1)}, u32[]{:S(2)}, u32[]{:S(2)}) collective-permute-start(bf16[128,1024]{1,0:T(8,128)(2,1)S(1)} %get-tuple-element.21), channel_id=1, source_target_pairs={{0,1},{1,0},{2,3},{3,2},{4,5},{5,4},{6,7},{7,6},{8,9},{9,8},{10,11... | collective-permute-start | bytes 786440 | tf_op jit(solution)/shard_map/ppermute | solution.py:259
  77.6 1.5 %copy-start.1 = (f32[16,128]{1,0:T(8,128)S(1)}, f32[16,128]{1,0:T(8,128)}, u32[]{:S(2)}) copy-start(f32[16,128]{1,0:T(8,128)} %old_ref.1) | copy-start | bytes 24580

commit v12 on v11

--- a/solution.py
+++ b/solution.py
@@ -1,5 +1,3 @@
-import functools
-
 import jax
 import jax.numpy as jnp
 from jax import lax
@@ -31,10 +29,11 @@
     return pl.CostEstimate(flops=flops, bytes_accessed=moved, transcendentals=0)
 
 
-def pack_kernel(emb_hbm, label_hbm, rows_hbm, out_hbm, emb_ref, label_ref, rows_ref, msg_ref, in_sems, out_sems, sems):
+def pack_kernel(emb_hbm, label_hbm, rows_hbm, len_hbm, out_hbm, emb_ref, label_ref, rows_ref, len_ref, msg_ref, in_sems, out_sems, sems):
     small = [
         pltpu.make_async_copy(label_hbm, label_ref, sems.at[0]),
         pltpu.make_async_copy(rows_hbm, rows_ref, sems.at[1]),
+        pltpu.make_async_copy(len_hbm, len_ref, sems.at[2]),
     ]
     halves = [pl.ds(0, 512), pl.ds(512, 512)]
     blocks = [pltpu.make_async_copy(emb_hbm.at[:, at], emb_ref.at[:, at], in_sems.at[k]) for k, at in enumerate(halves)]
@@ -50,6 +49,8 @@
     for k, pair in enumerate((high, low, r >> 3, r & 7)):
         codes = jnp.where(row == 2 * k, pair[0:1], codes)
         codes = jnp.where(row == 2 * k + 1, pair[1:2], codes)
+    for k in range(2):
+        codes = jnp.where(row == 8 + k, len_ref[k], codes)
     codes = codes.astype(F32).astype(BF16)
     sent = []
     for k in range(2):
@@ -72,7 +73,7 @@
     return lax.broadcasted_iota(I32, (n, 128), 0).astype(F32).astype(BF16)
 
 
-def sum_kernel(from_ref, msg_ref, out_ref, rows_ref):
+def sum_kernel(from_ref, msg_ref, out_ref, rows_ref, len_ref):
     cluster = lanes(256)
     one, zero = jnp.ones((), BF16), jnp.zeros((), BF16)
     contract = (((1,), (1,)), ((), ()))
@@ -106,6 +107,8 @@
     for k in range(2):
         codes = msg_ref[from_ref[0] ^ k, 64:80, :].astype(F32).astype(I32)
         rows_ref[2 * k : 2 * k + 2, :] = codes[4:6] * 8 + codes[6:8]
+        if k == 0:
+            len_ref[...] = codes[8:10]
 
 
 def regroup_kernel(in_ref, out_ref, s_ref):
@@ -144,46 +147,38 @@
     out_ref[...] = (sums + old_ref[...]) / (counts + 1.0)
 
 
-def member_kernel(of, after_ref, place_ref, rows_ref, *refs):
-    line_refs, out_refs = refs[:3], refs[3:]
+def member_kernel(after_ref, place_ref, rows_ref, *refs):
+    line_refs, (own_ref, *other_refs) = refs[:3], refs[3:]
     core, y = place_ref[0], place_ref[1]
-    r = rows_ref[2 * of : 2 * of + 2, :]
+    r = rows_ref[...]
     away, far = (r >> 9) ^ y, ((r >> 8) & 1) ^ core
     block = jnp.where(away == 1 + 2 * core, 1 + far, jnp.where(far == 1, -1, jnp.where(away == 0, 0, jnp.where(away == 2, 3, -1))))
     at = jnp.where(block < 0, -1, (block << 8) + (r & 255))
-    at = jnp.concatenate([at, jnp.zeros((6, 128), I32)], 0).astype(F32).T.astype(I32)
-    at = jnp.concatenate([at[:, 0:1], at[:, 1:2]], 0)
-    lane = lax.broadcasted_iota(I32, (256, ROWS), 1)
-    total = jnp.zeros((256, 1024), F32)
-    for first, line_ref in zip((0, 1, 3), line_refs):
-        for k in range(line_ref.shape[0] // ROWS):
-            pick = jnp.where(lane + ROWS * (first + k) == at, 1.0, 0.0).astype(BF16)
-            rows = line_ref[ROWS * k : ROWS * k + ROWS, :]
-            total = total + jnp.dot(pick, rows, preferred_element_type=F32)
-    for s, out_ref in enumerate(out_refs):
-        out_ref[...] = total[128 * s : 128 * s + 128].astype(BF16)
-
-
-def match_kernel(len_hbm, *refs):
+    at = jnp.concatenate([at, jnp.zeros((4, 128), I32)], 0).astype(F32).T.astype(I32)
+    at = jnp.concatenate([at[:, s : s + 1] for s in range(4)], 0)
+    lane = lax.broadcasted_iota(I32, (512, ROWS), 1)
+    picks = [jnp.where(lane + ROWS * k == at, 1.0, 0.0).astype(BF16) for k in range(4)]
+    for n in range(0, 1024, 256):
+        blocks = [line_ref[k : k + ROWS, n : n + 256] for line_ref in line_refs for k in range(0, line_ref.shape[0], ROWS)]
+        total = sum(jnp.dot(pick, block, preferred_element_type=F32) for pick, block in zip(picks, blocks)).astype(BF16)
+        own_ref[:, n : n + 256] = total[0:256]
+        for s in range(2):
+            other_refs[s][:, n : n + 256] = total[256 + 128 * s : 384 + 128 * s]
+
+
+def match_kernel(len_ref, own_ref, *refs):
+    *other_refs, out_ref = refs
     i = lax.broadcasted_iota(I32, (128, 128), 0)
     j = lax.broadcasted_iota(I32, (128, 128), 1)
-    own_refs, other_refs, (out_ref, len_ref, sem) = refs[0:2], refs[2:4], refs[4:7]
-    lengths = pltpu.make_async_copy(len_hbm, len_ref, sem)
-    lengths.start()
-    i = lax.broadcasted_iota(I32, (128, 128), 0)
-    j = lax.broadcasted_iota(I32, (128, 128), 1)
-    cosines = []
     for s in range(2):
-        one = own_refs[s][...] + other_refs[s][...]
+        one = own_ref[128 * s : 128 * s + 128, :] + other_refs[s][...]
         gram = lax.dot_general(one, one, (((1,), (1,)), ((), ())), preferred_element_type=F32)
         diagonal = jnp.where(i == j, gram, 0.0)
         down = lax.rsqrt(jnp.sum(diagonal, axis=1, keepdims=True) + 1e-06)
         across = lax.rsqrt(jnp.sum(diagonal, axis=0, keepdims=True) + 1e-06)
-        cosines.append(gram * down * across)
-    lengths.wait()
-    for s in range(2):
-        length = len_ref[s]
-        largest = jnp.max(jnp.where((i < length) & (i != j), cosines[s], -2.0), axis=0, keepdims=True)
+        cosine = gram * down * across
+        length = len_ref[s : s + 1, :]
+        largest = jnp.max(jnp.where((i < length) & (i != j), cosine, -2.0), axis=0, keepdims=True)
         out_ref[s : s + 1, :] = jnp.where(j[0:1] < length, largest, 0.0)
 
 
@@ -197,27 +192,28 @@
     messages = pl.pallas_call(
         pack_kernel,
         out_shape=pltpu.HBM((4, 8, MSG, 128), BF16),
-        in_specs=[HBM] * 3,
+        in_specs=[HBM] * 4,
         out_specs=HBM,
         scratch_shapes=[
             pltpu.VMEM((ROWS, 1024), BF16),
             pltpu.VMEM((2, 128), I32),
             pltpu.VMEM((2, 128), I32),
+            pltpu.SMEM((2,), I32),
             pltpu.VMEM((4, 8, MSG, 128), BF16),
             pltpu.SemaphoreType.DMA((2,)),
             pltpu.SemaphoreType.DMA((2,)),
-            pltpu.SemaphoreType.DMA((2,)),
+            pltpu.SemaphoreType.DMA((3,)),
         ],
         compiler_params=params(8),
         cost_estimate=cost(1 << 20, 3 << 19),
         name="pack",
-    )(*(pltpu.with_memory_space_constraint(a, pltpu.HBM) for a in (embeddings, assignments.reshape(2, 128), slab_rows)))
+    )(*(pltpu.with_memory_space_constraint(a, pltpu.HBM) for a in (embeddings, assignments.reshape(2, 128), slab_rows, slab_len)))
     messages = lax.all_to_all(messages.reshape(BLOCK, MSG, 128), ("x", "y", "c"), 0, 0, axis_index_groups=[BLOCK_ORDER], tiled=True)
-    parts, rows = pl.pallas_call(
+    parts, rows, lengths = pl.pallas_call(
         sum_kernel,
-        out_shape=(pltpu.VMEM((528, 128), F32), pltpu.VMEM((4, 128), I32)),
+        out_shape=(pltpu.VMEM((528, 128), F32), pltpu.VMEM((4, 128), I32), pltpu.VMEM((2, 128), I32)),
         in_specs=[SMEM, VMEM],
-        out_specs=(VMEM, VMEM),
+        out_specs=(VMEM, VMEM, VMEM),
         compiler_params=params(20),
         cost_estimate=cost(1 << 31, 1 << 20),
         name="sums",
@@ -244,29 +240,25 @@
     after = parts
     parts = lax.all_to_all(parts.reshape(8, 17, 1, 128), "zh", 0, 0, axis_index_groups=[RING_ORDER], tiled=True)
     place = jnp.stack([core, y])
-    own, others = (
-        pl.pallas_call(
-            functools.partial(member_kernel, of),
-            out_shape=[jax.ShapeDtypeStruct((128, 1024), BF16)] * 2,
-            in_specs=[pl.BlockSpec(memory_space=pl.ANY), SMEM] + [VMEM] * 4,
-            out_specs=[VMEM] * 2,
-            compiler_params=params(16),
-            cost_estimate=cost(0, 0),
-            name="members",
-        )(after, place, rows, *line)
-        for of in range(2)
-    )
+    own, *others = pl.pallas_call(
+        member_kernel,
+        out_shape=[jax.ShapeDtypeStruct((n, 1024), BF16) for n in (256, 128, 128)],
+        in_specs=[pl.BlockSpec(memory_space=pl.ANY), SMEM] + [VMEM] * 4,
+        out_specs=[VMEM] * 3,
+        compiler_params=params(16),
+        cost_estimate=cost(0, 0),
+        name="members",
+    )(after, place, rows, *line)
     others = [lax.ppermute(other, "c", [(0, 1), (1, 0)]) for other in others]
     best_cosine = pl.pallas_call(
         match_kernel,
         out_shape=jax.ShapeDtypeStruct((2, 128), F32),
-        in_specs=[HBM] + [VMEM] * 4,
+        in_specs=[VMEM] * 4,
         out_specs=VMEM,
-        scratch_shapes=[pltpu.SMEM((2,), I32), pltpu.SemaphoreType.DMA],
         compiler_params=params(8),
         cost_estimate=cost(0, 0),
         name="match",
-    )(pltpu.with_memory_space_constraint(slab_len, pltpu.HBM), *own, *others)
+    )(lengths, own, *others)
     parts, best_cosine = lax.optimization_barrier((parts, best_cosine))
     centroids = pl.pallas_call(
         finish_kernel,

time: 80.3 us -> 81.7 us (1.017)
  waiting for transfers between devices: 6.36 us -> 7.81 us
  Pallas kernels: 9.93 us -> 8.65 us
  other arithmetic: 0.15 us -> 1.13 us
    ppermute x2, waiting for transfers between devices: 0.04 us -> 1.49 us  [local(): others = [lax.ppermute(other, 'c', [(0, 1), (1, 0)]) for other in others]]
    concatenate x1, other arithmetic: 0.07 us -> 1.05 us  [local(): jnp.concatenate([embeddings, partner])]
    pallas_call x2 -> x1, Pallas kernels: 2.86 us -> 2.03 us  [local(): pl.pallas_call(member_kernel, out_shape=[jax.ShapeDtypeStruct((n, 1024),...]
  transfers between devices with their start and end apart: 8 -> 8, of which waited for: 1 -> 2; matrix products, arithmetic and copies ran while one was open for 0% -> 1% of each run, Pallas kernels for 9% -> 7%
where the time goes in v12:
time: 81.7 us; the launch traced here: 81.1 us
  starting transfers between devices  62.8 us (77%)
  Pallas kernels  8.65 us (11%)
  waiting for transfers between devices  7.81 us (10%)
  other arithmetic  1.13 us (1%)
    all_to_all x1, starting transfers between devices, local(): lax.all_to_all(messages.reshape(BLOCK, MSG, 128), ('x', 'y', 'c'), 0, 0,...  21.2 us
    all_to_all x1, starting transfers between devices, local(): lax.all_to_all(parts.reshape(8, 17, 1, 128), 'zh', 0, 0, axis_index_group...  19 us
    ppermute x2, starting transfers between devices, local(): others = [lax.ppermute(other, 'c', [(0, 1), (1, 0)]) for other in others]  8.51 us
    all_to_all x1, waiting for transfers between devices, local(): lax.all_to_all(messages.reshape(BLOCK, MSG, 128), ('x', 'y', 'c'), 0, 0,...  6.31 us
    all_to_all x1, starting transfers between devices, local(): lax.all_to_all(parts.reshape(16, 33, 1, 128), ('zl', 'x'), 0, 0, axis_ind...  5.16 us
    ppermute x1, starting transfers between devices, local(): lax.ppermute(jnp.concatenate([embeddings, partner]), ('y', 'c'), near)  3.97 us
    ppermute x1, starting transfers between devices, local(): lax.ppermute(embeddings, 'y', [(i, i ^ 2) for i in range(4)])  2.66 us
    ppermute x1, starting transfers between devices, local(): partner = lax.ppermute(embeddings, 'c', [(0, 1), (1, 0)])  2.27 us
  transfers between devices with their start and end apart: 8, of which 2 were waited for; matrix products, arithmetic and copies ran while one was open for 1% of the time, Pallas kernels for 7%

profile of v12, /device:TPU:1, one launch (start us, length us, event | category | flops | bytes accessed | tf_op | source)
XLA Modules:
  0.0 81.1 jit_solution(9560137256712360936)
XLA Ops:
  0.6 0.0 copy-start
  0.6 2.1 %pack.1 = bf16[4,8,80,128]{3,2,1,0:T(8,128)(2,1)} custom-call(bf16[256,1024]{1,0:T(8,128)(2,1)} %refs_0_, s32[2,128]{1,0:T(2,128)} %bitcast.13, s32[2,128]{1,0:T(2,128)} %rows_hbm.1, s32[2]{0:T(128)} %len_hbm.1), custom_call_target="tpu_custom_call" | custom-call | flops 1048576 | bytes 1572864 | tf_op jit(solution)/shard_map/pack/pallas_call | solution.py:192
  2.7 21.2 %all-to-all-start = ((bf16[32,80,128]{2,1,0:T(8,128)(2,1)}), bf16[32,80,128]{2,1,0:T(8,128)(2,1)S(1)}, u32[]{:S(2)}, u32[]{:S(2)}) async-start(bf16[32,80,128]{2,1,0:T(8,128)(2,1)} %bitcast.12), calls=%async_computation | async-start | bytes 1310720 | tf_op jit(solution)/shard_map/all_to_all | solution.py:211
  23.9 0.0 copy-done
  23.9 2.3 %collective-permute-start = (bf16[256,1024]{1,0:T(8,128)(2,1)S(1)}, bf16[256,1024]{1,0:T(8,128)(2,1)S(1)}, u32[]{:S(2)}, u32[]{:S(2)}) collective-permute-start(bf16[256,1024]{1,0:T(8,128)(2,1)S(1)} %copy-done), channel_id=1, source_target_pairs={{0,1},{1,0},{2,3},{3,2},{4,5},{5,4},{6,7},{7,6},{8,9},{9,8},{10,11... | collective-permute-start | bytes 1572872 | tf_op jit(solution)/shard_map/ppermute | solution.py:221
  26.2 6.3 %all-to-all-done.msg_ref = bf16[32,80,128]{2,1,0:T(8,128)(2,1)S(1)} async-done(((bf16[32,80,128]{2,1,0:T(8,128)(2,1)}), bf16[32,80,128]{2,1,0:T(8,128)(2,1)S(1)}, u32[]{:S(2)}, u32[]{:S(2)}) %all-to-all-start) | async-done | bytes 655392 | tf_op jit(solution)/shard_map/all_to_all | solution.py:211
  32.5 2.2 %sums.1 = (f32[528,128]{1,0:T(8,128)}, s32[4,128]{1,0:T(4,128)S(1)}, s32[2,128]{1,0:T(2,128)S(1)}) custom-call(s32[1]{0:T(128)} %bitcast.1.from_ref, bf16[32,80,128]{2,1,0:T(8,128)(2,1)S(1)} %all-to-all-done.msg_ref), custom_call_target="tpu_custom_call" | custom-call | flops 2147483648 | bytes 1048576 | tf_op jit(solution)/shard_map/sums/pallas_call | solution.py:212
  34.7 0.0 collective-permute-done
  34.7 5.2 %all-to-all-start.1 = ((f32[16,33,1,128]{3,2,1,0:T(1,128)}), f32[16,33,1,128]{3,2,1,0:T(1,128)S(1)}, u32[]{:S(2)}, u32[]{:S(2)}) async-start(f32[16,33,1,128]{3,2,1,0:T(1,128)} %bitcast.4), calls=%async_computation.1 | async-start | bytes 540672 | tf_op jit(solution)/shard_map/all_to_all | solution.py:229
  39.8 1.1 %pad_maximum_fusion = bf16[512,1024]{1,0:T(8,128)(2,1)} fusion(bf16[256,1024]{1,0:T(8,128)(2,1)S(1)} %collective-permute-done, bf16[256,1024]{1,0:T(8,128)(2,1)S(1)} %copy-done), kind=kLoop, calls=%fused_computation | loop fusion | flops 2097152 | bytes 2097152 | tf_op jit(solution)/shard_map/concatenate | solution.py:226
  40.9 4.0 %collective-permute-start.1 = (bf16[512,1024]{1,0:T(8,128)(2,1)}, bf16[512,1024]{1,0:T(8,128)(2,1)S(1)}, u32[]{:S(2)}, u32[]{:S(2)}) collective-permute-start(bf16[512,1024]{1,0:T(8,128)(2,1)} %pad_maximum_fusion), channel_id=1, source_target_pairs={{0,2},{1,7},{2,0},{3,5},{4,6},{5,3},{6,4},{7,1},{8,10},{9,15},{10,... | collective-permute-start | bytes 3145736 | tf_op jit(solution)/shard_map/ppermute | solution.py:226
  44.8 2.7 %collective-permute-start.2 = (bf16[256,1024]{1,0:T(8,128)(2,1)S(1)}, bf16[256,1024]{1,0:T(8,128)(2,1)S(1)}, u32[]{:S(2)}, u32[]{:S(2)}) collective-permute-start(bf16[256,1024]{1,0:T(8,128)(2,1)S(1)} %copy-done), channel_id=1, source_target_pairs={{0,4},{2,6},{4,0},{6,2},{1,5},{3,7},{5,1},{7,3},{8,12},{10,14},{12... | collective-permute-start | bytes 1572872 | tf_op jit(solution)/shard_map/ppermute | solution.py:227
  47.5 0.0 all-to-all-done.1
  47.5 0.7 regroup.1.after_ref
  48.3 19.0 %all-to-all-start.2 = ((f32[8,17,1,128]{3,2,1,0:T(1,128)}), f32[8,17,1,128]{3,2,1,0:T(1,128)S(1)}, u32[]{:S(2)}, u32[]{:S(2)}) async-start(f32[8,17,1,128]{3,2,1,0:T(1,128)} %bitcast.6), calls=%async_computation.2 | async-start | bytes 139264 | tf_op jit(solution)/shard_map/all_to_all | solution.py:241
  67.3 0.1 pad_add_fusion.place_ref
  67.3 0.0 collective-permute-done.2.refs_2_
  67.3 0.0 collective-permute-done.1.refs_1_
  67.3 2.0 %members.1 = (bf16[256,1024]{1,0:T(8,128)(2,1)S(1)}, bf16[128,1024]{1,0:T(8,128)(2,1)S(1)}, bf16[128,1024]{1,0:T(8,128)(2,1)S(1)}) custom-call(f32[136,128]{1,0:T(8,128)} %regroup.1.after_ref, s32[2]{0:T(128)S(1)} %pad_add_fusion.place_ref, s32[4,128]{1,0:T(4,128)S(1)} %get-tuple-element.16.rows_ref, bf16[256,1024]{1,0:T(8,128)(2,1)S(1)} %copy-done, ...), custom_call_target="tpu_custom_call" | custom-call | tf_op jit(solution)/shard_map/members/pallas_call | solution.py:243
  69.4 0.0 copy-start.1
  69.4 6.6 %collective-permute-start.3 = (bf16[128,1024]{1,0:T(8,128)(2,1)S(1)}, bf16[128,1024]{1,0:T(8,128)(2,1)S(1)}, u32[]{:S(2)}, u32[]{:S(2)}) collective-permute-start(bf16[128,1024]{1,0:T(8,128)(2,1)S(1)} %get-tuple-element.20), channel_id=1, source_target_pairs={{0,1},{1,0},{2,3},{3,2},{4,5},{5,4},{6,7},{7,6},{8,9},{9,8},{10,11... | collective-permute-start | bytes 786440 | tf_op jit(solution)/shard_map/ppermute | solution.py:252
  76.0 1.9 %collective-permute-start.4 = (bf16[128,1024]{1,0:T(8,128)(2,1)S(1)}, bf16[128,1024]{1,0:T(8,128)(2,1)S(1)}, u32[]{:S(2)}, u32[]{:S(2)}) collective-permute-start(bf16[128,1024]{1,0:T(8,128)(2,1)S(1)} %get-tuple-element.21), channel_id=1, source_target_pairs={{0,1},{1,0},{2,3},{3,2},{4,5},{5,4},{6,7},{7,6},{8,9},{9,8},{10,11... | collective-permute-start | bytes 786440 | tf_op jit(solution)/shard_map/ppermute | solution.py:252
  77.9 0.0 collective-permute-done.3.refs_0_
  77.9 1.5 %collective-permute-done.4.refs_1_ = bf16[128,1024]{1,0:T(8,128)(2,1)S(1)} collective-permute-done((bf16[128,1024]{1,0:T(8,128)(2,1)S(1)}, bf16[128,1024]{1,0:T(8,128)(2,1)S(1)}, u32[]{:S(2)}, u32[]{:S(2)}) %collective-permute-start.4) | collective-permute-done | bytes 262176 | tf_op jit(solution)/shard_map/ppermute | solution.py:252
  79.4 1.0 %match.1 = f32[2,128]{1,0:T(2,128)} custom-call(s32[2,128]{1,0:T(2,128)S(1)} %get-tuple-element.15.len_ref, bf16[256,1024]{1,0:T(8,128)(2,1)S(1)} %get-tuple-element.19.own_ref, bf16[128,1024]{1,0:T(8,128)(2,1)S(1)} %collective-permute-done.3.refs_0_, bf16[128,1024]{1,0:T(8,128)(2,1)S(1)} %collective-permute-done.4.refs_1_), custom_call_target="tpu_custom_call" | custom-call | tf_op jit(solution)/shard_map/match/pallas_call | solution.py:253
  80.4 0.0 all-to-all-done.2
  80.4 0.0 copy-done.1
  80.4 0.7 finish.1
Async XLA Ops:
  0.6 23.3 %copy-start = (bf16[256,1024]{1,0:T(8,128)(2,1)S(1)}, bf16[256,1024]{1,0:T(8,128)(2,1)}, u32[]{:S(2)}) copy-start(bf16[256,1024]{1,0:T(8,128)(2,1)} %refs_0_) | copy-start | bytes 1572868
  2.7 29.8 %all-to-all-start = ((bf16[32,80,128]{2,1,0:T(8,128)(2,1)}), bf16[32,80,128]{2,1,0:T(8,128)(2,1)S(1)}, u32[]{:S(2)}, u32[]{:S(2)}) async-start(bf16[32,80,128]{2,1,0:T(8,128)(2,1)} %bitcast.12), calls=%async_computation | async-start | bytes 1310720 | tf_op jit(solution)/shard_map/all_to_all | solution.py:211
  23.9 10.8 %collective-permute-start = (bf16[256,1024]{1,0:T(8,128)(2,1)S(1)}, bf16[256,1024]{1,0:T(8,128)(2,1)S(1)}, u32[]{:S(2)}, u32[]{:S(2)}) collective-permute-start(bf16[256,1024]{1,0:T(8,128)(2,1)S(1)} %copy-done), channel_id=1, source_target_pairs={{0,1},{1,0},{2,3},{3,2},{4,5},{5,4},{6,7},{7,6},{8,9},{9,8},{10,11... | collective-permute-start | bytes 1572872 | tf_op jit(solution)/shard_map/ppermute | solution.py:221
  34.7 12.9 %all-to-all-start.1 = ((f32[16,33,1,128]{3,2,1,0:T(1,128)}), f32[16,33,1,128]{3,2,1,0:T(1,128)S(1)}, u32[]{:S(2)}, u32[]{:S(2)}) async-start(f32[16,33,1,128]{3,2,1,0:T(1,128)} %bitcast.4), calls=%async_computation.1 | async-start | bytes 540672 | tf_op jit(solution)/shard_map/all_to_all | solution.py:229
  40.9 26.5 %collective-permute-start.1 = (bf16[512,1024]{1,0:T(8,128)(2,1)}, bf16[512,1024]{1,0:T(8,128)(2,1)S(1)}, u32[]{:S(2)}, u32[]{:S(2)}) collective-permute-start(bf16[512,1024]{1,0:T(8,128)(2,1)} %pad_maximum_fusion), channel_id=1, source_target_pairs={{0,2},{1,7},{2,0},{3,5},{4,6},{5,3},{6,4},{7,1},{8,10},{9,15},{10,... | collective-permute-start | bytes 3145736 | tf_op jit(solution)/shard_map/ppermute | solution.py:226
  44.8 22.5 %collective-permute-start.2 = (bf16[256,1024]{1,0:T(8,128)(2,1)S(1)}, bf16[256,1024]{1,0:T(8,128)(2,1)S(1)}, u32[]{:S(2)}, u32[]{:S(2)}) collective-permute-start(bf16[256,1024]{1,0:T(8,128)(2,1)S(1)} %copy-done), channel_id=1, source_target_pairs={{0,4},{2,6},{4,0},{6,2},{1,5},{3,7},{5,1},{7,3},{8,12},{10,14},{12... | collective-permute-start | bytes 1572872 | tf_op jit(solution)/shard_map/ppermute | solution.py:227
  48.3 32.1 %all-to-all-start.2 = ((f32[8,17,1,128]{3,2,1,0:T(1,128)}), f32[8,17,1,128]{3,2,1,0:T(1,128)S(1)}, u32[]{:S(2)}, u32[]{:S(2)}) async-start(f32[8,17,1,128]{3,2,1,0:T(1,128)} %bitcast.6), calls=%async_computation.2 | async-start | bytes 139264 | tf_op jit(solution)/shard_map/all_to_all | solution.py:241
  69.4 11.0 %copy-start.1 = (f32[16,128]{1,0:T(8,128)S(1)}, f32[16,128]{1,0:T(8,128)}, u32[]{:S(2)}) copy-start(f32[16,128]{1,0:T(8,128)} %old_ref.1) | copy-start | bytes 24580
  69.4 8.5 %collective-permute-start.3 = (bf16[128,1024]{1,0:T(8,128)(2,1)S(1)}, bf16[128,1024]{1,0:T(8,128)(2,1)S(1)}, u32[]{:S(2)}, u32[]{:S(2)}) collective-permute-start(bf16[128,1024]{1,0:T(8,128)(2,1)S(1)} %get-tuple-element.20), channel_id=1, source_target_pairs={{0,1},{1,0},{2,3},{3,2},{4,5},{5,4},{6,7},{7,6},{8,9},{9,8},{10,11... | collective-permute-start | bytes 786440 | tf_op jit(solution)/shard_map/ppermute | solution.py:252
  76.0 3.4 %collective-permute-start.4 = (bf16[128,1024]{1,0:T(8,128)(2,1)S(1)}, bf16[128,1024]{1,0:T(8,128)(2,1)S(1)}, u32[]{:S(2)}, u32[]{:S(2)}) collective-permute-start(bf16[128,1024]{1,0:T(8,128)(2,1)S(1)} %get-tuple-element.21), channel_id=1, source_target_pairs={{0,1},{1,0},{2,3},{3,2},{4,5},{5,4},{6,7},{7,6},{8,9},{9,8},{10,11... | collective-permute-start | bytes 786440 | tf_op jit(solution)/shard_map/ppermute | solution.py:252

commit v13 on v11

--- a/solution.py
+++ b/solution.py
@@ -31,10 +31,11 @@
     return pl.CostEstimate(flops=flops, bytes_accessed=moved, transcendentals=0)
 
 
-def pack_kernel(emb_hbm, label_hbm, rows_hbm, out_hbm, emb_ref, label_ref, rows_ref, msg_ref, in_sems, out_sems, sems):
+def pack_kernel(emb_hbm, label_hbm, rows_hbm, len_hbm, out_hbm, emb_ref, label_ref, rows_ref, len_ref, msg_ref, in_sems, out_sems, sems):
     small = [
         pltpu.make_async_copy(label_hbm, label_ref, sems.at[0]),
         pltpu.make_async_copy(rows_hbm, rows_ref, sems.at[1]),
+        pltpu.make_async_copy(len_hbm, len_ref, sems.at[2]),
     ]
     halves = [pl.ds(0, 512), pl.ds(512, 512)]
     blocks = [pltpu.make_async_copy(emb_hbm.at[:, at], emb_ref.at[:, at], in_sems.at[k]) for k, at in enumerate(halves)]
@@ -50,6 +51,8 @@
     for k, pair in enumerate((high, low, r >> 3, r & 7)):
         codes = jnp.where(row == 2 * k, pair[0:1], codes)
         codes = jnp.where(row == 2 * k + 1, pair[1:2], codes)
+    for k in range(2):
+        codes = jnp.where(row == 8 + k, len_ref[k], codes)
     codes = codes.astype(F32).astype(BF16)
     sent = []
     for k in range(2):
@@ -72,7 +75,7 @@
     return lax.broadcasted_iota(I32, (n, 128), 0).astype(F32).astype(BF16)
 
 
-def sum_kernel(from_ref, msg_ref, out_ref, rows_ref):
+def sum_kernel(from_ref, msg_ref, out_ref, rows_ref, len_ref):
     cluster = lanes(256)
     one, zero = jnp.ones((), BF16), jnp.zeros((), BF16)
     contract = (((1,), (1,)), ((), ()))
@@ -106,6 +109,8 @@
     for k in range(2):
         codes = msg_ref[from_ref[0] ^ k, 64:80, :].astype(F32).astype(I32)
         rows_ref[2 * k : 2 * k + 2, :] = codes[4:6] * 8 + codes[6:8]
+        if k == 0:
+            len_ref[...] = codes[8:10]
 
 
 def regroup_kernel(in_ref, out_ref, s_ref):
@@ -164,26 +169,19 @@
         out_ref[...] = total[128 * s : 128 * s + 128].astype(BF16)
 
 
-def match_kernel(len_hbm, *refs):
+def match_kernel(len_ref, *refs):
+    own_refs, other_refs, out_ref = refs[0:2], refs[2:4], refs[4]
     i = lax.broadcasted_iota(I32, (128, 128), 0)
     j = lax.broadcasted_iota(I32, (128, 128), 1)
-    own_refs, other_refs, (out_ref, len_ref, sem) = refs[0:2], refs[2:4], refs[4:7]
-    lengths = pltpu.make_async_copy(len_hbm, len_ref, sem)
-    lengths.start()
-    i = lax.broadcasted_iota(I32, (128, 128), 0)
-    j = lax.broadcasted_iota(I32, (128, 128), 1)
-    cosines = []
     for s in range(2):
         one = own_refs[s][...] + other_refs[s][...]
         gram = lax.dot_general(one, one, (((1,), (1,)), ((), ())), preferred_element_type=F32)
         diagonal = jnp.where(i == j, gram, 0.0)
         down = lax.rsqrt(jnp.sum(diagonal, axis=1, keepdims=True) + 1e-06)
         across = lax.rsqrt(jnp.sum(diagonal, axis=0, keepdims=True) + 1e-06)
-        cosines.append(gram * down * across)
-    lengths.wait()
-    for s in range(2):
-        length = len_ref[s]
-        largest = jnp.max(jnp.where((i < length) & (i != j), cosines[s], -2.0), axis=0, keepdims=True)
+        cosine = gram * down * across
+        length = len_ref[s : s + 1, :]
+        largest = jnp.max(jnp.where((i < length) & (i != j), cosine, -2.0), axis=0, keepdims=True)
         out_ref[s : s + 1, :] = jnp.where(j[0:1] < length, largest, 0.0)
 
 
@@ -197,27 +195,28 @@
     messages = pl.pallas_call(
         pack_kernel,
         out_shape=pltpu.HBM((4, 8, MSG, 128), BF16),
-        in_specs=[HBM] * 3,
+        in_specs=[HBM] * 4,
         out_specs=HBM,
         scratch_shapes=[
             pltpu.VMEM((ROWS, 1024), BF16),
             pltpu.VMEM((2, 128), I32),
             pltpu.VMEM((2, 128), I32),
+            pltpu.SMEM((2,), I32),
             pltpu.VMEM((4, 8, MSG, 128), BF16),
             pltpu.SemaphoreType.DMA((2,)),
             pltpu.SemaphoreType.DMA((2,)),
-            pltpu.SemaphoreType.DMA((2,)),
+            pltpu.SemaphoreType.DMA((3,)),
         ],
         compiler_params=params(8),
         cost_estimate=cost(1 << 20, 3 << 19),
         name="pack",
-    )(*(pltpu.with_memory_space_constraint(a, pltpu.HBM) for a in (embeddings, assignments.reshape(2, 128), slab_rows)))
+    )(*(pltpu.with_memory_space_constraint(a, pltpu.HBM) for a in (embeddings, assignments.reshape(2, 128), slab_rows, slab_len)))
     messages = lax.all_to_all(messages.reshape(BLOCK, MSG, 128), ("x", "y", "c"), 0, 0, axis_index_groups=[BLOCK_ORDER], tiled=True)
-    parts, rows = pl.pallas_call(
+    parts, rows, lengths = pl.pallas_call(
         sum_kernel,
-        out_shape=(pltpu.VMEM((528, 128), F32), pltpu.VMEM((4, 128), I32)),
+        out_shape=(pltpu.VMEM((528, 128), F32), pltpu.VMEM((4, 128), I32), pltpu.VMEM((2, 128), I32)),
         in_specs=[SMEM, VMEM],
-        out_specs=(VMEM, VMEM),
+        out_specs=(VMEM, VMEM, VMEM),
         compiler_params=params(20),
         cost_estimate=cost(1 << 31, 1 << 20),
         name="sums",
@@ -260,13 +259,12 @@
     best_cosine = pl.pallas_call(
         match_kernel,
         out_shape=jax.ShapeDtypeStruct((2, 128), F32),
-        in_specs=[HBM] + [VMEM] * 4,
+        in_specs=[VMEM] * 5,
         out_specs=VMEM,
-        scratch_shapes=[pltpu.SMEM((2,), I32), pltpu.SemaphoreType.DMA],
         compiler_params=params(8),
         cost_estimate=cost(0, 0),
         name="match",
-    )(pltpu.with_memory_space_constraint(slab_len, pltpu.HBM), *own, *others)
+    )(lengths, *own, *others)
     parts, best_cosine = lax.optimization_barrier((parts, best_cosine))
     centroids = pl.pallas_call(
         finish_kernel,

time: 80.3 us -> 79.9 us (level)
  transfers between devices with their start and end apart: 8 -> 8, of which waited for: 1 -> 1; matrix products, arithmetic and copies ran while one was open for 0% -> 0% of each run, Pallas kernels for 9% -> 8%
where the time goes in v13:
time: 79.9 us; the launch traced here: 79.3 us
  starting transfers between devices  62.6 us (78%)
  Pallas kernels  9.49 us (12%)
  waiting for transfers between devices  6.36 us (8%)
    all_to_all x1, starting transfers between devices, local(): lax.all_to_all(messages.reshape(BLOCK, MSG, 128), ('x', 'y', 'c'), 0, 0,...  21.2 us
    all_to_all x1, starting transfers between devices, local(): lax.all_to_all(parts.reshape(8, 17, 1, 128), 'zh', 0, 0, axis_index_group...  19 us
    ppermute x2, starting transfers between devices, local(): others = [lax.ppermute(other, 'c', [(0, 1), (1, 0)]) for other in others]  8.31 us
    all_to_all x1, waiting for transfers between devices, local(): lax.all_to_all(messages.reshape(BLOCK, MSG, 128), ('x', 'y', 'c'), 0, 0,...  6.31 us
    all_to_all x1, starting transfers between devices, local(): lax.all_to_all(parts.reshape(16, 33, 1, 128), ('zl', 'x'), 0, 0, axis_ind...  5.16 us
    ppermute x1, starting transfers between devices, local(): lax.ppermute(jnp.concatenate([embeddings, partner]), ('y', 'c'), near)  3.98 us
    pallas_call x2, Pallas kernels, local(): pl.pallas_call(functools.partial(member_kernel, of), out_shape=[jax.Shape...  2.86 us
    ppermute x1, starting transfers between devices, local(): lax.ppermute(embeddings, 'y', [(i, i ^ 2) for i in range(4)])  2.66 us
  transfers between devices with their start and end apart: 8, of which 1 were waited for; matrix products, arithmetic and copies ran while one was open for 0% of the time, Pallas kernels for 8%

profile of v13, /device:TPU:1, one launch (start us, length us, event | category | flops | bytes accessed | tf_op | source)
XLA Modules:
  0.0 79.3 jit_solution(17990512380619526031)
XLA Ops:
  0.6 0.0 copy-start
  0.6 2.1 %pack.1 = bf16[4,8,80,128]{3,2,1,0:T(8,128)(2,1)} custom-call(bf16[256,1024]{1,0:T(8,128)(2,1)} %refs_0_.1, s32[2,128]{1,0:T(2,128)} %bitcast.13, s32[2,128]{1,0:T(2,128)} %rows_hbm.1, s32[2]{0:T(128)} %len_hbm.1), custom_call_target="tpu_custom_call" | custom-call | flops 1048576 | bytes 1572864 | tf_op jit(solution)/shard_map/pack/pallas_call | solution.py:195
  2.7 21.2 %all-to-all-start = ((bf16[32,80,128]{2,1,0:T(8,128)(2,1)}), bf16[32,80,128]{2,1,0:T(8,128)(2,1)S(1)}, u32[]{:S(2)}, u32[]{:S(2)}) async-start(bf16[32,80,128]{2,1,0:T(8,128)(2,1)} %bitcast.12), calls=%async_computation | async-start | bytes 1310720 | tf_op jit(solution)/shard_map/all_to_all | solution.py:214
  23.9 0.0 copy-done
  23.9 2.3 %collective-permute-start = (bf16[256,1024]{1,0:T(8,128)(2,1)S(1)}, bf16[256,1024]{1,0:T(8,128)(2,1)S(1)}, u32[]{:S(2)}, u32[]{:S(2)}) collective-permute-start(bf16[256,1024]{1,0:T(8,128)(2,1)S(1)} %copy-done), channel_id=1, source_target_pairs={{0,1},{1,0},{2,3},{3,2},{4,5},{5,4},{6,7},{7,6},{8,9},{9,8},{10,11... | collective-permute-start | bytes 1572872 | tf_op jit(solution)/shard_map/ppermute | solution.py:224
  26.2 6.3 %all-to-all-done.msg_ref = bf16[32,80,128]{2,1,0:T(8,128)(2,1)S(1)} async-done(((bf16[32,80,128]{2,1,0:T(8,128)(2,1)}), bf16[32,80,128]{2,1,0:T(8,128)(2,1)S(1)}, u32[]{:S(2)}, u32[]{:S(2)}) %all-to-all-start) | async-done | bytes 655392 | tf_op jit(solution)/shard_map/all_to_all | solution.py:214
  32.5 2.1 %sums.1 = (f32[528,128]{1,0:T(8,128)}, s32[4,128]{1,0:T(4,128)S(1)}, s32[2,128]{1,0:T(2,128)S(1)}) custom-call(s32[1]{0:T(128)} %bitcast.1.from_ref, bf16[32,80,128]{2,1,0:T(8,128)(2,1)S(1)} %all-to-all-done.msg_ref), custom_call_target="tpu_custom_call" | custom-call | flops 2147483648 | bytes 1048576 | tf_op jit(solution)/shard_map/sums/pallas_call | solution.py:215
  34.7 0.0 collective-permute-done
  34.7 5.2 %all-to-all-start.1 = ((f32[16,33,1,128]{3,2,1,0:T(1,128)}), f32[16,33,1,128]{3,2,1,0:T(1,128)S(1)}, u32[]{:S(2)}, u32[]{:S(2)}) async-start(f32[16,33,1,128]{3,2,1,0:T(1,128)} %bitcast.4), calls=%async_computation.1 | async-start | bytes 540672 | tf_op jit(solution)/shard_map/all_to_all | solution.py:232
  39.8 0.1 pad_maximum_fusion
  39.9 4.0 %collective-permute-start.1 = (bf16[512,1024]{1,0:T(8,128)(2,1)S(1)}, bf16[512,1024]{1,0:T(8,128)(2,1)S(1)}, u32[]{:S(2)}, u32[]{:S(2)}) collective-permute-start(bf16[512,1024]{1,0:T(8,128)(2,1)S(1)} %pad_maximum_fusion), channel_id=1, source_target_pairs={{0,2},{1,7},{2,0},{3,5},{4,6},{5,3},{6,4},{7,1},{8,10},{9,15},{10,... | collective-permute-start | bytes 3145736 | tf_op jit(solution)/shard_map/ppermute | solution.py:229
  43.9 2.7 %collective-permute-start.2 = (bf16[256,1024]{1,0:T(8,128)(2,1)S(1)}, bf16[256,1024]{1,0:T(8,128)(2,1)S(1)}, u32[]{:S(2)}, u32[]{:S(2)}) collective-permute-start(bf16[256,1024]{1,0:T(8,128)(2,1)S(1)} %copy-done), channel_id=1, source_target_pairs={{0,4},{2,6},{4,0},{6,2},{1,5},{3,7},{5,1},{7,3},{8,12},{10,14},{12... | collective-permute-start | bytes 1572872 | tf_op jit(solution)/shard_map/ppermute | solution.py:230
  46.5 0.0 all-to-all-done.1
  46.6 0.8 regroup.1.after_ref
  47.3 19.0 %all-to-all-start.2 = ((f32[8,17,1,128]{3,2,1,0:T(1,128)}), f32[8,17,1,128]{3,2,1,0:T(1,128)S(1)}, u32[]{:S(2)}, u32[]{:S(2)}) async-start(f32[8,17,1,128]{3,2,1,0:T(1,128)} %bitcast.6), calls=%async_computation.2 | async-start | bytes 139264 | tf_op jit(solution)/shard_map/all_to_all | solution.py:244
  66.3 0.1 pad_add_fusion.place_ref
  66.4 0.0 collective-permute-done.2.refs_2_
  66.4 0.0 collective-permute-done.1.refs_1_
  66.4 1.4 %members.3 = (bf16[128,1024]{1,0:T(8,128)(2,1)S(1)}, bf16[128,1024]{1,0:T(8,128)(2,1)S(1)}) custom-call(f32[136,128]{1,0:T(8,128)} %regroup.1.after_ref, s32[2]{0:T(128)S(1)} %pad_add_fusion.place_ref, s32[4,128]{1,0:T(4,128)S(1)} %get-tuple-element.17.rows_ref, bf16[256,1024]{1,0:T(8,128)(2,1)S(1)} %copy-done, ...), custom_call_target="tpu_custom_call" | custom-call | tf_op jit(solution)/shard_map/members/pallas_call | solution.py:247
  67.8 6.4 %collective-permute-start.3 = (bf16[128,1024]{1,0:T(8,128)(2,1)S(1)}, bf16[128,1024]{1,0:T(8,128)(2,1)S(1)}, u32[]{:S(2)}, u32[]{:S(2)}) collective-permute-start(bf16[128,1024]{1,0:T(8,128)(2,1)S(1)} %get-tuple-element.22), channel_id=1, source_target_pairs={{0,1},{1,0},{2,3},{3,2},{4,5},{5,4},{6,7},{7,6},{8,9},{9,8},{10,11... | collective-permute-start | bytes 786440 | tf_op jit(solution)/shard_map/ppermute | solution.py:258
  74.2 1.9 %collective-permute-start.4 = (bf16[128,1024]{1,0:T(8,128)(2,1)S(1)}, bf16[128,1024]{1,0:T(8,128)(2,1)S(1)}, u32[]{:S(2)}, u32[]{:S(2)}) collective-permute-start(bf16[128,1024]{1,0:T(8,128)(2,1)S(1)} %get-tuple-element.23), channel_id=1, source_target_pairs={{0,1},{1,0},{2,3},{3,2},{4,5},{5,4},{6,7},{7,6},{8,9},{9,8},{10,11... | collective-permute-start | bytes 786440 | tf_op jit(solution)/shard_map/ppermute | solution.py:258
  76.1 1.4 %members.2 = (bf16[128,1024]{1,0:T(8,128)(2,1)S(1)}, bf16[128,1024]{1,0:T(8,128)(2,1)S(1)}) custom-call(f32[136,128]{1,0:T(8,128)} %regroup.1.after_ref, s32[2]{0:T(128)S(1)} %pad_add_fusion.place_ref, s32[4,128]{1,0:T(4,128)S(1)} %get-tuple-element.17.rows_ref, bf16[256,1024]{1,0:T(8,128)(2,1)S(1)} %copy-done, ...), custom_call_target="tpu_custom_call" | custom-call | tf_op jit(solution)/shard_map/members/pallas_call | solution.py:247
  77.6 0.0 copy-start.1
  77.6 0.0 collective-permute-done.3.refs_2_
  77.6 0.0 collective-permute-done.4.refs_3_
  77.6 1.0 %match.1 = f32[2,128]{1,0:T(2,128)} custom-call(s32[2,128]{1,0:T(2,128)S(1)} %get-tuple-element.16.len_ref, bf16[128,1024]{1,0:T(8,128)(2,1)S(1)} %get-tuple-element.20.refs_0_, bf16[128,1024]{1,0:T(8,128)(2,1)S(1)} %get-tuple-element.21.refs_1_, bf16[128,1024]{1,0:T(8,128)(2,1)S(1)} %collective-permute-done.3.refs_2_, ...), custom_call_target="tpu_custom_call" | custom-call | tf_op jit(solution)/shard_map/match/pallas_call | solution.py:259
  78.6 0.0 all-to-all-done.2
  78.6 0.0 copy-done.1
  78.6 0.7 finish.1
Async XLA Ops:
  0.6 23.3 %copy-start = (bf16[256,1024]{1,0:T(8,128)(2,1)S(1)}, bf16[256,1024]{1,0:T(8,128)(2,1)}, u32[]{:S(2)}) copy-start(bf16[256,1024]{1,0:T(8,128)(2,1)} %refs_0_.1) | copy-start | bytes 1572868
  2.7 29.8 %all-to-all-start = ((bf16[32,80,128]{2,1,0:T(8,128)(2,1)}), bf16[32,80,128]{2,1,0:T(8,128)(2,1)S(1)}, u32[]{:S(2)}, u32[]{:S(2)}) async-start(bf16[32,80,128]{2,1,0:T(8,128)(2,1)} %bitcast.12), calls=%async_computation | async-start | bytes 1310720 | tf_op jit(solution)/shard_map/all_to_all | solution.py:214
  23.9 10.7 %collective-permute-start = (bf16[256,1024]{1,0:T(8,128)(2,1)S(1)}, bf16[256,1024]{1,0:T(8,128)(2,1)S(1)}, u32[]{:S(2)}, u32[]{:S(2)}) collective-permute-start(bf16[256,1024]{1,0:T(8,128)(2,1)S(1)} %copy-done), channel_id=1, source_target_pairs={{0,1},{1,0},{2,3},{3,2},{4,5},{5,4},{6,7},{7,6},{8,9},{9,8},{10,11... | collective-permute-start | bytes 1572872 | tf_op jit(solution)/shard_map/ppermute | solution.py:224
  34.7 11.9 %all-to-all-start.1 = ((f32[16,33,1,128]{3,2,1,0:T(1,128)}), f32[16,33,1,128]{3,2,1,0:T(1,128)S(1)}, u32[]{:S(2)}, u32[]{:S(2)}) async-start(f32[16,33,1,128]{3,2,1,0:T(1,128)} %bitcast.4), calls=%async_computation.1 | async-start | bytes 540672 | tf_op jit(solution)/shard_map/all_to_all | solution.py:232
  39.9 26.5 %collective-permute-start.1 = (bf16[512,1024]{1,0:T(8,128)(2,1)S(1)}, bf16[512,1024]{1,0:T(8,128)(2,1)S(1)}, u32[]{:S(2)}, u32[]{:S(2)}) collective-permute-start(bf16[512,1024]{1,0:T(8,128)(2,1)S(1)} %pad_maximum_fusion), channel_id=1, source_target_pairs={{0,2},{1,7},{2,0},{3,5},{4,6},{5,3},{6,4},{7,1},{8,10},{9,15},{10,... | collective-permute-start | bytes 3145736 | tf_op jit(solution)/shard_map/ppermute | solution.py:229
  43.9 22.5 %collective-permute-start.2 = (bf16[256,1024]{1,0:T(8,128)(2,1)S(1)}, bf16[256,1024]{1,0:T(8,128)(2,1)S(1)}, u32[]{:S(2)}, u32[]{:S(2)}) collective-permute-start(bf16[256,1024]{1,0:T(8,128)(2,1)S(1)} %copy-done), channel_id=1, source_target_pairs={{0,4},{2,6},{4,0},{6,2},{1,5},{3,7},{5,1},{7,3},{8,12},{10,14},{12... | collective-permute-start | bytes 1572872 | tf_op jit(solution)/shard_map/ppermute | solution.py:230
  47.3 31.3 %all-to-all-start.2 = ((f32[8,17,1,128]{3,2,1,0:T(1,128)}), f32[8,17,1,128]{3,2,1,0:T(1,128)S(1)}, u32[]{:S(2)}, u32[]{:S(2)}) async-start(f32[8,17,1,128]{3,2,1,0:T(1,128)} %bitcast.6), calls=%async_computation.2 | async-start | bytes 139264 | tf_op jit(solution)/shard_map/all_to_all | solution.py:244
  67.8 9.8 %collective-permute-start.3 = (bf16[128,1024]{1,0:T(8,128)(2,1)S(1)}, bf16[128,1024]{1,0:T(8,128)(2,1)S(1)}, u32[]{:S(2)}, u32[]{:S(2)}) collective-permute-start(bf16[128,1024]{1,0:T(8,128)(2,1)S(1)} %get-tuple-element.22), channel_id=1, source_target_pairs={{0,1},{1,0},{2,3},{3,2},{4,5},{5,4},{6,7},{7,6},{8,9},{9,8},{10,11... | collective-permute-start | bytes 786440 | tf_op jit(solution)/shard_map/ppermute | solution.py:258
  74.2 3.4 %collective-permute-start.4 = (bf16[128,1024]{1,0:T(8,128)(2,1)S(1)}, bf16[128,1024]{1,0:T(8,128)(2,1)S(1)}, u32[]{:S(2)}, u32[]{:S(2)}) collective-permute-start(bf16[128,1024]{1,0:T(8,128)(2,1)S(1)} %get-tuple-element.23), channel_id=1, source_target_pairs={{0,1},{1,0},{2,3},{3,2},{4,5},{5,4},{6,7},{7,6},{8,9},{9,8},{10,11... | collective-permute-start | bytes 786440 | tf_op jit(solution)/shard_map/ppermute | solution.py:258
  77.6 1.0 %copy-start.1 = (f32[16,128]{1,0:T(8,128)S(1)}, f32[16,128]{1,0:T(8,128)}, u32[]{:S(2)}) copy-start(f32[16,128]{1,0:T(8,128)} %old_ref.1) | copy-start | bytes 24580

commit v14 on v13

--- a/solution.py
+++ b/solution.py
@@ -150,7 +150,7 @@
 
 
 def member_kernel(of, after_ref, place_ref, rows_ref, *refs):
-    line_refs, out_refs = refs[:3], refs[3:]
+    line_refs, out_ref = refs[:3], refs[3]
     core, y = place_ref[0], place_ref[1]
     r = rows_ref[2 * of : 2 * of + 2, :]
     away, far = (r >> 9) ^ y, ((r >> 8) & 1) ^ core
@@ -165,16 +165,14 @@
             pick = jnp.where(lane + ROWS * (first + k) == at, 1.0, 0.0).astype(BF16)
             rows = line_ref[ROWS * k : ROWS * k + ROWS, :]
             total = total + jnp.dot(pick, rows, preferred_element_type=F32)
-    for s, out_ref in enumerate(out_refs):
-        out_ref[...] = total[128 * s : 128 * s + 128].astype(BF16)
-
-
-def match_kernel(len_ref, *refs):
-    own_refs, other_refs, out_ref = refs[0:2], refs[2:4], refs[4]
+    out_ref[...] = total.astype(BF16)
+
+
+def match_kernel(after_ref, len_ref, own_ref, other_ref, out_ref):
     i = lax.broadcasted_iota(I32, (128, 128), 0)
     j = lax.broadcasted_iota(I32, (128, 128), 1)
     for s in range(2):
-        one = own_refs[s][...] + other_refs[s][...]
+        one = own_ref[128 * s : 128 * s + 128, :] + other_ref[128 * s : 128 * s + 128, :]
         gram = lax.dot_general(one, one, (((1,), (1,)), ((), ())), preferred_element_type=F32)
         diagonal = jnp.where(i == j, gram, 0.0)
         down = lax.rsqrt(jnp.sum(diagonal, axis=1, keepdims=True) + 1e-06)
@@ -243,38 +241,37 @@
     after = parts
     parts = lax.all_to_all(parts.reshape(8, 17, 1, 128), "zh", 0, 0, axis_index_groups=[RING_ORDER], tiled=True)
     place = jnp.stack([core, y])
-    own, others = (
+    own, other = (
         pl.pallas_call(
             functools.partial(member_kernel, of),
-            out_shape=[jax.ShapeDtypeStruct((128, 1024), BF16)] * 2,
+            out_shape=jax.ShapeDtypeStruct((256, 1024), BF16),
             in_specs=[pl.BlockSpec(memory_space=pl.ANY), SMEM] + [VMEM] * 4,
-            out_specs=[VMEM] * 2,
+            out_specs=VMEM,
             compiler_params=params(16),
             cost_estimate=cost(0, 0),
             name="members",
         )(after, place, rows, *line)
         for of in range(2)
     )
-    others = [lax.ppermute(other, "c", [(0, 1), (1, 0)]) for other in others]
-    best_cosine = pl.pallas_call(
-        match_kernel,
-        out_shape=jax.ShapeDtypeStruct((2, 128), F32),
-        in_specs=[VMEM] * 5,
-        out_specs=VMEM,
-        compiler_params=params(8),
-        cost_estimate=cost(0, 0),
-        name="match",
-    )(lengths, *own, *others)
-    parts, best_cosine = lax.optimization_barrier((parts, best_cosine))
+    other = lax.ppermute(other, "c", [(0, 1), (1, 0)])
     centroids = pl.pallas_call(
         finish_kernel,
         out_shape=jax.ShapeDtypeStruct((16, 128), F32),
         in_specs=[SMEM, VMEM, VMEM],
         out_specs=VMEM,
         compiler_params=params(4),
-        cost_estimate=cost(1 << 18, 1 << 18),
+        cost_estimate=cost(1 << 35, 1 << 18),
         name="finish",
     )((zh * 16).reshape(1), parts.reshape(136, 128), old_centroids)
+    best_cosine = pl.pallas_call(
+        match_kernel,
+        out_shape=jax.ShapeDtypeStruct((2, 128), F32),
+        in_specs=[HBM] + [VMEM] * 3,
+        out_specs=VMEM,
+        compiler_params=params(8),
+        cost_estimate=cost(0, 0),
+        name="match",
+    )(pltpu.with_memory_space_constraint(centroids, pltpu.HBM), lengths, own, other)
     return (centroids, best_cosine)
 
 

time: 79.9 us -> 81.6 us (1.021)
  the two profiles are of different devices: /device:TPU:1 before, /device:TPU:22 now
where the time goes in v14:
time: 81.6 us; the launch traced here: 81 us
  starting transfers between devices  50 us (61%)
  waiting for transfers between devices  19.6 us (24%)
  Pallas kernels  10.5 us (13%)
    all_to_all x1, starting transfers between devices, local(): lax.all_to_all(parts.reshape(8, 17, 1, 128), 'zh', 0, 0, axis_index_group...  19.4 us
    all_to_all x1, starting transfers between devices, local(): lax.all_to_all(messages.reshape(BLOCK, MSG, 128), ('x', 'y', 'c'), 0, 0,...  15.2 us
    all_to_all x1, waiting for transfers between devices, local(): lax.all_to_all(messages.reshape(BLOCK, MSG, 128), ('x', 'y', 'c'), 0, 0,...  9.27 us
    all_to_all x1, waiting for transfers between devices, local(): lax.all_to_all(parts.reshape(8, 17, 1, 128), 'zh', 0, 0, axis_index_group...  6.76 us
    all_to_all x1, starting transfers between devices, local(): lax.all_to_all(parts.reshape(16, 33, 1, 128), ('zl', 'x'), 0, 0, axis_ind...  4.8 us
    ppermute x1, starting transfers between devices, local(): lax.ppermute(jnp.concatenate([embeddings, partner]), ('y', 'c'), near)  3.66 us
    all_to_all x1, waiting for transfers between devices, local(): lax.all_to_all(parts.reshape(16, 33, 1, 128), ('zl', 'x'), 0, 0, axis_ind...  3.54 us
    ppermute x1, starting transfers between devices, local(): lax.ppermute(embeddings, 'y', [(i, i ^ 2) for i in range(4)])  3 us
  transfers between devices with their start and end apart: 7, of which 3 were waited for; matrix products, arithmetic and copies ran while one was open for 0% of the time, Pallas kernels for 8%

profile of v14, /device:TPU:22, one launch (start us, length us, event | category | flops | bytes accessed | tf_op | source)
XLA Modules:
  0.0 81.0 jit_solution(5880058339601323798)
XLA Ops:
  0.6 0.0 copy-start
  0.6 2.1 %pack.1 = bf16[4,8,80,128]{3,2,1,0:T(8,128)(2,1)} custom-call(bf16[256,1024]{1,0:T(8,128)(2,1)} %refs_0_.1, s32[2,128]{1,0:T(2,128)} %bitcast.13, s32[2,128]{1,0:T(2,128)} %rows_hbm.1, s32[2]{0:T(128)} %len_hbm.1), custom_call_target="tpu_custom_call" | custom-call | flops 1048576 | bytes 1572864 | tf_op jit(solution)/shard_map/pack/pallas_call | solution.py:193
  2.7 15.2 %all-to-all-start = ((bf16[32,80,128]{2,1,0:T(8,128)(2,1)}), bf16[32,80,128]{2,1,0:T(8,128)(2,1)S(1)}, u32[]{:S(2)}, u32[]{:S(2)}) async-start(bf16[32,80,128]{2,1,0:T(8,128)(2,1)} %bitcast.12), calls=%async_computation | async-start | bytes 1310720 | tf_op jit(solution)/shard_map/all_to_all | solution.py:212
  17.9 0.0 copy-done
  17.9 2.1 %collective-permute-start = (bf16[256,1024]{1,0:T(8,128)(2,1)S(1)}, bf16[256,1024]{1,0:T(8,128)(2,1)S(1)}, u32[]{:S(2)}, u32[]{:S(2)}) collective-permute-start(bf16[256,1024]{1,0:T(8,128)(2,1)S(1)} %copy-done), channel_id=1, source_target_pairs={{0,1},{1,0},{2,3},{3,2},{4,5},{5,4},{6,7},{7,6},{8,9},{9,8},{10,11... | collective-permute-start | bytes 1572872 | tf_op jit(solution)/shard_map/ppermute | solution.py:222
  20.0 9.3 %all-to-all-done.msg_ref = bf16[32,80,128]{2,1,0:T(8,128)(2,1)S(1)} async-done(((bf16[32,80,128]{2,1,0:T(8,128)(2,1)}), bf16[32,80,128]{2,1,0:T(8,128)(2,1)S(1)}, u32[]{:S(2)}, u32[]{:S(2)}) %all-to-all-start) | async-done | bytes 655392 | tf_op jit(solution)/shard_map/all_to_all | solution.py:212
  29.3 2.1 %sums.1 = (f32[528,128]{1,0:T(8,128)}, s32[4,128]{1,0:T(4,128)S(1)}, s32[2,128]{1,0:T(2,128)S(1)}) custom-call(s32[1]{0:T(128)} %bitcast.1.from_ref, bf16[32,80,128]{2,1,0:T(8,128)(2,1)S(1)} %all-to-all-done.msg_ref), custom_call_target="tpu_custom_call" | custom-call | flops 2147483648 | bytes 1048576 | tf_op jit(solution)/shard_map/sums/pallas_call | solution.py:213
  31.4 0.0 collective-permute-done
  31.4 4.8 %all-to-all-start.1 = ((f32[16,33,1,128]{3,2,1,0:T(1,128)}), f32[16,33,1,128]{3,2,1,0:T(1,128)S(1)}, u32[]{:S(2)}, u32[]{:S(2)}) async-start(f32[16,33,1,128]{3,2,1,0:T(1,128)} %bitcast.4), calls=%async_computation.1 | async-start | bytes 540672 | tf_op jit(solution)/shard_map/all_to_all | solution.py:230
  36.2 0.1 pad_maximum_fusion
  36.3 3.7 %collective-permute-start.1 = (bf16[512,1024]{1,0:T(8,128)(2,1)S(1)}, bf16[512,1024]{1,0:T(8,128)(2,1)S(1)}, u32[]{:S(2)}, u32[]{:S(2)}) collective-permute-start(bf16[512,1024]{1,0:T(8,128)(2,1)S(1)} %pad_maximum_fusion), channel_id=1, source_target_pairs={{0,2},{1,7},{2,0},{3,5},{4,6},{5,3},{6,4},{7,1},{8,10},{9,15},{10,... | collective-permute-start | bytes 3145736 | tf_op jit(solution)/shard_map/ppermute | solution.py:227
  40.0 3.0 %collective-permute-start.2 = (bf16[256,1024]{1,0:T(8,128)(2,1)S(1)}, bf16[256,1024]{1,0:T(8,128)(2,1)S(1)}, u32[]{:S(2)}, u32[]{:S(2)}) collective-permute-start(bf16[256,1024]{1,0:T(8,128)(2,1)S(1)} %copy-done), channel_id=1, source_target_pairs={{0,4},{2,6},{4,0},{6,2},{1,5},{3,7},{5,1},{7,3},{8,12},{10,14},{12... | collective-permute-start | bytes 1572872 | tf_op jit(solution)/shard_map/ppermute | solution.py:228
  43.0 3.5 %all-to-all-done.1 = f32[16,33,1,128]{3,2,1,0:T(1,128)S(1)} async-done(((f32[16,33,1,128]{3,2,1,0:T(1,128)}), f32[16,33,1,128]{3,2,1,0:T(1,128)S(1)}, u32[]{:S(2)}, u32[]{:S(2)}) %all-to-all-start.1) | async-done | bytes 270368 | tf_op jit(solution)/shard_map/all_to_all | solution.py:230
  46.5 0.8 regroup.1.after_ref
  47.3 19.4 %all-to-all-start.2 = ((f32[8,17,1,128]{3,2,1,0:T(1,128)}), f32[8,17,1,128]{3,2,1,0:T(1,128)S(1)}, u32[]{:S(2)}, u32[]{:S(2)}) async-start(f32[8,17,1,128]{3,2,1,0:T(1,128)} %bitcast.6), calls=%async_computation.2 | async-start | bytes 139264 | tf_op jit(solution)/shard_map/all_to_all | solution.py:242
  66.7 0.1 pad_add_fusion.place_ref
  66.7 0.0 collective-permute-done.2.refs_2_
  66.7 0.0 collective-permute-done.1.refs_1_
  66.7 1.4 %members.3 = bf16[256,1024]{1,0:T(8,128)(2,1)S(1)} custom-call(f32[136,128]{1,0:T(8,128)} %regroup.1.after_ref, s32[2]{0:T(128)S(1)} %pad_add_fusion.place_ref, s32[4,128]{1,0:T(4,128)S(1)} %get-tuple-element.11.rows_ref, bf16[256,1024]{1,0:T(8,128)(2,1)S(1)} %copy-done, bf16[512,1024]{1,0:T(8,128)(2,1)S(1)} %collective-permute-done.1.refs_1_, ...), custom_call_target="tpu_custom_call" | custom-call | tf_op jit(solution)/shard_map/members/pallas_call | solution.py:245
  68.2 0.0 copy-start.1
  68.2 1.9 %collective-permute-start.3 = (bf16[256,1024]{1,0:T(8,128)(2,1)S(1)}, bf16[256,1024]{1,0:T(8,128)(2,1)}, u32[]{:S(2)}, u32[]{:S(2)}) collective-permute-start(bf16[256,1024]{1,0:T(8,128)(2,1)S(1)} %members.3), channel_id=1, source_target_pairs={{0,1},{1,0},{2,3},{3,2},{4,5},{5,4},{6,7},{7,6},{8,9},{9,8},{10,11... | collective-permute-start | bytes 1572872 | tf_op jit(solution)/shard_map/ppermute | solution.py:256
  70.1 1.4 %members.2.own_ref = bf16[256,1024]{1,0:T(8,128)(2,1)S(1)} custom-call(f32[136,128]{1,0:T(8,128)} %regroup.1.after_ref, s32[2]{0:T(128)S(1)} %pad_add_fusion.place_ref, s32[4,128]{1,0:T(4,128)S(1)} %get-tuple-element.11.rows_ref, bf16[256,1024]{1,0:T(8,128)(2,1)S(1)} %copy-done, bf16[512,1024]{1,0:T(8,128)(2,1)S(1)} %collective-permute-done.1.refs_1_, ...), custom_call_target="tpu_custom_call" | custom-call | tf_op jit(solution)/shard_map/members/pallas_call | solution.py:245
  71.5 6.8 %all-to-all-done.2 = f32[8,17,1,128]{3,2,1,0:T(1,128)S(1)} async-done(((f32[8,17,1,128]{3,2,1,0:T(1,128)}), f32[8,17,1,128]{3,2,1,0:T(1,128)S(1)}, u32[]{:S(2)}, u32[]{:S(2)}) %all-to-all-start.2) | async-done | bytes 69664 | tf_op jit(solution)/shard_map/all_to_all | solution.py:242
  78.3 0.0 copy-done.1
  78.3 0.7 finish.1.after_ref
  79.0 0.0 collective-permute-done.3.other_ref
  79.0 2.0 %match.1 = f32[2,128]{1,0:T(2,128)} custom-call(f32[16,128]{1,0:T(8,128)} %finish.1.after_ref, s32[2,128]{1,0:T(2,128)S(1)} %get-tuple-element.10.len_ref, bf16[256,1024]{1,0:T(8,128)(2,1)S(1)} %members.2.own_ref, bf16[256,1024]{1,0:T(8,128)(2,1)} %collective-permute-done.3.other_ref), custom_call_target="tpu_custom_call" | custom-call | tf_op jit(solution)/shard_map/match/pallas_call | solution.py:266
Async XLA Ops:
  0.6 17.3 %copy-start = (bf16[256,1024]{1,0:T(8,128)(2,1)S(1)}, bf16[256,1024]{1,0:T(8,128)(2,1)}, u32[]{:S(2)}) copy-start(bf16[256,1024]{1,0:T(8,128)(2,1)} %refs_0_.1) | copy-start | bytes 1572868
  2.7 26.6 %all-to-all-start = ((bf16[32,80,128]{2,1,0:T(8,128)(2,1)}), bf16[32,80,128]{2,1,0:T(8,128)(2,1)S(1)}, u32[]{:S(2)}, u32[]{:S(2)}) async-start(bf16[32,80,128]{2,1,0:T(8,128)(2,1)} %bitcast.12), calls=%async_computation | async-start | bytes 1310720 | tf_op jit(solution)/shard_map/all_to_all | solution.py:212
  17.9 13.5 %collective-permute-start = (bf16[256,1024]{1,0:T(8,128)(2,1)S(1)}, bf16[256,1024]{1,0:T(8,128)(2,1)S(1)}, u32[]{:S(2)}, u32[]{:S(2)}) collective-permute-start(bf16[256,1024]{1,0:T(8,128)(2,1)S(1)} %copy-done), channel_id=1, source_target_pairs={{0,1},{1,0},{2,3},{3,2},{4,5},{5,4},{6,7},{7,6},{8,9},{9,8},{10,11... | collective-permute-start | bytes 1572872 | tf_op jit(solution)/shard_map/ppermute | solution.py:222
  31.4 15.1 %all-to-all-start.1 = ((f32[16,33,1,128]{3,2,1,0:T(1,128)}), f32[16,33,1,128]{3,2,1,0:T(1,128)S(1)}, u32[]{:S(2)}, u32[]{:S(2)}) async-start(f32[16,33,1,128]{3,2,1,0:T(1,128)} %bitcast.4), calls=%async_computation.1 | async-start | bytes 540672 | tf_op jit(solution)/shard_map/all_to_all | solution.py:230
  36.3 30.4 %collective-permute-start.1 = (bf16[512,1024]{1,0:T(8,128)(2,1)S(1)}, bf16[512,1024]{1,0:T(8,128)(2,1)S(1)}, u32[]{:S(2)}, u32[]{:S(2)}) collective-permute-start(bf16[512,1024]{1,0:T(8,128)(2,1)S(1)} %pad_maximum_fusion), channel_id=1, source_target_pairs={{0,2},{1,7},{2,0},{3,5},{4,6},{5,3},{6,4},{7,1},{8,10},{9,15},{10,... | collective-permute-start | bytes 3145736 | tf_op jit(solution)/shard_map/ppermute | solution.py:227
  40.0 26.8 %collective-permute-start.2 = (bf16[256,1024]{1,0:T(8,128)(2,1)S(1)}, bf16[256,1024]{1,0:T(8,128)(2,1)S(1)}, u32[]{:S(2)}, u32[]{:S(2)}) collective-permute-start(bf16[256,1024]{1,0:T(8,128)(2,1)S(1)} %copy-done), channel_id=1, source_target_pairs={{0,4},{2,6},{4,0},{6,2},{1,5},{3,7},{5,1},{7,3},{8,12},{10,14},{12... | collective-permute-start | bytes 1572872 | tf_op jit(solution)/shard_map/ppermute | solution.py:228
  47.3 31.0 %all-to-all-start.2 = ((f32[8,17,1,128]{3,2,1,0:T(1,128)}), f32[8,17,1,128]{3,2,1,0:T(1,128)S(1)}, u32[]{:S(2)}, u32[]{:S(2)}) async-start(f32[8,17,1,128]{3,2,1,0:T(1,128)} %bitcast.6), calls=%async_computation.2 | async-start | bytes 139264 | tf_op jit(solution)/shard_map/all_to_all | solution.py:242
  68.2 10.1 %copy-start.1 = (f32[16,128]{1,0:T(8,128)S(1)}, f32[16,128]{1,0:T(8,128)}, u32[]{:S(2)}) copy-start(f32[16,128]{1,0:T(8,128)} %old_ref.1) | copy-start | bytes 24580
  68.2 10.8 %collective-permute-start.3 = (bf16[256,1024]{1,0:T(8,128)(2,1)S(1)}, bf16[256,1024]{1,0:T(8,128)(2,1)}, u32[]{:S(2)}, u32[]{:S(2)}) collective-permute-start(bf16[256,1024]{1,0:T(8,128)(2,1)S(1)} %members.3), channel_id=1, source_target_pairs={{0,1},{1,0},{2,3},{3,2},{4,5},{5,4},{6,7},{7,6},{8,9},{9,8},{10,11... | collective-permute-start | bytes 1572872 | tf_op jit(solution)/shard_map/ppermute | solution.py:256

commit v15 on v13

--- a/solution.py
+++ b/solution.py
@@ -154,7 +154,7 @@
     core, y = place_ref[0], place_ref[1]
     r = rows_ref[2 * of : 2 * of + 2, :]
     away, far = (r >> 9) ^ y, ((r >> 8) & 1) ^ core
-    block = jnp.where(away == 1 + 2 * core, 1 + far, jnp.where(far == 1, -1, jnp.where(away == 0, 0, jnp.where(away == 2, 3, -1))))
+    block = jnp.where(away == 2 - core, 1 + far, jnp.where(far == 1, -1, jnp.where(away == 0, 0, jnp.where(away == 3, 3, -1))))
     at = jnp.where(block < 0, -1, (block << 8) + (r & 255))
     at = jnp.concatenate([at, jnp.zeros((6, 128), I32)], 0).astype(F32).T.astype(I32)
     at = jnp.concatenate([at[:, 0:1], at[:, 1:2]], 0)
@@ -223,11 +223,11 @@
     )(((x * 8 + y * 2 + core) ^ BLOCK_ORDER[0]).reshape(1), messages)
     partner = lax.ppermute(embeddings, "c", [(0, 1), (1, 0)])
     embeddings, partner, parts = lax.optimization_barrier((embeddings, partner, parts))
-    near = [(2 * i + c, 2 * (i ^ (1 + 2 * c)) + c) for i in range(4) for c in range(2)]
+    near = [(2 * i + c, 2 * (i ^ (2 - c)) + c) for i in range(4) for c in range(2)]
     line = [
         embeddings,
         lax.ppermute(jnp.concatenate([embeddings, partner]), ("y", "c"), near),
-        lax.ppermute(embeddings, "y", [(i, i ^ 2) for i in range(4)]),
+        lax.ppermute(embeddings, "y", [(i, i ^ 3) for i in range(4)]),
     ]
     parts = lax.all_to_all(parts.reshape(16, 33, 1, 128), ("zl", "x"), 0, 0, axis_index_groups=[PLANE_ORDER], tiled=True)
     parts = pl.pallas_call(

time: 79.9 us -> 80 us (level)
  waiting for transfers between devices: 6.36 us -> 8.74 us
  starting transfers between devices: 62.6 us -> 60.3 us
    ppermute x2, starting transfers between devices: 8.31 us -> 5.77 us  [local(): others = [lax.ppermute(other, 'c', [(0, 1), (1, 0)]) for other in others]]
    ppermute x1, waiting for transfers between devices: 0.01 us -> 2.38 us  [local(): lax.ppermute(embeddings, 'y', [(i, i ^ 3) for i in range(4)])]
    ppermute x1, starting transfers between devices: 2.66 us -> 4.19 us  [local(): lax.ppermute(embeddings, 'y', [(i, i ^ 3) for i in range(4)])]
    ppermute x1, starting transfers between devices: 3.98 us -> 2.72 us  [local(): lax.ppermute(jnp.concatenate([embeddings, partner]), ('y', 'c'), near)]
  transfers between devices with their start and end apart: 8 -> 8, of which waited for: 1 -> 2; matrix products, arithmetic and copies ran while one was open for 0% -> 0% of each run, Pallas kernels for 8% -> 8%
where the time goes in v15:
time: 80 us; the launch traced here: 79.4 us
  starting transfers between devices  60.3 us (75%)
  Pallas kernels  9.48 us (12%)
  waiting for transfers between devices  8.74 us (11%)
    all_to_all x1, starting transfers between devices, local(): lax.all_to_all(messages.reshape(BLOCK, MSG, 128), ('x', 'y', 'c'), 0, 0,...  21.2 us
    all_to_all x1, starting transfers between devices, local(): lax.all_to_all(parts.reshape(8, 17, 1, 128), 'zh', 0, 0, axis_index_group...  19 us
    all_to_all x1, waiting for transfers between devices, local(): lax.all_to_all(messages.reshape(BLOCK, MSG, 128), ('x', 'y', 'c'), 0, 0,...  6.31 us
    ppermute x2, starting transfers between devices, local(): others = [lax.ppermute(other, 'c', [(0, 1), (1, 0)]) for other in others]  5.77 us
    all_to_all x1, starting transfers between devices, local(): lax.all_to_all(parts.reshape(16, 33, 1, 128), ('zl', 'x'), 0, 0, axis_ind...  5.16 us
    ppermute x1, starting transfers between devices, local(): lax.ppermute(embeddings, 'y', [(i, i ^ 3) for i in range(4)])  4.19 us
    pallas_call x2, Pallas kernels, local(): pl.pallas_call(functools.partial(member_kernel, of), out_shape=[jax.Shape...  2.86 us
    ppermute x1, starting transfers between devices, local(): lax.ppermute(jnp.concatenate([embeddings, partner]), ('y', 'c'), near)  2.72 us
  transfers between devices with their start and end apart: 8, of which 2 were waited for; matrix products, arithmetic and copies ran while one was open for 0% of the time, Pallas kernels for 8%

profile of v15, /device:TPU:1, one launch (start us, length us, event | category | flops | bytes accessed | tf_op | source)
XLA Modules:
  0.0 79.4 jit_solution(16868473389342748679)
XLA Ops:
  0.6 0.0 copy-start
  0.6 2.1 %pack.1 = bf16[4,8,80,128]{3,2,1,0:T(8,128)(2,1)} custom-call(bf16[256,1024]{1,0:T(8,128)(2,1)} %refs_0_.1, s32[2,128]{1,0:T(2,128)} %bitcast.13, s32[2,128]{1,0:T(2,128)} %rows_hbm.1, s32[2]{0:T(128)} %len_hbm.1), custom_call_target="tpu_custom_call" | custom-call | flops 1048576 | bytes 1572864 | tf_op jit(solution)/shard_map/pack/pallas_call | solution.py:195
  2.7 21.2 %all-to-all-start = ((bf16[32,80,128]{2,1,0:T(8,128)(2,1)}), bf16[32,80,128]{2,1,0:T(8,128)(2,1)S(1)}, u32[]{:S(2)}, u32[]{:S(2)}) async-start(bf16[32,80,128]{2,1,0:T(8,128)(2,1)} %bitcast.12), calls=%async_computation | async-start | bytes 1310720 | tf_op jit(solution)/shard_map/all_to_all | solution.py:214
  23.9 0.0 copy-done
  23.9 2.3 %collective-permute-start = (bf16[256,1024]{1,0:T(8,128)(2,1)S(1)}, bf16[256,1024]{1,0:T(8,128)(2,1)S(1)}, u32[]{:S(2)}, u32[]{:S(2)}) collective-permute-start(bf16[256,1024]{1,0:T(8,128)(2,1)S(1)} %copy-done), channel_id=1, source_target_pairs={{0,1},{1,0},{2,3},{3,2},{4,5},{5,4},{6,7},{7,6},{8,9},{9,8},{10,11... | collective-permute-start | bytes 1572872 | tf_op jit(solution)/shard_map/ppermute | solution.py:224
  26.2 6.3 %all-to-all-done.msg_ref = bf16[32,80,128]{2,1,0:T(8,128)(2,1)S(1)} async-done(((bf16[32,80,128]{2,1,0:T(8,128)(2,1)}), bf16[32,80,128]{2,1,0:T(8,128)(2,1)S(1)}, u32[]{:S(2)}, u32[]{:S(2)}) %all-to-all-start) | async-done | bytes 655392 | tf_op jit(solution)/shard_map/all_to_all | solution.py:214
  32.5 2.1 %sums.1 = (f32[528,128]{1,0:T(8,128)}, s32[4,128]{1,0:T(4,128)S(1)}, s32[2,128]{1,0:T(2,128)S(1)}) custom-call(s32[1]{0:T(128)} %bitcast.1.from_ref, bf16[32,80,128]{2,1,0:T(8,128)(2,1)S(1)} %all-to-all-done.msg_ref), custom_call_target="tpu_custom_call" | custom-call | flops 2147483648 | bytes 1048576 | tf_op jit(solution)/shard_map/sums/pallas_call | solution.py:215
  34.7 0.0 collective-permute-done
  34.7 5.2 %all-to-all-start.1 = ((f32[16,33,1,128]{3,2,1,0:T(1,128)}), f32[16,33,1,128]{3,2,1,0:T(1,128)S(1)}, u32[]{:S(2)}, u32[]{:S(2)}) async-start(f32[16,33,1,128]{3,2,1,0:T(1,128)} %bitcast.4), calls=%async_computation.1 | async-start | bytes 540672 | tf_op jit(solution)/shard_map/all_to_all | solution.py:232
  39.8 0.1 pad_maximum_fusion
  39.9 2.7 %collective-permute-start.1 = (bf16[512,1024]{1,0:T(8,128)(2,1)S(1)}, bf16[512,1024]{1,0:T(8,128)(2,1)S(1)}, u32[]{:S(2)}, u32[]{:S(2)}) collective-permute-start(bf16[512,1024]{1,0:T(8,128)(2,1)S(1)} %pad_maximum_fusion), channel_id=1, source_target_pairs={{0,4},{1,3},{2,6},{3,1},{4,0},{5,7},{6,2},{7,5},{8,12},{9,11},{10,... | collective-permute-start | bytes 3145736 | tf_op jit(solution)/shard_map/ppermute | solution.py:229
  42.6 4.2 %collective-permute-start.2 = (bf16[256,1024]{1,0:T(8,128)(2,1)S(1)}, bf16[256,1024]{1,0:T(8,128)(2,1)S(1)}, u32[]{:S(2)}, u32[]{:S(2)}) collective-permute-start(bf16[256,1024]{1,0:T(8,128)(2,1)S(1)} %copy-done), channel_id=1, source_target_pairs={{0,6},{2,4},{4,2},{6,0},{1,7},{3,5},{5,3},{7,1},{8,14},{10,12},{12... | collective-permute-start | bytes 1572872 | tf_op jit(solution)/shard_map/ppermute | solution.py:230
  46.8 0.0 all-to-all-done.1
  46.8 0.8 regroup.1.after_ref
  47.6 19.0 %all-to-all-start.2 = ((f32[8,17,1,128]{3,2,1,0:T(1,128)}), f32[8,17,1,128]{3,2,1,0:T(1,128)S(1)}, u32[]{:S(2)}, u32[]{:S(2)}) async-start(f32[8,17,1,128]{3,2,1,0:T(1,128)} %bitcast.6), calls=%async_computation.2 | async-start | bytes 139264 | tf_op jit(solution)/shard_map/all_to_all | solution.py:244
  66.6 0.1 pad_add_fusion.place_ref
  66.7 2.4 %collective-permute-done.2.refs_2_ = bf16[256,1024]{1,0:T(8,128)(2,1)S(1)} collective-permute-done((bf16[256,1024]{1,0:T(8,128)(2,1)S(1)}, bf16[256,1024]{1,0:T(8,128)(2,1)S(1)}, u32[]{:S(2)}, u32[]{:S(2)}) %collective-permute-start.2) | collective-permute-done | bytes 524320 | tf_op jit(solution)/shard_map/ppermute | solution.py:230
  69.0 0.0 collective-permute-done.1.refs_1_
  69.0 1.4 %members.3 = (bf16[128,1024]{1,0:T(8,128)(2,1)S(1)}, bf16[128,1024]{1,0:T(8,128)(2,1)S(1)}) custom-call(f32[136,128]{1,0:T(8,128)} %regroup.1.after_ref, s32[2]{0:T(128)S(1)} %pad_add_fusion.place_ref, s32[4,128]{1,0:T(4,128)S(1)} %get-tuple-element.17.rows_ref, bf16[256,1024]{1,0:T(8,128)(2,1)S(1)} %copy-done, ...), custom_call_target="tpu_custom_call" | custom-call | tf_op jit(solution)/shard_map/members/pallas_call | solution.py:247
  70.5 3.8 %collective-permute-start.3 = (bf16[128,1024]{1,0:T(8,128)(2,1)S(1)}, bf16[128,1024]{1,0:T(8,128)(2,1)S(1)}, u32[]{:S(2)}, u32[]{:S(2)}) collective-permute-start(bf16[128,1024]{1,0:T(8,128)(2,1)S(1)} %get-tuple-element.22), channel_id=1, source_target_pairs={{0,1},{1,0},{2,3},{3,2},{4,5},{5,4},{6,7},{7,6},{8,9},{9,8},{10,11... | collective-permute-start | bytes 786440 | tf_op jit(solution)/shard_map/ppermute | solution.py:258
  74.3 1.9 %collective-permute-start.4 = (bf16[128,1024]{1,0:T(8,128)(2,1)S(1)}, bf16[128,1024]{1,0:T(8,128)(2,1)S(1)}, u32[]{:S(2)}, u32[]{:S(2)}) collective-permute-start(bf16[128,1024]{1,0:T(8,128)(2,1)S(1)} %get-tuple-element.23), channel_id=1, source_target_pairs={{0,1},{1,0},{2,3},{3,2},{4,5},{5,4},{6,7},{7,6},{8,9},{9,8},{10,11... | collective-permute-start | bytes 786440 | tf_op jit(solution)/shard_map/ppermute | solution.py:258
  76.3 1.4 %members.2 = (bf16[128,1024]{1,0:T(8,128)(2,1)S(1)}, bf16[128,1024]{1,0:T(8,128)(2,1)S(1)}) custom-call(f32[136,128]{1,0:T(8,128)} %regroup.1.after_ref, s32[2]{0:T(128)S(1)} %pad_add_fusion.place_ref, s32[4,128]{1,0:T(4,128)S(1)} %get-tuple-element.17.rows_ref, bf16[256,1024]{1,0:T(8,128)(2,1)S(1)} %copy-done, ...), custom_call_target="tpu_custom_call" | custom-call | tf_op jit(solution)/shard_map/members/pallas_call | solution.py:247
  77.7 0.0 copy-start.1
  77.7 0.0 collective-permute-done.3.refs_2_
  77.7 0.0 collective-permute-done.4.refs_3_
  77.8 1.0 %match.1 = f32[2,128]{1,0:T(2,128)} custom-call(s32[2,128]{1,0:T(2,128)S(1)} %get-tuple-element.16.len_ref, bf16[128,1024]{1,0:T(8,128)(2,1)S(1)} %get-tuple-element.20.refs_0_, bf16[128,1024]{1,0:T(8,128)(2,1)S(1)} %get-tuple-element.21.refs_1_, bf16[128,1024]{1,0:T(8,128)(2,1)S(1)} %collective-permute-done.3.refs_2_, ...), custom_call_target="tpu_custom_call" | custom-call | tf_op jit(solution)/shard_map/match/pallas_call | solution.py:259
  78.7 0.0 all-to-all-done.2
  78.7 0.0 copy-done.1
  78.7 0.7 finish.1
Async XLA Ops:
  0.6 23.3 %copy-start = (bf16[256,1024]{1,0:T(8,128)(2,1)S(1)}, bf16[256,1024]{1,0:T(8,128)(2,1)}, u32[]{:S(2)}) copy-start(bf16[256,1024]{1,0:T(8,128)(2,1)} %refs_0_.1) | copy-start | bytes 1572868
  2.7 29.8 %all-to-all-start = ((bf16[32,80,128]{2,1,0:T(8,128)(2,1)}), bf16[32,80,128]{2,1,0:T(8,128)(2,1)S(1)}, u32[]{:S(2)}, u32[]{:S(2)}) async-start(bf16[32,80,128]{2,1,0:T(8,128)(2,1)} %bitcast.12), calls=%async_computation | async-start | bytes 1310720 | tf_op jit(solution)/shard_map/all_to_all | solution.py:214
  23.9 10.7 %collective-permute-start = (bf16[256,1024]{1,0:T(8,128)(2,1)S(1)}, bf16[256,1024]{1,0:T(8,128)(2,1)S(1)}, u32[]{:S(2)}, u32[]{:S(2)}) collective-permute-start(bf16[256,1024]{1,0:T(8,128)(2,1)S(1)} %copy-done), channel_id=1, source_target_pairs={{0,1},{1,0},{2,3},{3,2},{4,5},{5,4},{6,7},{7,6},{8,9},{9,8},{10,11... | collective-permute-start | bytes 1572872 | tf_op jit(solution)/shard_map/ppermute | solution.py:224
  34.7 12.2 %all-to-all-start.1 = ((f32[16,33,1,128]{3,2,1,0:T(1,128)}), f32[16,33,1,128]{3,2,1,0:T(1,128)S(1)}, u32[]{:S(2)}, u32[]{:S(2)}) async-start(f32[16,33,1,128]{3,2,1,0:T(1,128)} %bitcast.4), calls=%async_computation.1 | async-start | bytes 540672 | tf_op jit(solution)/shard_map/all_to_all | solution.py:232
  39.9 29.1 %collective-permute-start.1 = (bf16[512,1024]{1,0:T(8,128)(2,1)S(1)}, bf16[512,1024]{1,0:T(8,128)(2,1)S(1)}, u32[]{:S(2)}, u32[]{:S(2)}) collective-permute-start(bf16[512,1024]{1,0:T(8,128)(2,1)S(1)} %pad_maximum_fusion), channel_id=1, source_target_pairs={{0,4},{1,3},{2,6},{3,1},{4,0},{5,7},{6,2},{7,5},{8,12},{9,11},{10,... | collective-permute-start | bytes 3145736 | tf_op jit(solution)/shard_map/ppermute | solution.py:229
  42.6 26.4 %collective-permute-start.2 = (bf16[256,1024]{1,0:T(8,128)(2,1)S(1)}, bf16[256,1024]{1,0:T(8,128)(2,1)S(1)}, u32[]{:S(2)}, u32[]{:S(2)}) collective-permute-start(bf16[256,1024]{1,0:T(8,128)(2,1)S(1)} %copy-done), channel_id=1, source_target_pairs={{0,6},{2,4},{4,2},{6,0},{1,7},{3,5},{5,3},{7,1},{8,14},{10,12},{12... | collective-permute-start | bytes 1572872 | tf_op jit(solution)/shard_map/ppermute | solution.py:230
  47.6 31.1 %all-to-all-start.2 = ((f32[8,17,1,128]{3,2,1,0:T(1,128)}), f32[8,17,1,128]{3,2,1,0:T(1,128)S(1)}, u32[]{:S(2)}, u32[]{:S(2)}) async-start(f32[8,17,1,128]{3,2,1,0:T(1,128)} %bitcast.6), calls=%async_computation.2 | async-start | bytes 139264 | tf_op jit(solution)/shard_map/all_to_all | solution.py:244
  70.5 7.2 %collective-permute-start.3 = (bf16[128,1024]{1,0:T(8,128)(2,1)S(1)}, bf16[128,1024]{1,0:T(8,128)(2,1)S(1)}, u32[]{:S(2)}, u32[]{:S(2)}) collective-permute-start(bf16[128,1024]{1,0:T(8,128)(2,1)S(1)} %get-tuple-element.22), channel_id=1, source_target_pairs={{0,1},{1,0},{2,3},{3,2},{4,5},{5,4},{6,7},{7,6},{8,9},{9,8},{10,11... | collective-permute-start | bytes 786440 | tf_op jit(solution)/shard_map/ppermute | solution.py:258
  74.3 3.4 %collective-permute-start.4 = (bf16[128,1024]{1,0:T(8,128)(2,1)S(1)}, bf16[128,1024]{1,0:T(8,128)(2,1)S(1)}, u32[]{:S(2)}, u32[]{:S(2)}) collective-permute-start(bf16[128,1024]{1,0:T(8,128)(2,1)S(1)} %get-tuple-element.23), channel_id=1, source_target_pairs={{0,1},{1,0},{2,3},{3,2},{4,5},{5,4},{6,7},{7,6},{8,9},{9,8},{10,11... | collective-permute-start | bytes 786440 | tf_op jit(solution)/shard_map/ppermute | solution.py:258
  77.7 1.0 %copy-start.1 = (f32[16,128]{1,0:T(8,128)S(1)}, f32[16,128]{1,0:T(8,128)}, u32[]{:S(2)}) copy-start(f32[16,128]{1,0:T(8,128)} %old_ref.1) | copy-start | bytes 24580
